TPU v7x, 32 devices: a whole 2x2x4 slice. The times are simulated.
32 devices in a mesh: ctx: 8 (over z, y), head: 4 (over x, core).
Axes of the slice: x: 2, y: 2, z: 4, core: 2. Of those that a mesh axis runs over, the one named last changes fastest.
Arguments:
- queries: bfloat16 [1024, 4096], P('ctx', 'head'), may hold values from -12 to 12
- keys: bfloat16 [1024, 512], P('ctx', 'head'), may hold values from -6 to 6
- values: bfloat16 [1024, 512], P('ctx', 'head'), may hold values from -18 to 18
- doc_ids: int32 [1024], P('ctx'), may hold values from 0 to 15, never falling along the last dimension, each value on 1 to 768 neighbouring positions
- plan: int32 [8, 8], P('ctx'), may hold values from 0 to 7, each once within a row
- w_out: bfloat16 [4096, 8192], P('head', 'ctx'), may hold values from -0.09375 to 0.09375
Outputs:
- output: bfloat16 [1024, 8192], P('ctx', 'head')
Inputs may be any that keep to these rules, and one draw needn't show every extreme that they name: doc_ids never fall along the window; every one of the 16 documents holds 1 to 768 positions, and one holds exactly 768. Each row of plan is a permutation of the device indices along ctx.
All inputs are finite; a program needn't handle non-finite values.
Results may differ from a plain program's by a relative error of at most 0.01.
Values may be sent and summed in bfloat16 or wider, within the bound.
No kernel may reach another device: no remote copies, remote signals or barrier semaphores. Data moves between devices by JAX's collectives and lax.ppermute only.
A program may use at most 64 MiB of HBM per device.

v0:
```python
import math

import jax
import jax.numpy as jnp
from jax import lax
from jax.sharding import PartitionSpec as P

HEAD_DIM = 128
DOCS = 16


NEG_FILL = -1e30


def spread_rows(block, order, parts):
    shaped = block.reshape(parts, block.shape[0] // parts, block.shape[1])
    return jnp.take(shaped, order, axis=0).reshape(block.shape)


def attend(query_rows, row_pos, row_start, all_keys, all_values):
    n_rows = query_rows.shape[0]
    kv_local = all_keys.shape[1] // HEAD_DIM
    group_size = query_rows.shape[1] // all_keys.shape[1]
    q_heads = query_rows.reshape(n_rows, kv_local, group_size, HEAD_DIM).transpose(1, 0, 2, 3)
    q_heads = q_heads.reshape(kv_local, n_rows * group_size, HEAD_DIM)
    pos_rows = jnp.repeat(row_pos, group_size)
    start_rows = jnp.repeat(row_start, group_size)
    q_block = min(n_rows, max(1, 512 // group_size))
    block_rows = q_block * group_size
    n_qblocks = n_rows // q_block
    score_scale = 1.0 / math.sqrt(HEAD_DIM)
    total_keys = all_keys.shape[0]
    key_size = math.gcd(total_keys, 512)
    n_kblocks = total_keys // key_size
    key_tiles = all_keys.reshape(n_kblocks, key_size, kv_local, HEAD_DIM)
    value_tiles = all_values.reshape(n_kblocks, key_size, kv_local, HEAD_DIM)
    initial = (
        jnp.full((kv_local, n_rows * group_size), NEG_FILL, jnp.float32),
        jnp.zeros((kv_local, n_rows * group_size), jnp.float32),
        jnp.zeros((kv_local, n_rows * group_size, HEAD_DIM), jnp.float32),
    )

    def one_query_block(block_index, state):
        run_max, run_sum, run_acc = state
        offset = block_index * block_rows
        q_part = lax.dynamic_slice_in_dim(q_heads, offset, block_rows, 1)
        pos_part = lax.dynamic_slice_in_dim(pos_rows, offset, block_rows, 0)
        start_part = lax.dynamic_slice_in_dim(start_rows, offset, block_rows, 0)
        first_block = jnp.clip(jnp.min(start_part) // key_size, 0, n_kblocks)
        last_block = jnp.clip(jnp.max(pos_part) // key_size + 1, 0, n_kblocks)

        def add_tile(key_index, inner):
            block_max, block_sum, block_acc = inner
            key_tile = lax.dynamic_index_in_dim(key_tiles, key_index, 0, keepdims=False)
            value_tile = lax.dynamic_index_in_dim(value_tiles, key_index, 0, keepdims=False)
            scores = (
                jnp.einsum("grd,kgd->grk", q_part, key_tile, preferred_element_type=jnp.float32)
                * score_scale
            )
            key_pos = key_index * key_size + jnp.arange(key_size, dtype=jnp.int32)
            allowed = (key_pos[None, :] >= start_part[:, None]) & (
                key_pos[None, :] <= pos_part[:, None]
            )
            scores = jnp.where(allowed[None], scores, NEG_FILL)
            new_max = jnp.maximum(block_max, jnp.max(scores, axis=-1))
            expo = jnp.where(allowed[None], jnp.exp(scores - new_max[..., None]), 0.0)
            rescale = jnp.exp(block_max - new_max)
            block_sum = block_sum * rescale + jnp.sum(expo, axis=-1)
            block_acc = block_acc * rescale[..., None] + jnp.einsum(
                "grk,kgd->grd",
                expo.astype(jnp.bfloat16),
                value_tile,
                preferred_element_type=jnp.float32,
            )
            return (new_max, block_sum, block_acc)

        def one_key_block(key_index, inner):
            tile_low = key_index * key_size
            tile_high = tile_low + key_size - 1
            meets = jnp.any((start_part <= tile_high) & (pos_part >= tile_low))
            return lax.cond(
                meets, lambda carried: add_tile(key_index, carried), lambda carried: carried, inner
            )

        inner = (
            lax.dynamic_slice_in_dim(run_max, offset, block_rows, 1),
            lax.dynamic_slice_in_dim(run_sum, offset, block_rows, 1),
            lax.dynamic_slice_in_dim(run_acc, offset, block_rows, 1),
        )
        new_max, new_sum, new_acc = lax.fori_loop(first_block, last_block, one_key_block, inner)
        run_max = lax.dynamic_update_slice_in_dim(run_max, new_max, offset, 1)
        run_sum = lax.dynamic_update_slice_in_dim(run_sum, new_sum, offset, 1)
        run_acc = lax.dynamic_update_slice_in_dim(run_acc, new_acc, offset, 1)
        return (run_max, run_sum, run_acc)

    final_max, final_sum, final_acc = lax.fori_loop(0, n_qblocks, one_query_block, initial)
    result = final_acc / final_sum[..., None]
    result = result.reshape(kv_local, n_rows, group_size, HEAD_DIM).transpose(1, 0, 2, 3)
    return result.reshape(n_rows, kv_local * group_size * HEAD_DIM).astype(jnp.bfloat16)


def body(queries, keys, values, doc_ids, plan, w_out):
    n_rows = queries.shape[0]
    parts = lax.axis_size("ctx")
    my_index = lax.axis_index("ctx")
    all_ids, all_plan = (
        lax.all_gather(doc_ids, "ctx", axis=0, tiled=True),
        lax.all_gather(plan, "ctx", axis=0, tiled=True),
    )
    all_keys, all_values = (
        lax.all_gather(keys, "ctx", axis=0, tiled=True),
        lax.all_gather(values, "ctx", axis=0, tiled=True),
    )
    doc_range = jnp.arange(DOCS, dtype=jnp.int32)
    doc_first = jnp.sum((all_ids[None, :] < doc_range[:, None]).astype(jnp.int32), axis=1)
    local_pos = my_index * n_rows + jnp.arange(n_rows, dtype=jnp.int32)
    ids_here = jnp.take(all_ids, local_pos)
    local_out = attend(
        queries,
        local_pos,
        jnp.sum(jnp.where(ids_here[:, None] == doc_range[None, :], doc_first[None, :], 0), axis=1),
        all_keys,
        all_values,
    )
    attended = lax.all_to_all(
        spread_rows(local_out, plan[0], parts), "ctx", split_axis=0, concat_axis=0, tiled=True
    )
    stacked = jnp.dot(
        lax.all_gather(attended, "ctx", axis=0, tiled=True),
        w_out,
        preferred_element_type=jnp.float32,
    )
    partial_sum = lax.all_to_all(
        stacked.astype(jnp.bfloat16), "ctx", split_axis=0, concat_axis=1, tiled=True
    ).astype(stacked.dtype)
    summed = lax.psum_scatter(
        partial_sum.astype(jnp.bfloat16), "head", scatter_dimension=1, tiled=True
    )
    return summed


def solution(mesh):
    return jax.shard_map(
        body,
        mesh=mesh,
        in_specs=(
            P("ctx", "head"),
            P("ctx", "head"),
            P("ctx", "head"),
            P("ctx"),
            P("ctx", None),
            P("head", "ctx"),
        ),
        out_specs=P("ctx", "head"),
        check_vma=False,
    )
```

profile of v0, /device:TPU:17, one launch (start us, length us, event | category | flops | bytes accessed | tf_op | source)
XLA Modules:
  0.0 281.1 jit_solution(9750532382548301338)
XLA Ops:
  6.5 0.8 fusion.20
  7.3 1.2 compare_and_fusion.1
  8.6 0.6 pad_clamp_fusion
  9.2 11.4 %all-gather = s32[8,1,128]{2,1,0:T(1,128)S(1)} all-gather(s32[1,1,128]{2,1,0:T(1,128)} %bitcast.62), channel_id=1, replica_groups=mesh['ctx'=8,'head'=4] {'ctx'}, dimensions={0}, use_global_device_ids=true | all-gather | bytes 4608 | tf_op jit(solution)/shard_map/all_gather | solution.py:107
  20.8 1.0 gather_fusion
  21.9 0.7 reshape.131
  22.7 0.7 reshape.132
  23.4 1.1 reshape_transpose_reshape.4
  24.5 26.0 %all_gather.13 = bf16[1024,128]{1,0:T(8,128)(2,1)S(1)} all-gather(bf16[128,128]{1,0:T(8,128)(2,1)} %param.13), channel_id=1, replica_groups=mesh['ctx'=8,'head'=4] {'ctx'}, dimensions={0}, use_global_device_ids=true | all-gather | bytes 294912 | tf_op jit(solution)/shard_map/all_gather | solution.py:111
  50.4 26.7 %all_gather.14 = bf16[1024,128]{1,0:T(8,128)(2,1)} all-gather(bf16[128,128]{1,0:T(8,128)(2,1)} %param.14), channel_id=1, replica_groups=mesh['ctx'=8,'head'=4] {'ctx'}, dimensions={0}, use_global_device_ids=true | all-gather | bytes 294912 | tf_op jit(solution)/shard_map/all_gather | solution.py:112
  77.2 0.6 broadcast_in_dim.65
  77.7 0.6 broadcast_in_dim.66
  78.4 30.8 %while.88 = (s32[]{:T(128)}, f32[1,1024]{1,0:T(1,128)}, f32[1,1024]{1,0:T(1,128)}, f32[1,1024,128]{2,1,0:T(8,128)S(1)}, s32[1024]{0:T(1024)}, /*index=5*/s32[102...) while((s32[]{:T(128)}, f32[1,1024]{1,0:T(1,128)}, ...), condition=%wide.region_12.13_spmd, body=%wide.region_2.12_spmd.sunk | while | flops 139072032 | bytes 6505564 | solution.py:96
  78.4 0.7 constant_dynamic-slice_fusion.9
  79.1 0.7 constant_dynamic-slice_fusion.8
  79.8 1.4 fusion.29
  83.4 1.4 fusion.28
  87.4 5.7 %while.89 = (s32[]{:T(128)}, f32[1,512]{1,0:T(1,128)S(1)}, f32[1,512]{1,0:T(1,128)S(1)}, f32[1,512,128]{2,1,0:T(8,128)S(1)}, s32[]{:T(128)}, /*index=5*/s32[512]...) while((s32[]{:T(128)}, f32[1,512]{1,0:T(1,128)S(1)}, ...), condition=%wide.region_11.11_spmd, body=%wide.region_5.10_spmd.sunk | while | flops 139070976 | bytes 5169537 | solution.py:90
  87.5 0.6 and_reduce_fusion.2
  88.7 1.5 conditional.2
  89.7 0.6 fusion.2
  90.3 0.6 and_reduce_fusion.2
  91.6 1.5 conditional.2
  91.6 0.4 fusion.23
  92.6 0.6 fusion.2
  93.1 0.6 constant_dynamic-update-slice_fusion.5
  93.8 0.7 constant_dynamic-slice_fusion.9
  94.5 0.7 constant_dynamic-slice_fusion.8
  95.1 1.4 fusion.29
  98.8 1.4 fusion.28
  102.8 5.7 %while.89 = (s32[]{:T(128)}, f32[1,512]{1,0:T(1,128)S(1)}, f32[1,512]{1,0:T(1,128)S(1)}, f32[1,512,128]{2,1,0:T(8,128)S(1)}, s32[]{:T(128)}, /*index=5*/s32[512]...) while((s32[]{:T(128)}, f32[1,512]{1,0:T(1,128)S(1)}, ...), condition=%wide.region_11.11_spmd, body=%wide.region_5.10_spmd.sunk | while | flops 139070976 | bytes 5169537 | solution.py:90
  102.9 0.6 and_reduce_fusion.2
  104.1 1.5 conditional.2
  104.2 0.4 fusion.23
  105.1 0.6 fusion.2
  105.7 0.6 and_reduce_fusion.2
  107.0 1.5 conditional.2
  107.9 0.6 fusion.2
  108.5 0.6 constant_dynamic-update-slice_fusion.5
  109.2 0.9 divide_convert_fusion
  110.2 0.7 gather_fusion.1
  110.9 0.8 broadcast_select_fusion
  111.6 8.5 %all_to_all.28 = bf16[8,16,1024]{2,1,0:T(8,128)(2,1)} all-to-all(bf16[8,16,1024]{2,1,0:T(8,128)(2,1)S(1)} %broadcast_select_fusion), channel_id=1, replica_groups=mesh['ctx'=8,'head'=4] {'ctx'}, dimensions={0} | all-to-all | bytes 524288 | tf_op jit(solution)/shard_map/all_to_all | solution.py:125
  120.2 65.8 %all-gather.3.cloned.1.call-done = bf16[1024,1024]{1,0:T(8,128)(2,1)} async-done(((bf16[128,1024]{1,0:T(8,128)(2,1)}), bf16[1024,1024]{1,0:T(8,128)(2,1)}) %all-gather.3.cloned.1.call-update) | async-done | bytes 2097168 | tf_op jit(solution)/shard_map/all_gather | solution.py:129
  186.0 3.9 %convolution_convert_fusion = bf16[1024,1024]{1,0:T(8,128)(2,1)S(1)} fusion(bf16[1024,1024]{1,0:T(8,128)(2,1)} %all-gather.3.cloned.1.call-done, bf16[1024,1024]{1,0:T(8,128)(2,1)S(1)} %copy-done), kind=kOutput, calls=%fused_computation.35 | convolution fusion | flops 2148532224 | bytes 6291456 | tf_op jit(solution)/shard_map/dot_general | solution.py:128
  190.0 50.0 %all_to_all.29 = bf16[8,128,1024]{2,1,0:T(8,128)(2,1)S(1)} all-to-all(bf16[8,128,1024]{2,1,0:T(8,128)(2,1)S(1)} %bitcast.56), channel_id=1, replica_groups=mesh['ctx'=8,'head'=4] {'ctx'}, dimensions={0} | all-to-all | bytes 4194304 | tf_op jit(solution)/shard_map/all_to_all | solution.py:133
  239.9 1.5 copy.17
  241.5 32.8 %reduce-scatter.2.cloned.1.call-done = bf16[128,2048]{1,0:T(8,128)(2,1)} async-done(((bf16[128,8192]{1,0:T(8,128)(2,1)}), bf16[128,2048]{1,0:T(8,128)(2,1)}) %reduce-scatter.2.cloned.1.call-update) | async-done | bytes 524304 | tf_op jit(solution)/shard_map/reduce_scatter | solution.py:136
  (51 shorter events, 3.7 us)
Async XLA Ops:
  6.5 179.5 %copy-start = (bf16[1024,1024]{1,0:T(8,128)(2,1)S(1)}, bf16[1024,1024]{1,0:T(8,128)(2,1)}, u32[]{:S(2)}) copy-start(bf16[1024,1024]{1,0:T(8,128)(2,1)} %param.17) | copy-start | bytes 6291460
  6.5 179.5 %all-gather.3.cloned.1.call-start = ((), (), s32[]{:S(2)}) async-start(), calls=%async_computation.3 | async-start | bytes 2359296 | tf_op jit(solution)/shard_map/all_gather | solution.py:129
  88.8 1.0 copy-start.1
  91.6 1.0 copy-start.1
  104.2 1.0 copy-start.1
  107.0 1.0 copy-start.1
  120.2 154.0 %reduce-scatter.2.cloned.1.call-start = ((), (), s32[]{:S(2)}) async-start(), calls=%async_computation.4 | async-start | bytes 2621440 | tf_op jit(solution)/shard_map/reduce_scatter | solution.py:136
Sparse Core Ops, SparseCore 0:
  120.3 65.6 all-gather.2
  241.6 32.5 reduce-scatter.1
where the time goes:
time: 284 us; the launch traced here: 281 us
  blocking collectives  123 us (43%)
  waiting for transfers between devices  98.6 us (35%)
  other arithmetic  14.1 us (5%)
  between operations  13.5 us (5%)
  loops' own time  12.6 us (4%)
  local copies, waits for them, and re-layouts  11.9 us (4%)
  matrix products  7.67 us (3%)
    all_gather x1, waiting for transfers between devices, body(): lax.all_gather(attended, 'ctx', axis=0, tiled=True)  65.8 us
    all_to_all x1, blocking collectives, body(): lax.all_to_all(stacked.astype(jnp.bfloat16), 'ctx', split_axis=0, concat_...  50 us
    reduce_scatter x1, waiting for transfers between devices, body(): lax.psum_scatter(partial_sum.astype(jnp.bfloat16), 'head', scatter_dimens...  32.8 us
    all_gather x1, blocking collectives, body(): lax.all_gather(values, 'ctx', axis=0, tiled=True)  26.7 us
    all_gather x1, blocking collectives, body(): lax.all_gather(keys, 'ctx', axis=0, tiled=True)  26 us
    all_gather x1, blocking collectives, body(): lax.all_gather(doc_ids, 'ctx', axis=0, tiled=True)  11.4 us
    another operation x1, loops' own time, attend(): lax.fori_loop(0, n_qblocks, one_query_block, initial)  9.7 us
    all_to_all x1, blocking collectives, body(): lax.all_to_all(spread_rows(local_out, plan[0], parts), 'ctx', split_axis=...  8.53 us
  transfers between devices with their start and end apart: 2, of which 2 were waited for; matrix products, arithmetic and copies ran while one was open for 0% of the time, Pallas kernels for 0%

commit v1 on v0

--- a/solution.py
+++ b/solution.py
@@ -1,15 +1,208 @@
+import functools
 import math
 
 import jax
 import jax.numpy as jnp
 from jax import lax
+from jax.experimental import pallas as pl
+from jax.experimental.pallas import tpu as pltpu
 from jax.sharding import PartitionSpec as P
 
 HEAD_DIM = 128
 DOCS = 16
-
-
+META = 16
 NEG_FILL = -1e30
+VMEM_LIMIT = 56 * 1024 * 1024
+
+ANY = pl.BlockSpec(memory_space=pl.ANY)
+VMEM = pl.BlockSpec(memory_space=pltpu.VMEM)
+SMEM = pl.BlockSpec(memory_space=pltpu.SMEM)
+
+
+def pack_kernel(parts, heads, plan_ref, q_ref, k_ref, v_ref, ids_ref, out_ref):
+    rows = q_ref.shape[0]
+    piece = rows // parts
+    lane = lax.broadcasted_iota(jnp.int32, (1, rows), 1)
+    source = jnp.zeros((1, rows), jnp.int32)
+    for j in range(parts):
+        p = plan_ref[0, j]
+        for h in range(heads):
+            out_ref[h * rows + j * piece : h * rows + (j + 1) * piece, :] = q_ref[
+                pl.ds(pl.multiple_of(p * piece, piece), piece),
+                h * HEAD_DIM : (h + 1) * HEAD_DIM,
+            ]
+        source = jnp.where(
+            (lane >= j * piece) & (lane < (j + 1) * piece), (p - j) * piece + lane, source
+        )
+    base = heads * rows
+    out_ref[base : base + rows, :] = k_ref[...]
+    out_ref[base + rows : base + 2 * rows, :] = v_ref[...]
+    ids = ids_ref[...].astype(jnp.float32)
+    row = lax.broadcasted_iota(jnp.int32, (META, rows), 0)
+    from_row = lax.broadcasted_iota(jnp.int32, (rows, rows), 0)
+    chosen = (from_row == source).astype(jnp.float32)
+    ids_rows = jnp.broadcast_to(ids, (META, rows))
+    ids_moved = jnp.dot(ids_rows, chosen, preferred_element_type=jnp.float32)
+    meta = jnp.where(
+        row == 0,
+        ids_rows,
+        jnp.where(row == 1, ids_moved, jnp.broadcast_to(source.astype(jnp.float32), (META, rows))),
+    )
+    out_ref[base + 2 * rows :, :] = meta.astype(jnp.bfloat16)
+
+
+def attend_project_kernel(parts, heads, scale, w_ref, *refs):
+    blocks, (send_ref, keep_ref, held, rows_ref, w_held, sems) = refs[:parts], refs[parts:]
+    rows = send_ref.shape[0] * 2 // parts
+    piece = rows // parts
+    base = heads * rows
+    me = lax.axis_index("ctx")
+    other = 1 - lax.rem(lax.axis_index("head"), 2)
+    copies = [
+        pltpu.make_async_copy(blocks[k], held.at[jnp.bitwise_xor(me, k)], sems.at[k])
+        for k in range(parts)
+    ]
+    w_copy = pltpu.make_async_copy(w_ref, w_held, sems.at[parts])
+    for copy in copies:
+        copy.start()
+    w_copy.start()
+    for copy in copies:
+        copy.wait()
+    for d in range(parts):
+        span = (d + 1) * rows
+        meta = held[d, base + 2 * rows :, :].astype(jnp.float32)
+        turned = meta.T
+        q_ids, q_pos = turned[:, 1:2], turned[:, 2:3]
+        k_ids = jnp.concatenate(
+            [held[b, base + 2 * rows :, :].astype(jnp.float32)[0:1] for b in range(d + 1)], axis=1
+        )
+        k_pos = lax.broadcasted_iota(jnp.int32, (1, span), 1) - d * rows
+        allowed = (k_ids == q_ids) & (k_pos.astype(jnp.float32) <= q_pos)
+        bias = jnp.where(allowed, 0.0, NEG_FILL)
+
+        def one_head(h, carry, d=d, span=span, bias=bias):
+            q = held[d, pl.ds(pl.multiple_of(h * rows, rows), rows), :]
+            keys = held[: d + 1, base : base + rows, :].reshape(span, HEAD_DIM)
+            vals = held[: d + 1, base + rows : base + 2 * rows, :].reshape(span, HEAD_DIM)
+            s = lax.dot_general(q, keys, (((1,), (1,)), ((), ())), preferred_element_type=jnp.float32)
+            s = s + bias
+            top = jnp.max(s, axis=1, keepdims=True)
+            e = jnp.exp2((s - top) * (scale * math.log2(math.e)))
+            total = jnp.sum(e, axis=1, keepdims=True)
+            o = jnp.dot(e.astype(jnp.bfloat16), vals, preferred_element_type=jnp.float32) / total
+            o = o.astype(jnp.bfloat16)
+            for j in range(parts):
+                at = (j // 2) * rows + d * piece
+                rows_ref[
+                    j % 2, at : at + piece, pl.ds(pl.multiple_of(h * HEAD_DIM, HEAD_DIM), HEAD_DIM)
+                ] = o[j * piece : (j + 1) * piece, :]
+            return carry
+
+        lax.fori_loop(0, heads, one_head, 0)
+    w_copy.wait()
+    send_ref[...] = jnp.dot(
+        rows_ref[other], w_held[...], preferred_element_type=jnp.float32
+    ).astype(jnp.bfloat16)
+    keep_ref[...] = jnp.dot(
+        rows_ref[1 - other], w_held[...], preferred_element_type=jnp.float32
+    ).astype(jnp.bfloat16)
+
+
+def pair_sum_kernel(group, half, keep_ref, got_ref, *out_refs):
+    count = len(out_refs)
+    rows = keep_ref.shape[0] // count
+    mine = lax.rem(lax.axis_index("ctx"), group) * half + lax.axis_index("head") // 2
+    for k, out_ref in enumerate(out_refs):
+        at = pl.ds(pl.multiple_of(jnp.bitwise_xor(mine, k) * rows, rows), rows)
+        out_ref[...] = (keep_ref[at, :].astype(jnp.float32) + got_ref[at, :].astype(jnp.float32)).astype(
+            jnp.bfloat16
+        )
+
+
+def final_kernel(group, half, *refs):
+    blocks, out_ref = refs[:-1], refs[-1]
+    cols = blocks[0].shape[1]
+    high = lax.axis_index("ctx") // 2
+    for first in range(0, len(blocks), half):
+        part = lax.div(jnp.bitwise_xor(high, first), half)
+        total = blocks[first][...].astype(jnp.float32)
+        for k in range(first + 1, first + half):
+            total = total + blocks[k][...].astype(jnp.float32)
+        out_ref[:, pl.ds(pl.multiple_of(part * cols, cols), cols)] = total.astype(jnp.bfloat16)
+
+
+def spread_over_ctx(block, parts):
+    def moved(x, k):
+        return lax.ppermute(x, "ctx", [(i, i ^ k) for i in range(parts)])
+
+    got = {0: block}
+    for k in range(2, parts, 2):
+        got[k] = moved(block, k)
+    got[1] = moved(block, 1)
+    for k in range(2, parts, 2):
+        got[k + 1] = moved(got[k], 1)
+    return [got[k] for k in range(parts)]
+
+
+def packed_body(groups, queries, keys, values, doc_ids, plan, w_out):
+    parts = lax.axis_size("ctx")
+    rows = queries.shape[0]
+    heads = queries.shape[1] // HEAD_DIM
+    width = w_out.shape[1]
+    group, half = parts // groups, groups // 2
+    bf16 = jnp.bfloat16
+    params = pltpu.CompilerParams(vmem_limit_bytes=VMEM_LIMIT)
+    block_rows = (heads + 2) * rows + META
+    block = pl.pallas_call(
+        functools.partial(pack_kernel, parts, heads),
+        out_shape=jax.ShapeDtypeStruct((block_rows, HEAD_DIM), bf16),
+        in_specs=[SMEM, VMEM, VMEM, VMEM, VMEM],
+        out_specs=VMEM,
+        compiler_params=params,
+        name="pack",
+    )(plan, queries, keys, values, doc_ids.reshape(1, rows))
+    blocks = spread_over_ctx(block, parts)
+    tokens = parts * rows
+    send, keep = pl.pallas_call(
+        functools.partial(attend_project_kernel, parts, heads, 1.0 / math.sqrt(HEAD_DIM)),
+        out_shape=[jax.ShapeDtypeStruct((tokens // 2, width), bf16)] * 2,
+        in_specs=[ANY] * (1 + parts),
+        out_specs=[VMEM, VMEM],
+        scratch_shapes=[
+            pltpu.VMEM((parts, block_rows, HEAD_DIM), bf16),
+            pltpu.VMEM((2, tokens // 2, heads * HEAD_DIM), bf16),
+            pltpu.VMEM(w_out.shape, bf16),
+            pltpu.SemaphoreType.DMA((parts + 1,)),
+        ],
+        compiler_params=params,
+        name="attend_project",
+    )(w_out, *blocks)
+    got = lax.ppermute(send, "head", [(g, g ^ 1) for g in range(groups)])
+    count = parts // 2
+    sums = pl.pallas_call(
+        functools.partial(pair_sum_kernel, group, half),
+        out_shape=[jax.ShapeDtypeStruct((rows, width), bf16)] * count,
+        in_specs=[VMEM, VMEM],
+        out_specs=[VMEM] * count,
+        compiler_params=params,
+        name="pair_sum",
+    )(keep, got)
+    arrived = []
+    for k in range(count):
+        pairs = []
+        for c in range(parts):
+            for g in range(groups):
+                high = ((c % group) * half + g // 2) ^ k
+                pairs.append((c * groups + g, (high * 2 + g % 2) * groups + c // group))
+        arrived.append(lax.ppermute(sums[k], ("ctx", "head"), pairs))
+    return pl.pallas_call(
+        functools.partial(final_kernel, group, half),
+        out_shape=jax.ShapeDtypeStruct((rows, group * width), bf16),
+        in_specs=[VMEM] * count,
+        out_specs=VMEM,
+        compiler_params=params,
+        name="final_sum",
+    )(*arrived)
 
 
 def spread_rows(block, order, parts):
@@ -139,9 +332,24 @@
     return summed
 
 
+def fits(parts, groups, rows, width):
+    powers = all(n & (n - 1) == 0 for n in (parts, groups))
+    window = parts * rows * width * 2
+    whole = rows % (16 * parts) == 0 and groups % 2 == 0 and parts % groups == 0
+    return powers and whole and 8 * window <= VMEM_LIMIT
+
+
 def solution(mesh):
+    parts, groups = mesh.shape["ctx"], mesh.shape["head"]
+
+    def one_device(queries, keys, values, doc_ids, plan, w_out):
+        one_pair = keys.shape[1] == HEAD_DIM
+        if one_pair and fits(parts, groups, queries.shape[0], queries.shape[1]):
+            return packed_body(groups, queries, keys, values, doc_ids, plan, w_out)
+        return body(queries, keys, values, doc_ids, plan, w_out)
+
     return jax.shard_map(
-        body,
+        one_device,
         mesh=mesh,
         in_specs=(
             P("ctx", "head"),

time: 284 us -> 126 us (0.44)
  blocking collectives: 123 us -> 0 us
  Pallas kernels: 0 us -> 41.8 us
  waiting for transfers between devices: 98.6 us -> 60.7 us
  starting transfers between devices: 0.04 us -> 20.4 us
  other arithmetic: 14.1 us -> 0 us
  between operations: 13.5 us -> 0.1 us
  loops' own time: 12.6 us -> 0 us
  local copies, waits for them, and re-layouts: 11.9 us -> 2.43 us
  matrix products: 7.67 us -> 0 us
    all_gather x1 -> x0, waiting for transfers between devices: 65.8 us -> none  [body(): lax.all_gather(attended, 'ctx', axis=0, tiled=True)]
    all_gather x3 -> x0, blocking collectives: 64.1 us -> none  [the longest x1 26.7 us: body(): lax.all_gather(values, 'ctx', axis=0, tiled=True)]
    ppermute x0 -> x12, waiting for transfers between devices: none -> 60.7 us  [the longest x7 38.1 us: moved(): return lax.ppermute(x, 'ctx', [(i, i ^ k) for i in range(parts)])]
    all_to_all x2 -> x0, blocking collectives: 58.5 us -> none  [the longest x1 50 us: body(): lax.all_to_all(stacked.astype(jnp.bfloat16), 'ctx', split_axis=0, concat_...]
    pallas_call x0 -> x4, Pallas kernels: none -> 41.8 us  [the longest x1 35.1 us: packed_body(): pl.pallas_call(functools.partial(attend_project_kernel, parts, heads, 1.0...]
    reduce_scatter x1 -> x0, waiting for transfers between devices: 32.8 us -> none  [body(): lax.psum_scatter(partial_sum.astype(jnp.bfloat16), 'head', scatter_dimens...]
    ppermute x0 -> x12, starting transfers between devices: none -> 20.4 us  [the longest x4 11 us: packed_body(): arrived.append(lax.ppermute(sums[k], ('ctx', 'head'), pairs))]
    another operation x7 -> x0, loops' own time: 12.6 us -> none  [the longest x1 9.7 us: attend(): lax.fori_loop(0, n_qblocks, one_query_block, initial)]
  transfers between devices with their start and end apart: 2 -> 12, of which waited for: 2 -> 8; matrix products, arithmetic and copies ran while one was open for 0% -> 0% of each run, Pallas kernels for 0% -> 0%
where the time goes in v1:
time: 126 us; the launch traced here: 125 us
  waiting for transfers between devices  60.7 us (48%)
  Pallas kernels  41.8 us (33%)
  starting transfers between devices  20.4 us (16%)
  local copies, waits for them, and re-layouts  2.43 us (2%)
    ppermute x7, waiting for transfers between devices, moved(): return lax.ppermute(x, 'ctx', [(i, i ^ k) for i in range(parts)])  38.1 us
    pallas_call x1, Pallas kernels, packed_body(): pl.pallas_call(functools.partial(attend_project_kernel, parts, heads, 1.0...  35.1 us
    ppermute x4, waiting for transfers between devices, packed_body(): arrived.append(lax.ppermute(sums[k], ('ctx', 'head'), pairs))  20.1 us
    ppermute x4, starting transfers between devices, packed_body(): arrived.append(lax.ppermute(sums[k], ('ctx', 'head'), pairs))  11 us
    ppermute x7, starting transfers between devices, moved(): return lax.ppermute(x, 'ctx', [(i, i ^ k) for i in range(parts)])  7.33 us
    pallas_call x1, Pallas kernels, packed_body(): pl.pallas_call(functools.partial(pair_sum_kernel, group, half), out_shape...  2.66 us
  transfers between devices with their start and end apart: 12, of which 8 were waited for; matrix products, arithmetic and copies ran while one was open for 0% of the time, Pallas kernels for 0%

profile of v1, /device:TPU:17, one launch (start us, length us, event | category | flops | bytes accessed | tf_op | source)
XLA Modules:
  0.0 125.5 jit_solution(13899614535718746337)
XLA Ops:
  0.0 1.9 %pack.1.refs_0_ = bf16[1296,128]{1,0:T(8,128)(2,1)} custom-call(s32[1,8]{1,0:T(1,128)} %plan_ref.1, bf16[128,1024]{1,0:T(8,128)(2,1)} %q_ref.1, bf16[128,128]{1,0:T(8,128)(2,1)} %k_ref.1, bf16[128,128]{1,0:T(8,128)(2,1)} %v_ref.1, s32[1,128]{1,0:T(1,128)} %bitcast.1), custom_call_target="tpu_custom_call" | custom-call | tf_op jit(solution)/shard_map/pack/pallas_call | solution.py:156
  1.9 0.2 collective-permute-start.5
  2.1 3.2 %collective-permute-start.3 = (bf16[1296,128]{1,0:T(8,128)(2,1)}, bf16[1296,128]{1,0:T(8,128)(2,1)S(1)}, u32[]{:S(2)}, u32[]{:S(2)}) collective-permute-start(bf16[1296,128]{1,0:T(8,128)(2,1)} %pack.1.refs_0_), channel_id=1, source_target_pairs={{0,16},{4,20},{8,24},{12,28},{16,0},{20,4},{24,8},{28,12},{1,17},{... | collective-permute-start | bytes 995336 | tf_op jit(solution)/shard_map/ppermute | solution.py:136
  5.3 0.0 collective-permute-start.1
  5.3 1.2 collective-permute-start
  6.5 18.5 %collective-permute-done.5.refs_6_ = bf16[1296,128]{1,0:T(8,128)(2,1)S(1)} collective-permute-done((bf16[1296,128]{1,0:T(8,128)(2,1)}, bf16[1296,128]{1,0:T(8,128)(2,1)S(1)}, u32[]{:S(2)}, u32[]{:S(2)}) %collective-permute-start.5) | collective-permute-done | bytes 331808 | tf_op jit(solution)/shard_map/ppermute | solution.py:136
  25.0 0.0 copy-start.1
  25.0 1.2 collective-permute-start.6
  26.2 4.1 %collective-permute-done.3.refs_4_ = bf16[1296,128]{1,0:T(8,128)(2,1)S(1)} collective-permute-done((bf16[1296,128]{1,0:T(8,128)(2,1)}, bf16[1296,128]{1,0:T(8,128)(2,1)S(1)}, u32[]{:S(2)}, u32[]{:S(2)}) %collective-permute-start.3) | collective-permute-done | bytes 331808 | tf_op jit(solution)/shard_map/ppermute | solution.py:136
  30.4 0.0 copy-start.2
  30.4 1.2 collective-permute-start.4
  31.6 0.0 collective-permute-done.1.refs_2_
  31.6 0.0 copy-start.3
  31.6 0.2 collective-permute-start.2
  31.8 0.0 collective-permute-done.refs_1_
  31.8 0.0 copy-start.4
  31.8 0.0 collective-permute-done.6.refs_7_
  31.9 0.0 copy-start.5
  31.9 8.4 %collective-permute-done.4.refs_5_ = bf16[1296,128]{1,0:T(8,128)(2,1)S(1)} collective-permute-done((bf16[1296,128]{1,0:T(8,128)(2,1)S(1)}, bf16[1296,128]{1,0:T(8,128)(2,1)S(1)}, u32[]{:S(2)}, u32[]{:S(2)}) %collective-permute-start.4) | collective-permute-done | bytes 331808 | tf_op jit(solution)/shard_map/ppermute | solution.py:136
  40.3 0.0 copy-start.6
  40.3 7.1 %collective-permute-done.2.refs_3_ = bf16[1296,128]{1,0:T(8,128)(2,1)S(1)} collective-permute-done((bf16[1296,128]{1,0:T(8,128)(2,1)S(1)}, bf16[1296,128]{1,0:T(8,128)(2,1)S(1)}, u32[]{:S(2)}, u32[]{:S(2)}) %collective-permute-start.2) | collective-permute-done | bytes 331808 | tf_op jit(solution)/shard_map/ppermute | solution.py:136
  47.4 0.0 copy-done.1
  47.4 0.0 copy-done.2
  47.4 0.0 copy-done.3
  47.4 0.0 copy-done.4
  47.4 0.0 copy-done.5
  47.4 0.0 copy-done.6
  47.4 0.0 copy-start.7
  47.4 0.7 copy-done.7
  48.1 35.1 %attend_project.1 = (bf16[512,1024]{1,0:T(8,128)(2,1)}, bf16[512,1024]{1,0:T(8,128)(2,1)}) custom-call(bf16[1024,1024]{1,0:T(8,128)(2,1)} %w_ref.1, bf16[1296,128]{1,0:T(8,128)(2,1)} %pack.1.refs_0_, bf16[1296,128]{1,0:T(8,128)(2,1)} %copy-done.4, bf16[1296,128]{1,0:T(8,128)(2,1)} %copy-done.3, bf16[1296,128]{1,0:T(8,128)(2,1)} %copy-done.7, ...), custom_call_target="tpu_custom_call" | custom-call | tf_op jit(solution)/shard_map/attend_project/pallas_call | solution.py:166
  83.3 2.1 %collective-permute-start.7 = (bf16[512,1024]{1,0:T(8,128)(2,1)}, bf16[512,1024]{1,0:T(8,128)(2,1)S(1)}, u32[]{:S(2)}, u32[]{:S(2)}) collective-permute-start(bf16[512,1024]{1,0:T(8,128)(2,1)} %get-tuple-element.12), channel_id=1, source_target_pairs={{0,1},{1,0},{2,3},{3,2},{4,5},{5,4},{6,7},{7,6},{8,9},{9,8},{10,11... | collective-permute-start | bytes 3145736 | tf_op jit(solution)/shard_map/ppermute | solution.py:180
  85.4 2.5 %collective-permute-done.7.got_ref = bf16[512,1024]{1,0:T(8,128)(2,1)S(1)} collective-permute-done((bf16[512,1024]{1,0:T(8,128)(2,1)}, bf16[512,1024]{1,0:T(8,128)(2,1)S(1)}, u32[]{:S(2)}, u32[]{:S(2)}) %collective-permute-start.7) | collective-permute-done | bytes 1048608 | tf_op jit(solution)/shard_map/ppermute | solution.py:180
  87.9 1.0 copy-done
  88.9 2.7 %pair_sum.1 = (bf16[128,1024]{1,0:T(8,128)(2,1)}, bf16[128,1024]{1,0:T(8,128)(2,1)}, bf16[128,1024]{1,0:T(8,128)(2,1)}, bf16[128,1024]{1,0:T(8,128)(2,1)}) custom-call(bf16[512,1024]{1,0:T(8,128)(2,1)} %get-tuple-element.11.keep_ref, bf16[512,1024]{1,0:T(8,128)(2,1)} %copy-done), custom_call_target="tpu_custom_call" | custom-call | tf_op jit(solution)/shard_map/pair_sum/pallas_call | solution.py:182
  91.5 5.3 %collective-permute-start.8 = (bf16[128,1024]{1,0:T(8,128)(2,1)}, bf16[128,1024]{1,0:T(8,128)(2,1)S(1)}, u32[]{:S(2)}, u32[]{:S(2)}) collective-permute-start(bf16[128,1024]{1,0:T(8,128)(2,1)} %get-tuple-element.13), channel_id=1, source_target_pairs={{0,0},{1,4},{2,8},{3,12},{4,16},{5,20},{6,24},{7,28},{8,1},{9,5},{... | collective-permute-start | bytes 786440 | tf_op jit(solution)/shard_map/ppermute | solution.py:197
  96.8 1.1 collective-permute-start.9
  97.9 0.0 collective-permute-start.10
  97.9 4.6 %collective-permute-start.11 = (bf16[128,1024]{1,0:T(8,128)(2,1)}, bf16[128,1024]{1,0:T(8,128)(2,1)S(1)}, u32[]{:S(2)}, u32[]{:S(2)}) collective-permute-start(bf16[128,1024]{1,0:T(8,128)(2,1)} %get-tuple-element.16), channel_id=1, source_target_pairs={{0,24},{1,28},{2,16},{3,20},{4,8},{5,12},{6,0},{7,4},{8,25},{9,29}... | collective-permute-start | bytes 786440 | tf_op jit(solution)/shard_map/ppermute | solution.py:197
  102.5 12.1 %collective-permute-done.8.refs_0_ = bf16[128,1024]{1,0:T(8,128)(2,1)S(1)} collective-permute-done((bf16[128,1024]{1,0:T(8,128)(2,1)}, bf16[128,1024]{1,0:T(8,128)(2,1)S(1)}, u32[]{:S(2)}, u32[]{:S(2)}) %collective-permute-start.8) | collective-permute-done | bytes 262176 | tf_op jit(solution)/shard_map/ppermute | solution.py:197
  114.6 6.7 %collective-permute-done.9.refs_1_ = bf16[128,1024]{1,0:T(8,128)(2,1)S(1)} collective-permute-done((bf16[128,1024]{1,0:T(8,128)(2,1)}, bf16[128,1024]{1,0:T(8,128)(2,1)S(1)}, u32[]{:S(2)}, u32[]{:S(2)}) %collective-permute-start.9) | collective-permute-done | bytes 262176 | tf_op jit(solution)/shard_map/ppermute | solution.py:197
  121.3 0.0 collective-permute-done.10.refs_2_
  121.3 1.3 %collective-permute-done.11.refs_3_ = bf16[128,1024]{1,0:T(8,128)(2,1)S(1)} collective-permute-done((bf16[128,1024]{1,0:T(8,128)(2,1)}, bf16[128,1024]{1,0:T(8,128)(2,1)S(1)}, u32[]{:S(2)}, u32[]{:S(2)}) %collective-permute-start.11) | collective-permute-done | bytes 262176 | tf_op jit(solution)/shard_map/ppermute | solution.py:197
  122.7 0.0 copy-done.8
  122.7 0.0 copy-done.9
  122.7 0.0 copy-done.10
  122.7 0.0 copy-start.11
  122.7 0.7 copy-done.11
  123.4 2.1 %final_sum.1 = bf16[128,2048]{1,0:T(8,128)(2,1)} custom-call(bf16[128,1024]{1,0:T(8,128)(2,1)} %copy-done.8, bf16[128,1024]{1,0:T(8,128)(2,1)} %copy-done.9, bf16[128,1024]{1,0:T(8,128)(2,1)} %copy-done.10, bf16[128,1024]{1,0:T(8,128)(2,1)} %copy-done.11), custom_call_target="tpu_custom_call" | custom-call | tf_op jit(solution)/shard_map/final_sum/pallas_call | solution.py:198
  (4 shorter events, 0.0 us)
Async XLA Ops:
  1.9 23.1 %collective-permute-start.5 = (bf16[1296,128]{1,0:T(8,128)(2,1)}, bf16[1296,128]{1,0:T(8,128)(2,1)S(1)}, u32[]{:S(2)}, u32[]{:S(2)}) collective-permute-start(bf16[1296,128]{1,0:T(8,128)(2,1)} %pack.1.refs_0_), channel_id=1, source_target_pairs={{0,24},{4,28},{8,16},{12,20},{16,8},{20,12},{24,0},{28,4},{1,25},{... | collective-permute-start | bytes 995336 | tf_op jit(solution)/shard_map/ppermute | solution.py:136
  2.1 28.3 %collective-permute-start.3 = (bf16[1296,128]{1,0:T(8,128)(2,1)}, bf16[1296,128]{1,0:T(8,128)(2,1)S(1)}, u32[]{:S(2)}, u32[]{:S(2)}) collective-permute-start(bf16[1296,128]{1,0:T(8,128)(2,1)} %pack.1.refs_0_), channel_id=1, source_target_pairs={{0,16},{4,20},{8,24},{12,28},{16,0},{20,4},{24,8},{28,12},{1,17},{... | collective-permute-start | bytes 995336 | tf_op jit(solution)/shard_map/ppermute | solution.py:136
  5.3 26.3 %collective-permute-start.1 = (bf16[1296,128]{1,0:T(8,128)(2,1)}, bf16[1296,128]{1,0:T(8,128)(2,1)S(1)}, u32[]{:S(2)}, u32[]{:S(2)}) collective-permute-start(bf16[1296,128]{1,0:T(8,128)(2,1)} %pack.1.refs_0_), channel_id=1, source_target_pairs={{0,8},{4,12},{8,0},{12,4},{16,24},{20,28},{24,16},{28,20},{1,9},{5... | collective-permute-start | bytes 995336 | tf_op jit(solution)/shard_map/ppermute | solution.py:136
  5.3 26.6 %collective-permute-start = (bf16[1296,128]{1,0:T(8,128)(2,1)}, bf16[1296,128]{1,0:T(8,128)(2,1)S(1)}, u32[]{:S(2)}, u32[]{:S(2)}) collective-permute-start(bf16[1296,128]{1,0:T(8,128)(2,1)} %pack.1.refs_0_), channel_id=1, source_target_pairs={{0,4},{4,0},{8,12},{12,8},{16,20},{20,16},{24,28},{28,24},{1,5},{5... | collective-permute-start | bytes 995336 | tf_op jit(solution)/shard_map/ppermute | solution.py:136
  25.0 22.4 %copy-start.1 = (bf16[1296,128]{1,0:T(8,128)(2,1)}, bf16[1296,128]{1,0:T(8,128)(2,1)S(1)}, u32[]{:S(2)}) copy-start(bf16[1296,128]{1,0:T(8,128)(2,1)S(1)} %collective-permute-done.5.refs_6_) | copy-start | bytes 995332
  25.0 6.9 %collective-permute-start.6 = (bf16[1296,128]{1,0:T(8,128)(2,1)S(1)}, bf16[1296,128]{1,0:T(8,128)(2,1)S(1)}, u32[]{:S(2)}, u32[]{:S(2)}) collective-permute-start(bf16[1296,128]{1,0:T(8,128)(2,1)S(1)} %collective-permute-done.5.refs_6_), channel_id=1, source_target_pairs={{0,4},{4,0},{8,12},{12,8},{16,20},{20,16},{24,28},{28,24},{1,5},{5... | collective-permute-start | bytes 995336 | tf_op jit(solution)/shard_map/ppermute | solution.py:136
  30.4 17.0 %copy-start.2 = (bf16[1296,128]{1,0:T(8,128)(2,1)}, bf16[1296,128]{1,0:T(8,128)(2,1)S(1)}, u32[]{:S(2)}) copy-start(bf16[1296,128]{1,0:T(8,128)(2,1)S(1)} %collective-permute-done.3.refs_4_) | copy-start | bytes 995332
  30.4 9.9 %collective-permute-start.4 = (bf16[1296,128]{1,0:T(8,128)(2,1)S(1)}, bf16[1296,128]{1,0:T(8,128)(2,1)S(1)}, u32[]{:S(2)}, u32[]{:S(2)}) collective-permute-start(bf16[1296,128]{1,0:T(8,128)(2,1)S(1)} %collective-permute-done.3.refs_4_), channel_id=1, source_target_pairs={{0,4},{4,0},{8,12},{12,8},{16,20},{20,16},{24,28},{28,24},{1,5},{5... | collective-permute-start | bytes 995336 | tf_op jit(solution)/shard_map/ppermute | solution.py:136
  31.6 15.8 %copy-start.3 = (bf16[1296,128]{1,0:T(8,128)(2,1)}, bf16[1296,128]{1,0:T(8,128)(2,1)S(1)}, u32[]{:S(2)}) copy-start(bf16[1296,128]{1,0:T(8,128)(2,1)S(1)} %collective-permute-done.1.refs_2_) | copy-start | bytes 995332
  31.6 15.7 %collective-permute-start.2 = (bf16[1296,128]{1,0:T(8,128)(2,1)S(1)}, bf16[1296,128]{1,0:T(8,128)(2,1)S(1)}, u32[]{:S(2)}, u32[]{:S(2)}) collective-permute-start(bf16[1296,128]{1,0:T(8,128)(2,1)S(1)} %collective-permute-done.1.refs_2_), channel_id=1, source_target_pairs={{0,4},{4,0},{8,12},{12,8},{16,20},{20,16},{24,28},{28,24},{1,5},{5... | collective-permute-start | bytes 995336 | tf_op jit(solution)/shard_map/ppermute | solution.py:136
  31.8 15.5 %copy-start.4 = (bf16[1296,128]{1,0:T(8,128)(2,1)}, bf16[1296,128]{1,0:T(8,128)(2,1)S(1)}, u32[]{:S(2)}) copy-start(bf16[1296,128]{1,0:T(8,128)(2,1)S(1)} %collective-permute-done.refs_1_) | copy-start | bytes 995332
  31.9 15.5 %copy-start.5 = (bf16[1296,128]{1,0:T(8,128)(2,1)}, bf16[1296,128]{1,0:T(8,128)(2,1)S(1)}, u32[]{:S(2)}) copy-start(bf16[1296,128]{1,0:T(8,128)(2,1)S(1)} %collective-permute-done.6.refs_7_) | copy-start | bytes 995332
  40.3 7.1 %copy-start.6 = (bf16[1296,128]{1,0:T(8,128)(2,1)}, bf16[1296,128]{1,0:T(8,128)(2,1)S(1)}, u32[]{:S(2)}) copy-start(bf16[1296,128]{1,0:T(8,128)(2,1)S(1)} %collective-permute-done.4.refs_5_) | copy-start | bytes 995332
  47.4 0.7 copy-start.7
  83.3 4.6 %collective-permute-start.7 = (bf16[512,1024]{1,0:T(8,128)(2,1)}, bf16[512,1024]{1,0:T(8,128)(2,1)S(1)}, u32[]{:S(2)}, u32[]{:S(2)}) collective-permute-start(bf16[512,1024]{1,0:T(8,128)(2,1)} %get-tuple-element.12), channel_id=1, source_target_pairs={{0,1},{1,0},{2,3},{3,2},{4,5},{5,4},{6,7},{7,6},{8,9},{9,8},{10,11... | collective-permute-start | bytes 3145736 | tf_op jit(solution)/shard_map/ppermute | solution.py:180
  87.9 1.0 copy-start
  91.5 23.1 %collective-permute-start.8 = (bf16[128,1024]{1,0:T(8,128)(2,1)}, bf16[128,1024]{1,0:T(8,128)(2,1)S(1)}, u32[]{:S(2)}, u32[]{:S(2)}) collective-permute-start(bf16[128,1024]{1,0:T(8,128)(2,1)} %get-tuple-element.13), channel_id=1, source_target_pairs={{0,0},{1,4},{2,8},{3,12},{4,16},{5,20},{6,24},{7,28},{8,1},{9,5},{... | collective-permute-start | bytes 786440 | tf_op jit(solution)/shard_map/ppermute | solution.py:197
  96.8 24.5 %collective-permute-start.9 = (bf16[128,1024]{1,0:T(8,128)(2,1)}, bf16[128,1024]{1,0:T(8,128)(2,1)S(1)}, u32[]{:S(2)}, u32[]{:S(2)}) collective-permute-start(bf16[128,1024]{1,0:T(8,128)(2,1)} %get-tuple-element.14), channel_id=1, source_target_pairs={{0,8},{1,12},{2,0},{3,4},{4,24},{5,28},{6,16},{7,20},{8,9},{9,13},... | collective-permute-start | bytes 786440 | tf_op jit(solution)/shard_map/ppermute | solution.py:197
  97.9 23.4 %collective-permute-start.10 = (bf16[128,1024]{1,0:T(8,128)(2,1)}, bf16[128,1024]{1,0:T(8,128)(2,1)S(1)}, u32[]{:S(2)}, u32[]{:S(2)}) collective-permute-start(bf16[128,1024]{1,0:T(8,128)(2,1)} %get-tuple-element.15), channel_id=1, source_target_pairs={{0,16},{1,20},{2,24},{3,28},{4,0},{5,4},{6,8},{7,12},{8,17},{9,21}... | collective-permute-start | bytes 786440 | tf_op jit(solution)/shard_map/ppermute | solution.py:197
  97.9 24.7 %collective-permute-start.11 = (bf16[128,1024]{1,0:T(8,128)(2,1)}, bf16[128,1024]{1,0:T(8,128)(2,1)S(1)}, u32[]{:S(2)}, u32[]{:S(2)}) collective-permute-start(bf16[128,1024]{1,0:T(8,128)(2,1)} %get-tuple-element.16), channel_id=1, source_target_pairs={{0,24},{1,28},{2,16},{3,20},{4,8},{5,12},{6,0},{7,4},{8,25},{9,29}... | collective-permute-start | bytes 786440 | tf_op jit(solution)/shard_map/ppermute | solution.py:197
  114.6 8.1 %copy-start.8 = (bf16[128,1024]{1,0:T(8,128)(2,1)}, bf16[128,1024]{1,0:T(8,128)(2,1)S(1)}, u32[]{:S(2)}) copy-start(bf16[128,1024]{1,0:T(8,128)(2,1)S(1)} %collective-permute-done.8.refs_0_) | copy-start | bytes 786436
  121.3 1.4 %copy-start.9 = (bf16[128,1024]{1,0:T(8,128)(2,1)}, bf16[128,1024]{1,0:T(8,128)(2,1)S(1)}, u32[]{:S(2)}) copy-start(bf16[128,1024]{1,0:T(8,128)(2,1)S(1)} %collective-permute-done.9.refs_1_) | copy-start | bytes 786436
  121.3 1.4 %copy-start.10 = (bf16[128,1024]{1,0:T(8,128)(2,1)}, bf16[128,1024]{1,0:T(8,128)(2,1)S(1)}, u32[]{:S(2)}) copy-start(bf16[128,1024]{1,0:T(8,128)(2,1)S(1)} %collective-permute-done.10.refs_2_) | copy-start | bytes 786436
  122.7 0.7 copy-start.11

commit v2 on v0

--- a/solution.py
+++ b/solution.py
@@ -1,15 +1,238 @@
+import functools
 import math
 
 import jax
 import jax.numpy as jnp
 from jax import lax
+from jax.experimental import pallas as pl
+from jax.experimental.pallas import tpu as pltpu
 from jax.sharding import PartitionSpec as P
 
 HEAD_DIM = 128
 DOCS = 16
-
-
+META = 16
 NEG_FILL = -1e30
+VMEM_LIMIT = 56 * 1024 * 1024
+
+ANY = pl.BlockSpec(memory_space=pl.ANY)
+VMEM = pl.BlockSpec(memory_space=pltpu.VMEM)
+SMEM = pl.BlockSpec(memory_space=pltpu.SMEM)
+
+
+def pack_kernel(parts, heads, plan_ref, q_ref, k_ref, v_ref, ids_ref, kv_out, send_out, keep_out, meta_out):
+    rows = q_ref.shape[0]
+    piece = rows // parts
+    own = lax.rem(lax.axis_index("head"), 2)
+    lane = lax.rem(lax.broadcasted_iota(jnp.int32, (1, rows), 1), rows // 2)
+    source = jnp.zeros((1, rows), jnp.int32)
+    for a in range(parts // 2):
+        for out_ref, parity in ((keep_out, own), (send_out, 1 - own)):
+            p = plan_ref[0, 2 * a + parity]
+            for h in range(heads):
+                at = h * rows // 2 + a * piece
+                out_ref[at : at + piece, :] = q_ref[
+                    pl.ds(pl.multiple_of(p * piece, piece), piece),
+                    h * HEAD_DIM : (h + 1) * HEAD_DIM,
+                ]
+        p = plan_ref[0, 2 * a + own]
+        inside = (lane >= a * piece) & (lane < (a + 1) * piece)
+        source = jnp.where(inside, (p - a) * piece + lane, source)
+    ids = ids_ref[...].astype(jnp.float32)
+    ids_rows = jnp.broadcast_to(ids, (META, rows))
+    for b in range(parts):
+        kv_out[b, :rows, :] = k_ref[...]
+        kv_out[b, rows : 2 * rows, :] = v_ref[...]
+        kv_out[b, 2 * rows :, :] = ids_rows.astype(jnp.bfloat16)
+    from_row = lax.broadcasted_iota(jnp.int32, (rows, rows), 0)
+    chosen = (from_row == source).astype(jnp.float32)
+    ids_moved = jnp.dot(ids_rows, chosen, preferred_element_type=jnp.float32)
+    row = lax.broadcasted_iota(jnp.int32, (META, rows), 0)
+    positions = jnp.broadcast_to(source.astype(jnp.float32), (META, rows))
+    meta_out[...] = jnp.where(row == 0, ids_moved, positions)
+
+
+def attend_kernel(heads, scale, keep_ref, got_ref, kv_ref, kv_pair_ref, meta_ref, out_ref):
+    parts = kv_ref.shape[0]
+    rows = (kv_ref.shape[1] - META) // 2
+    piece = rows // parts
+    d = lax.axis_index("ctx")
+    turned = meta_ref[...].T
+    q_ids, q_pos = turned[:, 0:1], turned[:, 1:2]
+
+    def ids_of(block):
+        return kv_ref[block, 2 * rows :, :].astype(jnp.float32)[0:1]
+
+    first_id = jnp.min(ids_of(d))
+    start = jnp.int32(0)
+    for b in range(parts):
+        start = start + (jnp.max(ids_of(b)) < first_id).astype(jnp.int32)
+    b0 = lax.div(start, 2) * 2
+    tiles = lax.div(d, 2) + 1 - lax.div(start, 2)
+    for w in range(1, parts // 2 + 1):
+
+        @pl.when(tiles == w)
+        def _(w=w):
+            span = 2 * w * rows
+            k_ids = jnp.concatenate([ids_of(b0 + n) for n in range(2 * w)], axis=1)
+            k_pos = lax.broadcasted_iota(jnp.int32, (1, span), 1) + (b0 - d) * rows
+            allowed = (k_ids == q_ids) & (k_pos.astype(jnp.float32) <= q_pos)
+            bias = jnp.where(allowed, 0.0, NEG_FILL)
+            for side, (q_ref, side_kv) in enumerate(((keep_ref, kv_ref), (got_ref, kv_pair_ref))):
+                keys = side_kv[pl.ds(b0, 2 * w), :rows, :].reshape(span, HEAD_DIM)
+                vals = side_kv[pl.ds(b0, 2 * w), rows : 2 * rows, :].reshape(span, HEAD_DIM)
+                vals = jnp.concatenate([vals, jnp.ones((span, HEAD_DIM), jnp.bfloat16)], axis=1)
+                for t in range(heads // 2):
+                    q = q_ref[t * rows : (t + 1) * rows, :]
+                    s = lax.dot_general(
+                        q, keys, (((1,), (1,)), ((), ())), preferred_element_type=jnp.float32
+                    )
+                    s = s + bias
+                    top = jnp.max(s, axis=1, keepdims=True)
+                    e = jnp.exp2((s - top) * (scale * math.log2(math.e)))
+                    o = jnp.dot(e.astype(jnp.bfloat16), vals, preferred_element_type=jnp.float32)
+                    o = (o[:, :HEAD_DIM] / o[:, HEAD_DIM:]).astype(jnp.bfloat16)
+                    for n in range(2):
+                        col = (side * heads + 2 * t + n) * HEAD_DIM
+                        for a in range(parts // 2):
+                            at = n * rows // 2 + a * piece
+                            out_ref[a, :, col : col + HEAD_DIM] = o[at : at + piece, :]
+
+
+def project_kernel(group, half, wave, parts, *refs):
+    count = parts // 2
+    blocks, refs = refs[:count], refs[count:]
+    w_ref, w_pair_ref, refs = refs[0], refs[1], refs[2:]
+    out_refs, (x_held, w_held, total, sems) = refs[:count], refs[count:]
+    depth = w_ref.shape[0]
+    me = lax.axis_index("ctx")
+    copies = [
+        pltpu.make_async_copy(w_ref, w_held.at[:depth], sems.at[count]),
+        pltpu.make_async_copy(w_pair_ref, w_held.at[depth:], sems.at[count + 1]),
+    ] + [
+        pltpu.make_async_copy(
+            blocks[k], x_held.at[:, jnp.bitwise_xor(lax.rem(me, count), k)], sems.at[k]
+        )
+        for k in range(count)
+    ]
+    for copy in copies:
+        copy.start()
+    for copy in copies:
+        copy.wait()
+    rows = total.shape[0]
+    x = x_held[...].reshape(rows, 2 * depth)
+    total[...] = jnp.dot(x, w_held[...], preferred_element_type=jnp.float32)
+    mine = lax.rem(me, group) * half + lax.div(lax.axis_index("head"), 2)
+    for k, out_ref in enumerate(out_refs):
+        each = rows // count
+        at = pl.ds(pl.multiple_of(jnp.bitwise_xor(mine, k) * each, each), each)
+        out_ref[...] = total[at, :].astype(jnp.bfloat16)
+
+
+def final_kernel(group, half, parts, *refs):
+    blocks, out_ref = refs[:-1], refs[-1]
+    count = len(blocks) // 2
+    rows, cols = blocks[0].shape
+    high = lax.div(lax.axis_index("ctx"), 2)
+    upper = lax.div(lax.axis_index("head") * group, parts // 2)
+    for wave in range(2):
+        at = pl.ds(pl.multiple_of(lax.rem(upper + wave, 2) * rows, rows), rows)
+        for first in range(0, count, half):
+            part = lax.div(jnp.bitwise_xor(high, first), half)
+            total = blocks[wave * count + first][...].astype(jnp.float32)
+            for k in range(first + 1, first + half):
+                total = total + blocks[wave * count + k][...].astype(jnp.float32)
+            out_ref[at, pl.ds(pl.multiple_of(part * cols, cols), cols)] = total.astype(jnp.bfloat16)
+
+
+def along_ctx(x, parts, k):
+    return lax.ppermute(x, "ctx", [(i, i ^ k) for i in range(parts)])
+
+
+def spread_over_ctx(block, parts):
+    half = parts // 2
+    got = {0: block}
+    got[half] = along_ctx(block, parts, half)
+    for k in [*range(2, half, 2), 1]:
+        got[k] = along_ctx(block, parts, k)
+    names = sorted(got)
+    held = dict(zip(names, lax.optimization_barrier([got[k] for k in names])))
+    for k in range(2, half, 2):
+        got[half + k] = along_ctx(held[half], parts, k)
+    for k in range(2, half + 1, 2):
+        got[k + 1] = along_ctx(held[k], parts, 1)
+    for k in range(half + 2, parts, 2):
+        got[k + 1] = along_ctx(got[k], parts, 1)
+    return [got[k] for k in range(parts)]
+
+
+def packed_body(groups, queries, keys, values, doc_ids, plan, w_out):
+    parts = lax.axis_size("ctx")
+    rows = queries.shape[0]
+    heads = queries.shape[1] // HEAD_DIM
+    depth, width = w_out.shape
+    group, half = parts // groups, groups // 2
+    count, piece = parts // 2, rows // parts
+    bf16 = jnp.bfloat16
+    params = pltpu.CompilerParams(vmem_limit_bytes=VMEM_LIMIT)
+    pair = [(g, g ^ 1) for g in range(groups)]
+    kv_rows = 2 * rows + META
+    w_pair = lax.ppermute(w_out, "head", pair)
+    kv_copies, q_send, q_keep, meta = pl.pallas_call(
+        functools.partial(pack_kernel, parts, heads),
+        out_shape=[
+            jax.ShapeDtypeStruct((parts, kv_rows, HEAD_DIM), bf16),
+            jax.ShapeDtypeStruct((heads * rows // 2, HEAD_DIM), bf16),
+            jax.ShapeDtypeStruct((heads * rows // 2, HEAD_DIM), bf16),
+            jax.ShapeDtypeStruct((META, rows), jnp.float32),
+        ],
+        in_specs=[SMEM, VMEM, VMEM, VMEM, VMEM],
+        out_specs=[VMEM] * 4,
+        compiler_params=params,
+        name="pack",
+    )(plan, queries, keys, values, doc_ids.reshape(1, rows))
+    q_got = lax.ppermute(q_send, "head", pair)
+    kv = lax.all_to_all(kv_copies, "ctx", split_axis=0, concat_axis=0, tiled=True)
+    kv_pair = lax.ppermute(kv, "head", pair)
+    attended = pl.pallas_call(
+        functools.partial(attend_kernel, heads, 1.0 / math.sqrt(HEAD_DIM)),
+        out_shape=jax.ShapeDtypeStruct((count, piece, 2 * depth), bf16),
+        in_specs=[VMEM] * 5,
+        out_specs=VMEM,
+        compiler_params=params,
+        name="attend",
+    )(q_keep, q_got, kv, kv_pair, meta)
+    blocks = spread_over_ctx(attended, parts)
+    arrived = []
+    for wave in range(2):
+        sums = pl.pallas_call(
+            functools.partial(project_kernel, group, half, wave, parts),
+            out_shape=[jax.ShapeDtypeStruct((rows // 2, width), bf16)] * count,
+            in_specs=[ANY] * (count + 2),
+            out_specs=[VMEM] * count,
+            scratch_shapes=[
+                pltpu.VMEM((count, count, piece, 2 * depth), bf16),
+                pltpu.VMEM((2 * depth, width), bf16),
+                pltpu.VMEM((count * rows // 2, width), jnp.float32),
+                pltpu.SemaphoreType.DMA((count + 2,)),
+            ],
+            compiler_params=params,
+            name="project",
+        )(*blocks[wave * count : (wave + 1) * count], w_out, w_pair)
+        for k in range(count):
+            pairs = []
+            for c in range(parts):
+                for g in range(groups):
+                    high = ((c % group) * half + g // 2) ^ k
+                    pairs.append((c * groups + g, (high * 2 + g % 2) * groups + c // group))
+            arrived.append(lax.ppermute(sums[k], ("ctx", "head"), pairs))
+    return pl.pallas_call(
+        functools.partial(final_kernel, group, half, parts),
+        out_shape=jax.ShapeDtypeStruct((rows, group * width), bf16),
+        in_specs=[VMEM] * (2 * count),
+        out_specs=VMEM,
+        compiler_params=params,
+        name="final_sum",
+    )(*arrived)
 
 
 def spread_rows(block, order, parts):
@@ -139,9 +362,24 @@
     return summed
 
 
+def fits(parts, groups, rows, width):
+    powers = all(n & (n - 1) == 0 for n in (parts, groups))
+    window = parts * rows * width * 2
+    whole = rows % (16 * parts) == 0 and groups % 2 == 0 and parts % groups == 0
+    return powers and whole and 8 * window <= VMEM_LIMIT
+
+
 def solution(mesh):
+    parts, groups = mesh.shape["ctx"], mesh.shape["head"]
+
+    def one_device(queries, keys, values, doc_ids, plan, w_out):
+        one_pair = keys.shape[1] == HEAD_DIM
+        if one_pair and fits(parts, groups, queries.shape[0], queries.shape[1]):
+            return packed_body(groups, queries, keys, values, doc_ids, plan, w_out)
+        return body(queries, keys, values, doc_ids, plan, w_out)
+
     return jax.shard_map(
-        body,
+        one_device,
         mesh=mesh,
         in_specs=(
             P("ctx", "head"),

time: 284 us -> 103 us (0.36)
  the two profiles are of different devices: /device:TPU:17 before, /device:TPU:1 now
where the time goes in v2:
time: 103 us; the launch traced here: 102 us
  waiting for transfers between devices  41.9 us (41%)
  starting transfers between devices  39.7 us (39%)
  Pallas kernels  16.1 us (16%)
  local copies, waits for them, and re-layouts  4.31 us (4%)
    ppermute x8, starting transfers between devices, packed_body(): arrived.append(lax.ppermute(sums[k], ('ctx', 'head'), pairs))  26.1 us
    ppermute x7, waiting for transfers between devices, along_ctx(): return lax.ppermute(x, 'ctx', [(i, i ^ k) for i in range(parts)])  17.6 us
    all_to_all x1, waiting for transfers between devices, packed_body(): lax.all_to_all(kv_copies, 'ctx', split_axis=0, concat_axis=0, tiled=True)  13 us
    ppermute x8, waiting for transfers between devices, packed_body(): arrived.append(lax.ppermute(sums[k], ('ctx', 'head'), pairs))  9.34 us
    pallas_call x2, Pallas kernels, packed_body(): pl.pallas_call(functools.partial(project_kernel, group, half, wave, parts...  9.1 us
    all_to_all x1, starting transfers between devices, packed_body(): lax.all_to_all(kv_copies, 'ctx', split_axis=0, concat_axis=0, tiled=True)  6.38 us
    unnamed x38, local copies, waits for them, and re-layouts  4.31 us
    ppermute x7, starting transfers between devices, along_ctx(): return lax.ppermute(x, 'ctx', [(i, i ^ k) for i in range(parts)])  4.14 us
  transfers between devices with their start and end apart: 19, of which 9 were waited for; matrix products, arithmetic and copies ran while one was open for 0% of the time, Pallas kernels for 12%

profile of v2, /device:TPU:1, one launch (start us, length us, event | category | flops | bytes accessed | tf_op | source)
XLA Modules:
  0.0 102.2 jit_solution(3800991971814168648)
XLA Ops:
  0.0 1.9 %pack.1 = (bf16[8,272,128]{2,1,0:T(8,128)(2,1)}, bf16[512,128]{1,0:T(8,128)(2,1)}, bf16[512,128]{1,0:T(8,128)(2,1)}, f32[16,128]{1,0:T(8,128)}) custom-call(s32[1,8]{1,0:T(1,128)} %plan_ref.1, bf16[128,1024]{1,0:T(8,128)(2,1)} %q_ref.1, bf16[128,128]{1,0:T(8,128)(2,1)} %k_ref.1, bf16[128,128]{1,0:T(8,128)(2,1)} %v_ref.1, s32[1,128]{1,0:T(1,128)} %bitcast.1), custom_call_target="tpu_custom_call" | custom-call | tf_op jit(solution)/shard_map/pack/pallas_call | solution.py:180
  1.9 6.4 %all-to-all-start = ((bf16[8,272,128]{2,1,0:T(8,128)(2,1)}), bf16[8,272,128]{2,1,0:T(8,128)(2,1)S(1)}, u32[]{:S(2)}, u32[]{:S(2)}) async-start(bf16[8,272,128]{2,1,0:T(8,128)(2,1)} %get-tuple-element.21), calls=%async_computation | async-start | bytes 1114112 | tf_op jit(solution)/shard_map/all_to_all | solution.py:194
  8.3 1.0 collective-permute-start.6
  9.3 13.0 %all-to-all-done.kv_ref = bf16[8,272,128]{2,1,0:T(8,128)(2,1)S(1)} async-done(((bf16[8,272,128]{2,1,0:T(8,128)(2,1)}), bf16[8,272,128]{2,1,0:T(8,128)(2,1)S(1)}, u32[]{:S(2)}, u32[]{:S(2)}) %all-to-all-start) | async-done | bytes 557088 | tf_op jit(solution)/shard_map/all_to_all | solution.py:194
  22.3 2.2 %collective-permute-start.1 = (bf16[8,272,128]{2,1,0:T(8,128)(2,1)S(1)}, bf16[8,272,128]{2,1,0:T(8,128)(2,1)S(1)}, u32[]{:S(2)}, u32[]{:S(2)}) collective-permute-start(bf16[8,272,128]{2,1,0:T(8,128)(2,1)S(1)} %all-to-all-done.kv_ref), channel_id=1, source_target_pairs={{0,1},{1,0},{2,3},{3,2},{4,5},{5,4},{6,7},{7,6},{8,9},{9,8},{10,11... | collective-permute-start | bytes 1671176 | tf_op jit(solution)/shard_map/ppermute | solution.py:195
  24.5 0.0 collective-permute-start
  24.5 1.8 %collective-permute-done.got_ref = bf16[512,128]{1,0:T(8,128)(2,1)S(1)} collective-permute-done((bf16[512,128]{1,0:T(8,128)(2,1)}, bf16[512,128]{1,0:T(8,128)(2,1)S(1)}, u32[]{:S(2)}, u32[]{:S(2)}) %collective-permute-start) | collective-permute-done | bytes 131104 | tf_op jit(solution)/shard_map/ppermute | solution.py:193
  26.3 0.0 collective-permute-done.1.kv_pair_ref
  26.3 0.6 copy-done.18
  27.0 0.2 copy-done.2
  27.2 2.8 %attend.1.refs_0_ = bf16[4,16,2048]{2,1,0:T(8,128)(2,1)} custom-call(bf16[512,128]{1,0:T(8,128)(2,1)} %get-tuple-element.19.keep_ref, bf16[512,128]{1,0:T(8,128)(2,1)} %copy-done.18, bf16[8,272,128]{2,1,0:T(8,128)(2,1)} %copy-done.1, bf16[8,272,128]{2,1,0:T(8,128)(2,1)} %copy-done.2, f32[16,128]{1,0:T(8,128)} %get-tuple-element.22.meta_ref), custom_call_target="tpu_custom_call" | custom-call | tf_op jit(solution)/shard_map/attend/pallas_call | solution.py:196
  30.0 1.2 %collective-permute-start.2 = (bf16[4,16,2048]{2,1,0:T(8,128)(2,1)}, bf16[4,16,2048]{2,1,0:T(8,128)(2,1)S(1)}, u32[]{:S(2)}, u32[]{:S(2)}) collective-permute-start(bf16[4,16,2048]{2,1,0:T(8,128)(2,1)} %attend.1.refs_0_), channel_id=1, source_target_pairs={{0,4},{4,0},{8,12},{12,8},{16,20},{20,16},{24,28},{28,24},{1,5},{5... | collective-permute-start | bytes 786440 | tf_op jit(solution)/shard_map/ppermute | solution.py:148
  31.2 0.0 collective-permute-start.3
  31.2 1.5 %collective-permute-start.4 = (bf16[4,16,2048]{2,1,0:T(8,128)(2,1)}, bf16[4,16,2048]{2,1,0:T(8,128)(2,1)S(1)}, u32[]{:S(2)}, u32[]{:S(2)}) collective-permute-start(bf16[4,16,2048]{2,1,0:T(8,128)(2,1)} %attend.1.refs_0_), channel_id=1, source_target_pairs={{0,16},{4,20},{8,24},{12,28},{16,0},{20,4},{24,8},{28,12},{1,17},{... | collective-permute-start | bytes 786440 | tf_op jit(solution)/shard_map/ppermute | solution.py:148
  32.7 5.2 %collective-permute-done.2.refs_1_ = bf16[4,16,2048]{2,1,0:T(8,128)(2,1)S(1)} collective-permute-done((bf16[4,16,2048]{2,1,0:T(8,128)(2,1)}, bf16[4,16,2048]{2,1,0:T(8,128)(2,1)S(1)}, u32[]{:S(2)}, u32[]{:S(2)}) %collective-permute-start.2) | collective-permute-done | bytes 262176 | tf_op jit(solution)/shard_map/ppermute | solution.py:148
  37.9 5.5 %collective-permute-done.3.refs_2_ = bf16[4,16,2048]{2,1,0:T(8,128)(2,1)S(1)} collective-permute-done((bf16[4,16,2048]{2,1,0:T(8,128)(2,1)}, bf16[4,16,2048]{2,1,0:T(8,128)(2,1)S(1)}, u32[]{:S(2)}, u32[]{:S(2)}) %collective-permute-start.3) | collective-permute-done | bytes 262176 | tf_op jit(solution)/shard_map/ppermute | solution.py:148
  43.4 1.9 %collective-permute-done.4.refs_0_ = bf16[4,16,2048]{2,1,0:T(8,128)(2,1)S(1)} collective-permute-done((bf16[4,16,2048]{2,1,0:T(8,128)(2,1)}, bf16[4,16,2048]{2,1,0:T(8,128)(2,1)S(1)}, u32[]{:S(2)}, u32[]{:S(2)}) %collective-permute-start.4) | collective-permute-done | bytes 262176 | tf_op jit(solution)/shard_map/ppermute | solution.py:148
  45.4 0.0 collective-permute-start.12
  45.4 0.5 collective-permute-start.5
  45.8 1.0 collective-permute-start.11
  46.8 5.0 %collective-permute-done.12.refs_2_ = bf16[4,16,2048]{2,1,0:T(8,128)(2,1)S(1)} collective-permute-done((bf16[4,16,2048]{2,1,0:T(8,128)(2,1)S(1)}, bf16[4,16,2048]{2,1,0:T(8,128)(2,1)S(1)}, u32[]{:S(2)}, u32[]{:S(2)}) %collective-permute-start.12) | collective-permute-done | bytes 262176 | tf_op jit(solution)/shard_map/ppermute | solution.py:148
  51.8 0.0 collective-permute-start.13
  51.8 0.0 collective-permute-done.5.refs_3_
  51.8 0.0 collective-permute-done.6.refs_5_
  51.9 0.7 copy-done.9
  52.6 1.4 %copy-done = bf16[1024,1024]{1,0:T(8,128)(2,1)} copy-done((bf16[1024,1024]{1,0:T(8,128)(2,1)}, bf16[1024,1024]{1,0:T(8,128)(2,1)S(1)}, u32[]{:S(2)}) %copy-start) | copy-done | bytes 2097176
  53.9 4.5 %project.2 = (bf16[64,1024]{1,0:T(8,128)(2,1)}, bf16[64,1024]{1,0:T(8,128)(2,1)}, bf16[64,1024]{1,0:T(8,128)(2,1)}, bf16[64,1024]{1,0:T(8,128)(2,1)}) custom-call(bf16[4,16,2048]{2,1,0:T(8,128)(2,1)} %attend.1.refs_0_, bf16[4,16,2048]{2,1,0:T(8,128)(2,1)} %copy-done.6, bf16[4,16,2048]{2,1,0:T(8,128)(2,1)} %copy-done.8, bf16[4,16,2048]{2,1,0:T(8,128)(2,1)} %copy-done.9, ...), custom_call_target="tpu_custom_call" | custom-call | tf_op jit(solution)/shard_map/project/pallas_call | solution.py:207
  58.5 7.0 %collective-permute-start.7 = (bf16[64,1024]{1,0:T(8,128)(2,1)}, bf16[64,1024]{1,0:T(8,128)(2,1)S(1)}, u32[]{:S(2)}, u32[]{:S(2)}) collective-permute-start(bf16[64,1024]{1,0:T(8,128)(2,1)} %get-tuple-element.24), channel_id=1, source_target_pairs={{0,0},{1,4},{2,8},{3,12},{4,16},{5,20},{6,24},{7,28},{8,1},{9,5},{... | collective-permute-start | bytes 393224 | tf_op jit(solution)/shard_map/ppermute | solution.py:227
  65.4 1.5 %collective-permute-start.8 = (bf16[64,1024]{1,0:T(8,128)(2,1)}, bf16[64,1024]{1,0:T(8,128)(2,1)S(1)}, u32[]{:S(2)}, u32[]{:S(2)}) collective-permute-start(bf16[64,1024]{1,0:T(8,128)(2,1)} %get-tuple-element.25), channel_id=1, source_target_pairs={{0,8},{1,12},{2,0},{3,4},{4,24},{5,28},{6,16},{7,20},{8,9},{9,13},... | collective-permute-start | bytes 393224 | tf_op jit(solution)/shard_map/ppermute | solution.py:227
  67.0 1.8 %collective-permute-start.9 = (bf16[64,1024]{1,0:T(8,128)(2,1)}, bf16[64,1024]{1,0:T(8,128)(2,1)S(1)}, u32[]{:S(2)}, u32[]{:S(2)}) collective-permute-start(bf16[64,1024]{1,0:T(8,128)(2,1)} %get-tuple-element.26), channel_id=1, source_target_pairs={{0,16},{1,20},{2,24},{3,28},{4,0},{5,4},{6,8},{7,12},{8,17},{9,21}... | collective-permute-start | bytes 393224 | tf_op jit(solution)/shard_map/ppermute | solution.py:227
  68.8 0.0 collective-permute-done.11.refs_1_
  68.8 6.2 %collective-permute-start.10 = (bf16[64,1024]{1,0:T(8,128)(2,1)}, bf16[64,1024]{1,0:T(8,128)(2,1)S(1)}, u32[]{:S(2)}, u32[]{:S(2)}) collective-permute-start(bf16[64,1024]{1,0:T(8,128)(2,1)} %get-tuple-element.27), channel_id=1, source_target_pairs={{0,24},{1,28},{2,16},{3,20},{4,8},{5,12},{6,0},{7,4},{8,25},{9,29}... | collective-permute-start | bytes 393224 | tf_op jit(solution)/shard_map/ppermute | solution.py:227
  75.0 0.0 collective-permute-done.13.refs_3_
  75.1 0.7 copy-done.7
  75.8 4.5 %project.3 = (bf16[64,1024]{1,0:T(8,128)(2,1)}, bf16[64,1024]{1,0:T(8,128)(2,1)}, bf16[64,1024]{1,0:T(8,128)(2,1)}, bf16[64,1024]{1,0:T(8,128)(2,1)}) custom-call(bf16[4,16,2048]{2,1,0:T(8,128)(2,1)} %copy-done.3, bf16[4,16,2048]{2,1,0:T(8,128)(2,1)} %copy-done.5, bf16[4,16,2048]{2,1,0:T(8,128)(2,1)} %copy-done.4, bf16[4,16,2048]{2,1,0:T(8,128)(2,1)} %copy-done.7, ...), custom_call_target="tpu_custom_call" | custom-call | tf_op jit(solution)/shard_map/project/pallas_call | solution.py:207
  80.3 1.9 %collective-permute-start.14 = (bf16[64,1024]{1,0:T(8,128)(2,1)}, bf16[64,1024]{1,0:T(8,128)(2,1)S(1)}, u32[]{:S(2)}, u32[]{:S(2)}) collective-permute-start(bf16[64,1024]{1,0:T(8,128)(2,1)} %get-tuple-element.29), channel_id=1, source_target_pairs={{0,0},{1,4},{2,8},{3,12},{4,16},{5,20},{6,24},{7,28},{8,1},{9,5},{... | collective-permute-start | bytes 393224 | tf_op jit(solution)/shard_map/ppermute | solution.py:227
  82.3 0.0 collective-permute-done.7.refs_0_
  82.3 1.3 %collective-permute-start.15 = (bf16[64,1024]{1,0:T(8,128)(2,1)}, bf16[64,1024]{1,0:T(8,128)(2,1)S(1)}, u32[]{:S(2)}, u32[]{:S(2)}) collective-permute-start(bf16[64,1024]{1,0:T(8,128)(2,1)} %get-tuple-element.30), channel_id=1, source_target_pairs={{0,8},{1,12},{2,0},{3,4},{4,24},{5,28},{6,16},{7,20},{8,9},{9,13},... | collective-permute-start | bytes 393224 | tf_op jit(solution)/shard_map/ppermute | solution.py:227
  83.5 0.0 collective-permute-done.8.refs_1_
  83.6 3.1 %collective-permute-start.16 = (bf16[64,1024]{1,0:T(8,128)(2,1)}, bf16[64,1024]{1,0:T(8,128)(2,1)S(1)}, u32[]{:S(2)}, u32[]{:S(2)}) collective-permute-start(bf16[64,1024]{1,0:T(8,128)(2,1)} %get-tuple-element.31), channel_id=1, source_target_pairs={{0,16},{1,20},{2,24},{3,28},{4,0},{5,4},{6,8},{7,12},{8,17},{9,21}... | collective-permute-start | bytes 393224 | tf_op jit(solution)/shard_map/ppermute | solution.py:227
  86.7 3.2 %collective-permute-start.17 = (bf16[64,1024]{1,0:T(8,128)(2,1)}, bf16[64,1024]{1,0:T(8,128)(2,1)S(1)}, u32[]{:S(2)}, u32[]{:S(2)}) collective-permute-start(bf16[64,1024]{1,0:T(8,128)(2,1)} %get-tuple-element.32), channel_id=1, source_target_pairs={{0,24},{1,28},{2,16},{3,20},{4,8},{5,12},{6,0},{7,4},{8,25},{9,29}... | collective-permute-start | bytes 393224 | tf_op jit(solution)/shard_map/ppermute | solution.py:227
  89.9 0.0 collective-permute-done.10.refs_3_
  89.9 1.1 %collective-permute-done.14.refs_4_ = bf16[64,1024]{1,0:T(8,128)(2,1)S(1)} collective-permute-done((bf16[64,1024]{1,0:T(8,128)(2,1)}, bf16[64,1024]{1,0:T(8,128)(2,1)S(1)}, u32[]{:S(2)}, u32[]{:S(2)}) %collective-permute-start.14) | collective-permute-done | bytes 131104 | tf_op jit(solution)/shard_map/ppermute | solution.py:227
  91.1 0.0 collective-permute-done.15.refs_5_
  91.1 1.3 %collective-permute-done.16.refs_6_ = bf16[64,1024]{1,0:T(8,128)(2,1)S(1)} collective-permute-done((bf16[64,1024]{1,0:T(8,128)(2,1)}, bf16[64,1024]{1,0:T(8,128)(2,1)S(1)}, u32[]{:S(2)}, u32[]{:S(2)}) %collective-permute-start.16) | collective-permute-done | bytes 131104 | tf_op jit(solution)/shard_map/ppermute | solution.py:227
  92.4 6.9 %collective-permute-done.17.refs_7_ = bf16[64,1024]{1,0:T(8,128)(2,1)S(1)} collective-permute-done((bf16[64,1024]{1,0:T(8,128)(2,1)}, bf16[64,1024]{1,0:T(8,128)(2,1)S(1)}, u32[]{:S(2)}, u32[]{:S(2)}) %collective-permute-start.17) | collective-permute-done | bytes 131104 | tf_op jit(solution)/shard_map/ppermute | solution.py:227
  99.3 0.6 copy-done.17
  100.0 2.2 %final_sum.1 = bf16[128,2048]{1,0:T(8,128)(2,1)} custom-call(bf16[64,1024]{1,0:T(8,128)(2,1)} %copy-done.10, bf16[64,1024]{1,0:T(8,128)(2,1)} %copy-done.11, bf16[64,1024]{1,0:T(8,128)(2,1)} %copy-done.12, bf16[64,1024]{1,0:T(8,128)(2,1)} %copy-done.13, bf16[64,1024]{1,0:T(8,128)(2,1)} %copy-done.14, bf16[64,1024]{1,0:T(8,128)(2,1)} %copy-done.15, ...), custom_call_target="tpu_custom_call" | custom-call | tf_op jit(solution)/shard_map/final_sum/pallas_call | solution.py:228
  (33 shorter events, 0.1 us)
Async XLA Ops:
  1.9 20.4 %all-to-all-start = ((bf16[8,272,128]{2,1,0:T(8,128)(2,1)}), bf16[8,272,128]{2,1,0:T(8,128)(2,1)S(1)}, u32[]{:S(2)}, u32[]{:S(2)}) async-start(bf16[8,272,128]{2,1,0:T(8,128)(2,1)} %get-tuple-element.21), calls=%async_computation | async-start | bytes 1114112 | tf_op jit(solution)/shard_map/all_to_all | solution.py:194
  8.3 43.5 %collective-permute-start.6 = (bf16[1024,1024]{1,0:T(8,128)(2,1)}, bf16[1024,1024]{1,0:T(8,128)(2,1)S(1)}, u32[]{:S(2)}, u32[]{:S(2)}) collective-permute-start(bf16[1024,1024]{1,0:T(8,128)(2,1)} %refs_4_.3), channel_id=1, source_target_pairs={{0,1},{1,0},{2,3},{3,2},{4,5},{5,4},{6,7},{7,6},{8,9},{9,8},{10,11... | collective-permute-start | bytes 6291464 | tf_op jit(solution)/shard_map/ppermute | solution.py:179
  22.3 4.0 %copy-start.1 = (bf16[8,272,128]{2,1,0:T(8,128)(2,1)}, bf16[8,272,128]{2,1,0:T(8,128)(2,1)S(1)}, u32[]{:S(2)}) copy-start(bf16[8,272,128]{2,1,0:T(8,128)(2,1)S(1)} %all-to-all-done.kv_ref) | copy-start | bytes 1671172
  22.3 4.0 %collective-permute-start.1 = (bf16[8,272,128]{2,1,0:T(8,128)(2,1)S(1)}, bf16[8,272,128]{2,1,0:T(8,128)(2,1)S(1)}, u32[]{:S(2)}, u32[]{:S(2)}) collective-permute-start(bf16[8,272,128]{2,1,0:T(8,128)(2,1)S(1)} %all-to-all-done.kv_ref), channel_id=1, source_target_pairs={{0,1},{1,0},{2,3},{3,2},{4,5},{5,4},{6,7},{7,6},{8,9},{9,8},{10,11... | collective-permute-start | bytes 1671176 | tf_op jit(solution)/shard_map/ppermute | solution.py:195
  24.5 1.8 %collective-permute-start = (bf16[512,128]{1,0:T(8,128)(2,1)}, bf16[512,128]{1,0:T(8,128)(2,1)S(1)}, u32[]{:S(2)}, u32[]{:S(2)}) collective-permute-start(bf16[512,128]{1,0:T(8,128)(2,1)} %get-tuple-element.20), channel_id=1, source_target_pairs={{0,1},{1,0},{2,3},{3,2},{4,5},{5,4},{6,7},{7,6},{8,9},{9,8},{10,11... | collective-permute-start | bytes 393224 | tf_op jit(solution)/shard_map/ppermute | solution.py:193
  26.3 0.7 copy-start.18
  26.3 0.9 copy-start.2
  30.0 7.9 %collective-permute-start.2 = (bf16[4,16,2048]{2,1,0:T(8,128)(2,1)}, bf16[4,16,2048]{2,1,0:T(8,128)(2,1)S(1)}, u32[]{:S(2)}, u32[]{:S(2)}) collective-permute-start(bf16[4,16,2048]{2,1,0:T(8,128)(2,1)} %attend.1.refs_0_), channel_id=1, source_target_pairs={{0,4},{4,0},{8,12},{12,8},{16,20},{20,16},{24,28},{28,24},{1,5},{5... | collective-permute-start | bytes 786440 | tf_op jit(solution)/shard_map/ppermute | solution.py:148
  31.2 12.2 %collective-permute-start.3 = (bf16[4,16,2048]{2,1,0:T(8,128)(2,1)}, bf16[4,16,2048]{2,1,0:T(8,128)(2,1)S(1)}, u32[]{:S(2)}, u32[]{:S(2)}) collective-permute-start(bf16[4,16,2048]{2,1,0:T(8,128)(2,1)} %attend.1.refs_0_), channel_id=1, source_target_pairs={{0,8},{4,12},{8,0},{12,4},{16,24},{20,28},{24,16},{28,20},{1,9},{5... | collective-permute-start | bytes 786440 | tf_op jit(solution)/shard_map/ppermute | solution.py:148
  31.2 14.1 %collective-permute-start.4 = (bf16[4,16,2048]{2,1,0:T(8,128)(2,1)}, bf16[4,16,2048]{2,1,0:T(8,128)(2,1)S(1)}, u32[]{:S(2)}, u32[]{:S(2)}) collective-permute-start(bf16[4,16,2048]{2,1,0:T(8,128)(2,1)} %attend.1.refs_0_), channel_id=1, source_target_pairs={{0,16},{4,20},{8,24},{12,28},{16,0},{20,4},{24,8},{28,12},{1,17},{... | collective-permute-start | bytes 786440 | tf_op jit(solution)/shard_map/ppermute | solution.py:148
  37.9 13.9 %copy-start.6 = (bf16[4,16,2048]{2,1,0:T(8,128)(2,1)}, bf16[4,16,2048]{2,1,0:T(8,128)(2,1)S(1)}, u32[]{:S(2)}) copy-start(bf16[4,16,2048]{2,1,0:T(8,128)(2,1)S(1)} %collective-permute-done.2.refs_1_) | copy-start | bytes 786436
  43.4 8.4 %copy-start.8 = (bf16[4,16,2048]{2,1,0:T(8,128)(2,1)}, bf16[4,16,2048]{2,1,0:T(8,128)(2,1)S(1)}, u32[]{:S(2)}) copy-start(bf16[4,16,2048]{2,1,0:T(8,128)(2,1)S(1)} %collective-permute-done.3.refs_2_) | copy-start | bytes 786436
  45.4 29.7 %copy-start.3 = (bf16[4,16,2048]{2,1,0:T(8,128)(2,1)}, bf16[4,16,2048]{2,1,0:T(8,128)(2,1)S(1)}, u32[]{:S(2)}) copy-start(bf16[4,16,2048]{2,1,0:T(8,128)(2,1)S(1)} %collective-permute-done.4.refs_0_) | copy-start | bytes 786436
  45.4 6.4 %collective-permute-start.12 = (bf16[4,16,2048]{2,1,0:T(8,128)(2,1)S(1)}, bf16[4,16,2048]{2,1,0:T(8,128)(2,1)S(1)}, u32[]{:S(2)}, u32[]{:S(2)}) collective-permute-start(bf16[4,16,2048]{2,1,0:T(8,128)(2,1)S(1)} %collective-permute-done.4.refs_0_), channel_id=1, source_target_pairs={{0,8},{4,12},{8,0},{12,4},{16,24},{20,28},{24,16},{28,20},{1,9},{5... | collective-permute-start | bytes 786440 | tf_op jit(solution)/shard_map/ppermute | solution.py:148
  45.4 6.5 %collective-permute-start.5 = (bf16[4,16,2048]{2,1,0:T(8,128)(2,1)S(1)}, bf16[4,16,2048]{2,1,0:T(8,128)(2,1)S(1)}, u32[]{:S(2)}, u32[]{:S(2)}) collective-permute-start(bf16[4,16,2048]{2,1,0:T(8,128)(2,1)S(1)} %collective-permute-done.3.refs_2_), channel_id=1, source_target_pairs={{0,4},{4,0},{8,12},{12,8},{16,20},{20,16},{24,28},{28,24},{1,5},{5... | collective-permute-start | bytes 786440 | tf_op jit(solution)/shard_map/ppermute | solution.py:148
  45.8 22.9 %collective-permute-start.11 = (bf16[4,16,2048]{2,1,0:T(8,128)(2,1)S(1)}, bf16[4,16,2048]{2,1,0:T(8,128)(2,1)S(1)}, u32[]{:S(2)}, u32[]{:S(2)}) collective-permute-start(bf16[4,16,2048]{2,1,0:T(8,128)(2,1)S(1)} %collective-permute-done.4.refs_0_), channel_id=1, source_target_pairs={{0,4},{4,0},{8,12},{12,8},{16,20},{20,16},{24,28},{28,24},{1,5},{5... | collective-permute-start | bytes 786440 | tf_op jit(solution)/shard_map/ppermute | solution.py:148
  51.8 23.2 %copy-start.4 = (bf16[4,16,2048]{2,1,0:T(8,128)(2,1)}, bf16[4,16,2048]{2,1,0:T(8,128)(2,1)S(1)}, u32[]{:S(2)}) copy-start(bf16[4,16,2048]{2,1,0:T(8,128)(2,1)S(1)} %collective-permute-done.12.refs_2_) | copy-start | bytes 786436
  51.8 23.2 %collective-permute-start.13 = (bf16[4,16,2048]{2,1,0:T(8,128)(2,1)S(1)}, bf16[4,16,2048]{2,1,0:T(8,128)(2,1)S(1)}, u32[]{:S(2)}, u32[]{:S(2)}) collective-permute-start(bf16[4,16,2048]{2,1,0:T(8,128)(2,1)S(1)} %collective-permute-done.12.refs_2_), channel_id=1, source_target_pairs={{0,4},{4,0},{8,12},{12,8},{16,20},{20,16},{24,28},{28,24},{1,5},{5... | collective-permute-start | bytes 786440 | tf_op jit(solution)/shard_map/ppermute | solution.py:148
  51.8 0.7 copy-start.9
  52.6 1.4 %copy-start = (bf16[1024,1024]{1,0:T(8,128)(2,1)}, bf16[1024,1024]{1,0:T(8,128)(2,1)S(1)}, u32[]{:S(2)}) copy-start(bf16[1024,1024]{1,0:T(8,128)(2,1)S(1)} %collective-permute-done.6.refs_5_) | copy-start | bytes 6291460
  58.5 23.8 %collective-permute-start.7 = (bf16[64,1024]{1,0:T(8,128)(2,1)}, bf16[64,1024]{1,0:T(8,128)(2,1)S(1)}, u32[]{:S(2)}, u32[]{:S(2)}) collective-permute-start(bf16[64,1024]{1,0:T(8,128)(2,1)} %get-tuple-element.24), channel_id=1, source_target_pairs={{0,0},{1,4},{2,8},{3,12},{4,16},{5,20},{6,24},{7,28},{8,1},{9,5},{... | collective-permute-start | bytes 393224 | tf_op jit(solution)/shard_map/ppermute | solution.py:227
  65.4 18.1 %collective-permute-start.8 = (bf16[64,1024]{1,0:T(8,128)(2,1)}, bf16[64,1024]{1,0:T(8,128)(2,1)S(1)}, u32[]{:S(2)}, u32[]{:S(2)}) collective-permute-start(bf16[64,1024]{1,0:T(8,128)(2,1)} %get-tuple-element.25), channel_id=1, source_target_pairs={{0,8},{1,12},{2,0},{3,4},{4,24},{5,28},{6,16},{7,20},{8,9},{9,13},... | collective-permute-start | bytes 393224 | tf_op jit(solution)/shard_map/ppermute | solution.py:227
  67.0 19.7 %collective-permute-start.9 = (bf16[64,1024]{1,0:T(8,128)(2,1)}, bf16[64,1024]{1,0:T(8,128)(2,1)S(1)}, u32[]{:S(2)}, u32[]{:S(2)}) collective-permute-start(bf16[64,1024]{1,0:T(8,128)(2,1)} %get-tuple-element.26), channel_id=1, source_target_pairs={{0,16},{1,20},{2,24},{3,28},{4,0},{5,4},{6,8},{7,12},{8,17},{9,21}... | collective-permute-start | bytes 393224 | tf_op jit(solution)/shard_map/ppermute | solution.py:227
  68.8 6.3 %copy-start.5 = (bf16[4,16,2048]{2,1,0:T(8,128)(2,1)}, bf16[4,16,2048]{2,1,0:T(8,128)(2,1)S(1)}, u32[]{:S(2)}) copy-start(bf16[4,16,2048]{2,1,0:T(8,128)(2,1)S(1)} %collective-permute-done.11.refs_1_) | copy-start | bytes 786436
  68.8 21.1 %collective-permute-start.10 = (bf16[64,1024]{1,0:T(8,128)(2,1)}, bf16[64,1024]{1,0:T(8,128)(2,1)S(1)}, u32[]{:S(2)}, u32[]{:S(2)}) collective-permute-start(bf16[64,1024]{1,0:T(8,128)(2,1)} %get-tuple-element.27), channel_id=1, source_target_pairs={{0,24},{1,28},{2,16},{3,20},{4,8},{5,12},{6,0},{7,4},{8,25},{9,29}... | collective-permute-start | bytes 393224 | tf_op jit(solution)/shard_map/ppermute | solution.py:227
  75.1 0.7 copy-start.7
  80.3 10.8 %collective-permute-start.14 = (bf16[64,1024]{1,0:T(8,128)(2,1)}, bf16[64,1024]{1,0:T(8,128)(2,1)S(1)}, u32[]{:S(2)}, u32[]{:S(2)}) collective-permute-start(bf16[64,1024]{1,0:T(8,128)(2,1)} %get-tuple-element.29), channel_id=1, source_target_pairs={{0,0},{1,4},{2,8},{3,12},{4,16},{5,20},{6,24},{7,28},{8,1},{9,5},{... | collective-permute-start | bytes 393224 | tf_op jit(solution)/shard_map/ppermute | solution.py:227
  82.3 17.0 %copy-start.10 = (bf16[64,1024]{1,0:T(8,128)(2,1)}, bf16[64,1024]{1,0:T(8,128)(2,1)S(1)}, u32[]{:S(2)}) copy-start(bf16[64,1024]{1,0:T(8,128)(2,1)S(1)} %collective-permute-done.7.refs_0_) | copy-start | bytes 393220
  82.3 8.8 %collective-permute-start.15 = (bf16[64,1024]{1,0:T(8,128)(2,1)}, bf16[64,1024]{1,0:T(8,128)(2,1)S(1)}, u32[]{:S(2)}, u32[]{:S(2)}) collective-permute-start(bf16[64,1024]{1,0:T(8,128)(2,1)} %get-tuple-element.30), channel_id=1, source_target_pairs={{0,8},{1,12},{2,0},{3,4},{4,24},{5,28},{6,16},{7,20},{8,9},{9,13},... | collective-permute-start | bytes 393224 | tf_op jit(solution)/shard_map/ppermute | solution.py:227
  83.6 15.7 %copy-start.11 = (bf16[64,1024]{1,0:T(8,128)(2,1)}, bf16[64,1024]{1,0:T(8,128)(2,1)S(1)}, u32[]{:S(2)}) copy-start(bf16[64,1024]{1,0:T(8,128)(2,1)S(1)} %collective-permute-done.8.refs_1_) | copy-start | bytes 393220
  83.6 8.9 %collective-permute-start.16 = (bf16[64,1024]{1,0:T(8,128)(2,1)}, bf16[64,1024]{1,0:T(8,128)(2,1)S(1)}, u32[]{:S(2)}, u32[]{:S(2)}) collective-permute-start(bf16[64,1024]{1,0:T(8,128)(2,1)} %get-tuple-element.31), channel_id=1, source_target_pairs={{0,16},{1,20},{2,24},{3,28},{4,0},{5,4},{6,8},{7,12},{8,17},{9,21}... | collective-permute-start | bytes 393224 | tf_op jit(solution)/shard_map/ppermute | solution.py:227
  86.7 12.6 %copy-start.12 = (bf16[64,1024]{1,0:T(8,128)(2,1)}, bf16[64,1024]{1,0:T(8,128)(2,1)S(1)}, u32[]{:S(2)}) copy-start(bf16[64,1024]{1,0:T(8,128)(2,1)S(1)} %collective-permute-done.9.refs_2_) | copy-start | bytes 393220
  86.7 12.6 %collective-permute-start.17 = (bf16[64,1024]{1,0:T(8,128)(2,1)}, bf16[64,1024]{1,0:T(8,128)(2,1)S(1)}, u32[]{:S(2)}, u32[]{:S(2)}) collective-permute-start(bf16[64,1024]{1,0:T(8,128)(2,1)} %get-tuple-element.32), channel_id=1, source_target_pairs={{0,24},{1,28},{2,16},{3,20},{4,8},{5,12},{6,0},{7,4},{8,25},{9,29}... | collective-permute-start | bytes 393224 | tf_op jit(solution)/shard_map/ppermute | solution.py:227
  89.9 9.4 %copy-start.13 = (bf16[64,1024]{1,0:T(8,128)(2,1)}, bf16[64,1024]{1,0:T(8,128)(2,1)S(1)}, u32[]{:S(2)}) copy-start(bf16[64,1024]{1,0:T(8,128)(2,1)S(1)} %collective-permute-done.10.refs_3_) | copy-start | bytes 393220
  91.1 8.2 %copy-start.14 = (bf16[64,1024]{1,0:T(8,128)(2,1)}, bf16[64,1024]{1,0:T(8,128)(2,1)S(1)}, u32[]{:S(2)}) copy-start(bf16[64,1024]{1,0:T(8,128)(2,1)S(1)} %collective-permute-done.14.refs_4_) | copy-start | bytes 393220
  91.1 8.2 %copy-start.15 = (bf16[64,1024]{1,0:T(8,128)(2,1)}, bf16[64,1024]{1,0:T(8,128)(2,1)S(1)}, u32[]{:S(2)}) copy-start(bf16[64,1024]{1,0:T(8,128)(2,1)S(1)} %collective-permute-done.15.refs_5_) | copy-start | bytes 393220
  92.4 6.9 %copy-start.16 = (bf16[64,1024]{1,0:T(8,128)(2,1)}, bf16[64,1024]{1,0:T(8,128)(2,1)S(1)}, u32[]{:S(2)}) copy-start(bf16[64,1024]{1,0:T(8,128)(2,1)S(1)} %collective-permute-done.16.refs_6_) | copy-start | bytes 393220
  99.3 0.7 copy-start.17

commit v3 on v0

--- a/solution.py
+++ b/solution.py
@@ -1,15 +1,282 @@
+import functools
 import math
 
 import jax
 import jax.numpy as jnp
 from jax import lax
+from jax.experimental import pallas as pl
+from jax.experimental.pallas import tpu as pltpu
 from jax.sharding import PartitionSpec as P
 
 HEAD_DIM = 128
 DOCS = 16
-
-
+META = 16
 NEG_FILL = -1e30
+VMEM_LIMIT = 24 * 1024 * 1024
+PACK_LIMIT = 56 * 1024 * 1024
+
+ANY = pl.BlockSpec(memory_space=pl.ANY)
+VMEM = pl.BlockSpec(memory_space=pltpu.VMEM)
+SMEM = pl.BlockSpec(memory_space=pltpu.SMEM)
+
+
+def pack_kernel(parts, heads, plan_ref, q_ref, k_ref, v_ref, ids_ref, all_out, q_out, kv_out):
+    rows = q_ref.shape[0]
+    piece = rows // parts
+    lane = lax.broadcasted_iota(jnp.int32, (1, rows), 1)
+    source = jnp.zeros((1, rows), jnp.int32)
+    for j in range(parts):
+        p = plan_ref[0, j]
+        for h in range(heads):
+            moved = q_ref[
+                pl.ds(pl.multiple_of(p * piece, piece), piece), h * HEAD_DIM : (h + 1) * HEAD_DIM
+            ]
+            q_out[h * rows + j * piece : h * rows + (j + 1) * piece, :] = moved
+            all_out[h * rows + j * piece : h * rows + (j + 1) * piece, :] = moved
+        source = jnp.where(
+            (lane >= j * piece) & (lane < (j + 1) * piece), (p - j) * piece + lane, source
+        )
+    ids = ids_ref[...].astype(jnp.float32)
+    row = lax.broadcasted_iota(jnp.int32, (META, rows), 0)
+    from_row = lax.broadcasted_iota(jnp.int32, (rows, rows), 0)
+    chosen = (from_row == source).astype(jnp.float32)
+    ids_rows = jnp.broadcast_to(ids, (META, rows))
+    ids_moved = jnp.dot(ids_rows, chosen, preferred_element_type=jnp.float32)
+    positions = jnp.broadcast_to(source.astype(jnp.float32), (META, rows))
+    meta = jnp.where(row == 0, ids_rows, jnp.where(row == 1, ids_moved, positions))
+    for out_ref, base in ((all_out, heads * rows), (kv_out, 0)):
+        out_ref[base : base + rows, :] = k_ref[...]
+        out_ref[base + rows : base + 2 * rows, :] = v_ref[...]
+        out_ref[base + 2 * rows :, :] = meta.astype(jnp.bfloat16)
+
+
+def attend_kernel(parts, heads, scale, wave, *refs):
+    half = parts // 2
+    near, far, refs = refs[:half], refs[half : 2 * half], refs[2 * half :]
+    q_blocks = near
+    if wave:
+        q_blocks, refs = refs[:half], refs[half:]
+    send_ref, keep_ref, q_held, kv_held, vals_ref, rows_ref, ends, sems = refs
+    rows = q_held.shape[1] // heads
+    piece = rows // parts
+    me = lax.axis_index("ctx")
+    other = 1 - lax.rem(lax.axis_index("head"), 2)
+    first_block = half * lax.rem(lax.div(me, half) + wave, 2)
+    q_rows = heads * rows
+    kv_copies = [
+        pltpu.make_async_copy(
+            near[k].at[q_rows:], kv_held.at[jnp.bitwise_xor(me, k)], sems.at[half + k]
+        )
+        for k in range(half)
+    ] + [
+        pltpu.make_async_copy(
+            far[k], kv_held.at[jnp.bitwise_xor(me, half + k)], sems.at[2 * half + k]
+        )
+        for k in range(half)
+    ]
+    copies = [
+        pltpu.make_async_copy(
+            q_blocks[k].at[:q_rows], q_held.at[jnp.bitwise_xor(lax.rem(me, half), k)], sems.at[k]
+        )
+        for k in range(half)
+    ]
+    for copy in kv_copies + copies:
+        copy.start()
+    for copy in kv_copies:
+        copy.wait()
+
+    def ids_of(block):
+        return kv_held[block, 2 * rows :, :].astype(jnp.float32)
+
+    for b in range(parts):
+        vals_ref[b, :, :HEAD_DIM] = kv_held[b, rows : 2 * rows, :]
+        vals_ref[b, :, HEAD_DIM:] = jnp.ones((rows, HEAD_DIM), jnp.bfloat16)
+        ids = ids_of(b)[0:1]
+        ends[0, b] = jnp.min(ids)
+        ends[1, b] = jnp.max(ids)
+
+    for copy in copies:
+        copy.wait()
+
+    def one_block(i, carry):
+        d = first_block + i
+        turned = ids_of(d).T
+        q_ids, q_pos = turned[:, 1:2], turned[:, 2:3]
+        start = jnp.int32(0)
+        for b in range(parts):
+            start = start + (ends[1, b] < ends[0, d]).astype(jnp.int32)
+        b0 = lax.div(start, 2) * 2
+        tiles = lax.div(d, 2) + 1 - lax.div(start, 2)
+        for w in range(1, half + 1):
+
+            @pl.when(tiles == w)
+            def _(w=w):
+                span = 2 * w * rows
+                k_ids = jnp.concatenate([ids_of(b0 + n)[0:1] for n in range(2 * w)], axis=1)
+                k_pos = lax.broadcasted_iota(jnp.int32, (1, span), 1) + (b0 - d) * rows
+                allowed = (k_ids == q_ids) & (k_pos.astype(jnp.float32) <= q_pos)
+                bias = jnp.where(allowed, 0.0, NEG_FILL)
+                keys = kv_held[pl.ds(b0, 2 * w), :rows, :].reshape(span, HEAD_DIM)
+                vals = vals_ref[pl.ds(b0, 2 * w), :, :].reshape(span, 2 * HEAD_DIM)
+                for h in range(heads):
+                    q = q_held[i, h * rows : (h + 1) * rows, :]
+                    s = lax.dot_general(
+                        q, keys, (((1,), (1,)), ((), ())), preferred_element_type=jnp.float32
+                    )
+                    s = s + bias
+                    top = jnp.max(s, axis=1, keepdims=True)
+                    e = jnp.exp2((s - top) * (scale * math.log2(math.e)))
+                    o = jnp.dot(e.astype(jnp.bfloat16), vals, preferred_element_type=jnp.float32)
+                    o = (o[:, :HEAD_DIM] / o[:, HEAD_DIM:]).astype(jnp.bfloat16)
+                    for j in range(parts):
+                        at = pl.multiple_of((j // 2) * half * piece + i * piece, piece)
+                        rows_ref[
+                            jnp.bitwise_xor(other, j % 2),
+                            pl.ds(at, piece),
+                            h * HEAD_DIM : (h + 1) * HEAD_DIM,
+                        ] = o[j * piece : (j + 1) * piece, :]
+
+        return carry
+
+    lax.fori_loop(0, half, one_block, 0)
+    out = [
+        pltpu.make_async_copy(rows_ref.at[0], send_ref, sems.at[0]),
+        pltpu.make_async_copy(rows_ref.at[1], keep_ref, sems.at[1]),
+    ]
+    for copy in out:
+        copy.start()
+    for copy in out:
+        copy.wait()
+
+
+def project_kernel(group, half, *refs):
+    (keep_0, got_0, keep_1, got_1, w_ref, w_pair_ref), refs = refs[:6], refs[6:]
+    out_refs, total = refs[:-1], refs[-1]
+    count = len(out_refs)
+    rows = keep_0.shape[0] // count
+    me = lax.axis_index("ctx")
+    upper = lax.div(me, count)
+    mine = lax.rem(me, group) * half + lax.div(lax.axis_index("head"), 2)
+    for wave, keep_ref, got_ref in ((0, keep_0, got_0), (1, keep_1, got_1)):
+        total[...] = jnp.dot(
+            keep_ref[...], w_ref[...], preferred_element_type=jnp.float32
+        ) + jnp.dot(got_ref[...], w_pair_ref[...], preferred_element_type=jnp.float32)
+        place = pl.ds(pl.multiple_of(lax.rem(upper + wave, 2) * rows, rows), rows)
+        for k, out_ref in enumerate(out_refs):
+            at = pl.ds(pl.multiple_of(jnp.bitwise_xor(mine, k) * rows, rows), rows)
+            out_ref[place, :] = total[at, :].astype(jnp.bfloat16)
+
+
+def final_kernel(group, half, *refs):
+    blocks, out_ref = refs[:-1], refs[-1]
+    cols = blocks[0].shape[1]
+    high = lax.div(lax.axis_index("ctx"), 2)
+    for first in range(0, len(blocks), half):
+        part = lax.div(jnp.bitwise_xor(high, first), half)
+        total = blocks[first][...].astype(jnp.float32)
+        for k in range(first + 1, first + half):
+            total = total + blocks[k][...].astype(jnp.float32)
+        out_ref[:, pl.ds(pl.multiple_of(part * cols, cols), cols)] = total.astype(jnp.bfloat16)
+
+
+def along_ctx(x, parts, k):
+    return lax.ppermute(x, "ctx", [(i, i ^ k) for i in range(parts)])
+
+
+def spread_over_ctx(block, q_block, kv_block, parts):
+    half = parts // 2
+    near, far_q, far_kv = {0: block}, {}, {}
+    far_q[0] = along_ctx(q_block, parts, half)
+    for k in [*range(2, half, 2), 1]:
+        near[k] = along_ctx(block, parts, k)
+    far_kv[0] = along_ctx(kv_block, parts, half)
+    far_kv[1] = along_ctx(kv_block, parts, half + 1)
+    near, far_q, far_kv = lax.optimization_barrier((near, far_q, far_kv))
+    for k in range(2, half, 2):
+        near[k + 1] = along_ctx(near[k], parts, 1)
+        far_q[k] = along_ctx(far_q[0], parts, k)
+        far_kv[k] = along_ctx(far_kv[0], parts, k)
+        far_kv[k + 1] = along_ctx(far_kv[1], parts, k)
+    far_q[1] = along_ctx(far_q[0], parts, 1)
+    near, far_q, far_kv = lax.optimization_barrier((near, far_q, far_kv))
+    for k in range(2, half, 2):
+        far_q[k + 1] = along_ctx(far_q[k], parts, 1)
+    return [[some[k] for k in range(half)] for some in (near, far_q, far_kv)]
+
+
+def packed_body(groups, queries, keys, values, doc_ids, plan, w_out):
+    parts = lax.axis_size("ctx")
+    rows = queries.shape[0]
+    heads = queries.shape[1] // HEAD_DIM
+    width = w_out.shape[1]
+    group, half = parts // groups, groups // 2
+    bf16 = jnp.bfloat16
+    params = pltpu.CompilerParams(vmem_limit_bytes=VMEM_LIMIT)
+    pair = [(g, g ^ 1) for g in range(groups)]
+    kv_rows = 2 * rows + META
+    w_pair = lax.ppermute(w_out, "head", pair)
+    block, q_block, kv_block = pl.pallas_call(
+        functools.partial(pack_kernel, parts, heads),
+        out_shape=[
+            jax.ShapeDtypeStruct((heads * rows + kv_rows, HEAD_DIM), bf16),
+            jax.ShapeDtypeStruct((heads * rows, HEAD_DIM), bf16),
+            jax.ShapeDtypeStruct((kv_rows, HEAD_DIM), bf16),
+        ],
+        in_specs=[SMEM, VMEM, VMEM, VMEM, VMEM],
+        out_specs=[VMEM] * 3,
+        compiler_params=pltpu.CompilerParams(vmem_limit_bytes=PACK_LIMIT),
+        name="pack",
+    )(plan, queries, keys, values, doc_ids.reshape(1, rows))
+    near, far_q, far_kv = spread_over_ctx(block, q_block, kv_block, parts)
+    wave_rows = parts * rows // 4
+    count = parts // 2
+    arrived, halves = [], []
+    for wave in range(2):
+        inputs = [*near, *far_kv]
+        if wave:
+            inputs = inputs + far_q
+        send, keep = pl.pallas_call(
+            functools.partial(attend_kernel, parts, heads, 1.0 / math.sqrt(HEAD_DIM), wave),
+            out_shape=[jax.ShapeDtypeStruct((wave_rows, heads * HEAD_DIM), bf16)] * 2,
+            in_specs=[ANY] * len(inputs),
+            out_specs=[ANY, ANY],
+            scratch_shapes=[
+                pltpu.VMEM((count, heads * rows, HEAD_DIM), bf16),
+                pltpu.VMEM((parts, kv_rows, HEAD_DIM), bf16),
+                pltpu.VMEM((parts, rows, 2 * HEAD_DIM), bf16),
+                pltpu.VMEM((2, wave_rows, heads * HEAD_DIM), bf16),
+                pltpu.SMEM((2, parts), jnp.float32),
+                pltpu.SemaphoreType.DMA((count + parts,)),
+            ],
+            compiler_params=params,
+            cost_estimate=pl.CostEstimate(flops=8 * 10**9, bytes_accessed=2**22, transcendentals=0),
+            name="attend",
+        )(*inputs)
+        halves += [keep, lax.ppermute(send, "head", pair)]
+    sums = pl.pallas_call(
+        functools.partial(project_kernel, group, half),
+        out_shape=[jax.ShapeDtypeStruct((rows, width), bf16)] * count,
+        in_specs=[VMEM] * 6,
+        out_specs=[VMEM] * count,
+        scratch_shapes=[pltpu.VMEM((wave_rows, width), jnp.float32)],
+        compiler_params=params,
+        name="project",
+    )(*halves, w_out, w_pair)
+    for k in range(count):
+        pairs = []
+        for c in range(parts):
+            for g in range(groups):
+                high = ((c % group) * half + g // 2) ^ k
+                pairs.append((c * groups + g, (high * 2 + g % 2) * groups + c // group))
+        arrived.append(lax.ppermute(sums[k], ("ctx", "head"), pairs))
+    return pl.pallas_call(
+        functools.partial(final_kernel, group, half),
+        out_shape=jax.ShapeDtypeStruct((rows, group * width), bf16),
+        in_specs=[VMEM] * count,
+        out_specs=VMEM,
+        compiler_params=params,
+        name="final_sum",
+    )(*arrived)
 
 
 def spread_rows(block, order, parts):
@@ -139,9 +406,24 @@
     return summed
 
 
+def fits(parts, groups, rows, width):
+    powers = all(n & (n - 1) == 0 for n in (parts, groups))
+    window = parts * rows * width * 2
+    whole = rows % (16 * parts) == 0 and groups % 2 == 0 and parts % groups == 0
+    return powers and whole and 8 * window <= VMEM_LIMIT
+
+
 def solution(mesh):
+    parts, groups = mesh.shape["ctx"], mesh.shape["head"]
+
+    def one_device(queries, keys, values, doc_ids, plan, w_out):
+        one_pair = keys.shape[1] == HEAD_DIM
+        if one_pair and fits(parts, groups, queries.shape[0], queries.shape[1]):
+            return packed_body(groups, queries, keys, values, doc_ids, plan, w_out)
+        return body(queries, keys, values, doc_ids, plan, w_out)
+
     return jax.shard_map(
-        body,
+        one_device,
         mesh=mesh,
         in_specs=(
             P("ctx", "head"),

time: 284 us -> 89.1 us (0.31)
  blocking collectives: 123 us -> 0 us
  waiting for transfers between devices: 98.6 us -> 41 us
  starting transfers between devices: 0.04 us -> 28.9 us
  Pallas kernels: 0 us -> 18 us
  other arithmetic: 14.1 us -> 0 us
  between operations: 13.5 us -> 0.08 us
  loops' own time: 12.6 us -> 0 us
  local copies, waits for them, and re-layouts: 11.9 us -> 0.98 us
  matrix products: 7.67 us -> 0 us
    all_gather x1 -> x0, waiting for transfers between devices: 65.8 us -> none  [body(): lax.all_gather(attended, 'ctx', axis=0, tiled=True)]
    all_gather x3 -> x0, blocking collectives: 64.1 us -> none  [the longest x1 26.7 us: body(): lax.all_gather(values, 'ctx', axis=0, tiled=True)]
    all_to_all x2 -> x0, blocking collectives: 58.5 us -> none  [the longest x1 50 us: body(): lax.all_to_all(stacked.astype(jnp.bfloat16), 'ctx', split_axis=0, concat_...]
    ppermute x0 -> x18, waiting for transfers between devices: none -> 41 us  [the longest x4 21 us: packed_body(): arrived.append(lax.ppermute(sums[k], ('ctx', 'head'), pairs))]
    reduce_scatter x1 -> x0, waiting for transfers between devices: 32.8 us -> none  [body(): lax.psum_scatter(partial_sum.astype(jnp.bfloat16), 'head', scatter_dimens...]
    ppermute x0 -> x18, starting transfers between devices: none -> 28.9 us  [the longest x11 11.7 us: along_ctx(): return lax.ppermute(x, 'ctx', [(i, i ^ k) for i in range(parts)])]
    pallas_call x0 -> x5, Pallas kernels: none -> 18 us  [the longest x2 12.8 us: packed_body(): pl.pallas_call(functools.partial(attend_kernel, parts, heads, 1.0 / math....]
    another operation x7 -> x0, loops' own time: 12.6 us -> none  [the longest x1 9.7 us: attend(): lax.fori_loop(0, n_qblocks, one_query_block, initial)]
  transfers between devices with their start and end apart: 2 -> 18, of which waited for: 2 -> 9; matrix products, arithmetic and copies ran while one was open for 0% -> 0% of each run, Pallas kernels for 0% -> 14%
where the time goes in v3:
time: 89.1 us; the launch traced here: 88.9 us
  waiting for transfers between devices  41 us (46%)
  starting transfers between devices  28.9 us (32%)
  Pallas kernels  18 us (20%)
  local copies, waits for them, and re-layouts  0.98 us (1%)
    ppermute x4, waiting for transfers between devices, packed_body(): arrived.append(lax.ppermute(sums[k], ('ctx', 'head'), pairs))  21 us
    ppermute x11, waiting for transfers between devices, along_ctx(): return lax.ppermute(x, 'ctx', [(i, i ^ k) for i in range(parts)])  18.1 us
    pallas_call x2, Pallas kernels, packed_body(): pl.pallas_call(functools.partial(attend_kernel, parts, heads, 1.0 / math....  12.8 us
    ppermute x11, starting transfers between devices, along_ctx(): return lax.ppermute(x, 'ctx', [(i, i ^ k) for i in range(parts)])  11.7 us
    ppermute x4, starting transfers between devices, packed_body(): arrived.append(lax.ppermute(sums[k], ('ctx', 'head'), pairs))  9.82 us
    ppermute x2, starting transfers between devices, packed_body(): halves += [keep, lax.ppermute(send, 'head', pair)]  4.37 us
    ppermute x1, starting transfers between devices, packed_body(): w_pair = lax.ppermute(w_out, 'head', pair)  2.96 us
    pallas_call x1, Pallas kernels, packed_body(): pl.pallas_call(functools.partial(project_kernel, group, half), out_shape=...  2.39 us
  transfers between devices with their start and end apart: 18, of which 9 were waited for; matrix products, arithmetic and copies ran while one was open for 0% of the time, Pallas kernels for 14%

profile of v3, /device:TPU:17, one launch (start us, length us, event | category | flops | bytes accessed | tf_op | source)
XLA Modules:
  0.0 88.9 jit_solution(326764427829432290)
XLA Ops:
  0.0 1.9 %pack.1 = (bf16[1296,128]{1,0:T(8,128)(2,1)}, bf16[1024,128]{1,0:T(8,128)(2,1)}, bf16[272,128]{1,0:T(8,128)(2,1)}) custom-call(s32[1,8]{1,0:T(1,128)} %plan_ref.1, bf16[128,1024]{1,0:T(8,128)(2,1)} %q_ref.1, bf16[128,128]{1,0:T(8,128)(2,1)} %k_ref.1, bf16[128,128]{1,0:T(8,128)(2,1)} %v_ref.1, s32[1,128]{1,0:T(1,128)} %bitcast.1), custom_call_target="tpu_custom_call" | custom-call | tf_op jit(solution)/shard_map/pack/pallas_call | solution.py:218
  1.9 1.3 %collective-permute-start.1 = (bf16[1296,128]{1,0:T(8,128)(2,1)}, bf16[1296,128]{1,0:T(8,128)(2,1)S(1)}, u32[]{:S(2)}, u32[]{:S(2)}) collective-permute-start(bf16[1296,128]{1,0:T(8,128)(2,1)} %get-tuple-element.42.refs_0_), channel_id=1, source_target_pairs={{0,8},{4,12},{8,0},{12,4},{16,24},{20,28},{24,16},{28,20},{1,9},{5... | collective-permute-start | bytes 995336 | tf_op jit(solution)/shard_map/ppermute | solution.py:183
  3.2 1.2 %collective-permute-start = (bf16[1296,128]{1,0:T(8,128)(2,1)}, bf16[1296,128]{1,0:T(8,128)(2,1)S(1)}, u32[]{:S(2)}, u32[]{:S(2)}) collective-permute-start(bf16[1296,128]{1,0:T(8,128)(2,1)} %get-tuple-element.42.refs_0_), channel_id=1, source_target_pairs={{0,4},{4,0},{8,12},{12,8},{16,20},{20,16},{24,28},{28,24},{1,5},{5... | collective-permute-start | bytes 995336 | tf_op jit(solution)/shard_map/ppermute | solution.py:183
  4.5 0.1 collective-permute-start.2
  4.5 2.3 %collective-permute-start.4 = (bf16[272,128]{1,0:T(8,128)(2,1)}, bf16[272,128]{1,0:T(8,128)(2,1)S(1)}, u32[]{:S(2)}, u32[]{:S(2)}) collective-permute-start(bf16[272,128]{1,0:T(8,128)(2,1)} %get-tuple-element.35), channel_id=1, source_target_pairs={{0,20},{4,16},{8,28},{12,24},{16,4},{20,0},{24,12},{28,8},{1,21},{... | collective-permute-start | bytes 208904 | tf_op jit(solution)/shard_map/ppermute | solution.py:183
  6.8 0.1 collective-permute-start.3
  6.8 11.7 %collective-permute-done.4.refs_5_ = bf16[272,128]{1,0:T(8,128)(2,1)S(1)} collective-permute-done((bf16[272,128]{1,0:T(8,128)(2,1)}, bf16[272,128]{1,0:T(8,128)(2,1)S(1)}, u32[]{:S(2)}, u32[]{:S(2)}) %collective-permute-start.4) | collective-permute-done | bytes 69664 | tf_op jit(solution)/shard_map/ppermute | solution.py:183
  18.6 2.3 %collective-permute-done.3.refs_4_ = bf16[272,128]{1,0:T(8,128)(2,1)S(1)} collective-permute-done((bf16[272,128]{1,0:T(8,128)(2,1)}, bf16[272,128]{1,0:T(8,128)(2,1)S(1)}, u32[]{:S(2)}, u32[]{:S(2)}) %collective-permute-start.3) | collective-permute-done | bytes 69664 | tf_op jit(solution)/shard_map/ppermute | solution.py:183
  20.9 0.0 collective-permute-done.2.refs_8_
  20.9 0.0 collective-permute-done.1.refs_2_
  20.9 0.0 collective-permute-done.refs_1_
  20.9 0.1 collective-permute-start.5
  21.0 3.3 %collective-permute-start.7 = (bf16[1024,128]{1,0:T(8,128)(2,1)S(1)}, bf16[1024,128]{1,0:T(8,128)(2,1)S(1)}, u32[]{:S(2)}, u32[]{:S(2)}) collective-permute-start(bf16[1024,128]{1,0:T(8,128)(2,1)S(1)} %collective-permute-done.2.refs_8_), channel_id=1, source_target_pairs={{0,8},{4,12},{8,0},{12,4},{16,24},{20,28},{24,16},{28,20},{1,9},{5... | collective-permute-start | bytes 786440 | tf_op jit(solution)/shard_map/ppermute | solution.py:183
  24.3 1.2 %collective-permute-start.6 = (bf16[1024,128]{1,0:T(8,128)(2,1)S(1)}, bf16[1024,128]{1,0:T(8,128)(2,1)S(1)}, u32[]{:S(2)}, u32[]{:S(2)}) collective-permute-start(bf16[1024,128]{1,0:T(8,128)(2,1)S(1)} %collective-permute-done.2.refs_8_), channel_id=1, source_target_pairs={{0,4},{4,0},{8,12},{12,8},{16,20},{20,16},{24,28},{28,24},{1,5},{5... | collective-permute-start | bytes 786440 | tf_op jit(solution)/shard_map/ppermute | solution.py:183
  25.5 0.0 collective-permute-start.8
  25.5 3.0 %collective-permute-start.13 = (bf16[1024,1024]{1,0:T(8,128)(2,1)}, bf16[1024,1024]{1,0:T(8,128)(2,1)S(1)}, u32[]{:S(2)}, u32[]{:S(2)}) collective-permute-start(bf16[1024,1024]{1,0:T(8,128)(2,1)} %refs_4_.1), channel_id=1, source_target_pairs={{0,1},{1,0},{2,3},{3,2},{4,5},{5,4},{6,7},{7,6},{8,9},{9,8},{10,11... | collective-permute-start | bytes 6291464 | tf_op jit(solution)/shard_map/ppermute | solution.py:217
  28.5 1.3 %collective-permute-done.8.refs_6_ = bf16[272,128]{1,0:T(8,128)(2,1)S(1)} collective-permute-done((bf16[272,128]{1,0:T(8,128)(2,1)S(1)}, bf16[272,128]{1,0:T(8,128)(2,1)S(1)}, u32[]{:S(2)}, u32[]{:S(2)}) %collective-permute-start.8) | collective-permute-done | bytes 69664 | tf_op jit(solution)/shard_map/ppermute | solution.py:183
  29.8 1.2 %collective-permute-start.9 = (bf16[272,128]{1,0:T(8,128)(2,1)S(1)}, bf16[272,128]{1,0:T(8,128)(2,1)S(1)}, u32[]{:S(2)}, u32[]{:S(2)}) collective-permute-start(bf16[272,128]{1,0:T(8,128)(2,1)S(1)} %collective-permute-done.4.refs_5_), channel_id=1, source_target_pairs={{0,8},{4,12},{8,0},{12,4},{16,24},{20,28},{24,16},{28,20},{1,9},{5... | collective-permute-start | bytes 208904 | tf_op jit(solution)/shard_map/ppermute | solution.py:183
  31.0 2.4 %collective-permute-done.9.refs_7_ = bf16[272,128]{1,0:T(8,128)(2,1)S(1)} collective-permute-done((bf16[272,128]{1,0:T(8,128)(2,1)S(1)}, bf16[272,128]{1,0:T(8,128)(2,1)S(1)}, u32[]{:S(2)}, u32[]{:S(2)}) %collective-permute-start.9) | collective-permute-done | bytes 69664 | tf_op jit(solution)/shard_map/ppermute | solution.py:183
  33.4 0.0 collective-permute-done.7.refs_10_
  33.4 0.4 collective-permute-done.6.refs_9_
  33.7 0.0 collective-permute-done.5.refs_3_
  33.8 1.0 %collective-permute-start.11 = (bf16[1024,128]{1,0:T(8,128)(2,1)S(1)}, bf16[1024,128]{1,0:T(8,128)(2,1)S(1)}, u32[]{:S(2)}, u32[]{:S(2)}) collective-permute-start(bf16[1024,128]{1,0:T(8,128)(2,1)S(1)} %collective-permute-done.7.refs_10_), channel_id=1, source_target_pairs={{0,4},{4,0},{8,12},{12,8},{16,20},{20,16},{24,28},{28,24},{1,5},{5... | collective-permute-start | bytes 786440 | tf_op jit(solution)/shard_map/ppermute | solution.py:183
  34.8 0.0 copy-start.1
  34.8 1.0 %copy-done.1 = bf16[1296,128]{1,0:T(8,128)(2,1)S(1)} copy-done((bf16[1296,128]{1,0:T(8,128)(2,1)S(1)}, bf16[1296,128]{1,0:T(8,128)(2,1)}, u32[]{:S(2)}) %copy-start.1) | copy-done | bytes 331800
  35.7 7.9 %attend.2 = (bf16[256,1024]{1,0:T(8,128)(2,1)S(1)}, bf16[256,1024]{1,0:T(8,128)(2,1)S(1)}) custom-call(bf16[1296,128]{1,0:T(8,128)(2,1)S(1)} %copy-done.1, bf16[1296,128]{1,0:T(8,128)(2,1)S(1)} %collective-permute-done.refs_1_, bf16[1296,128]{1,0:T(8,128)(2,1)S(1)} %collective-permute-done.1.refs_2_, bf16[1296,128]{1,0:T(8,128)(2,1)S(1)} %collective-permute-done.5.refs_3_, ...), custom_call_target="tpu_custom_call" | custom-call | flops 8000000000 | bytes 4194304 | tf_op jit(solution)/shard_map/attend/pallas_call | solution.py:238
  43.7 0.0 copy-start
  43.7 4.2 %collective-permute-start.10 = (bf16[256,1024]{1,0:T(8,128)(2,1)S(1)}, bf16[256,1024]{1,0:T(8,128)(2,1)S(1)}, u32[]{:S(2)}, u32[]{:S(2)}) collective-permute-start(bf16[256,1024]{1,0:T(8,128)(2,1)S(1)} %get-tuple-element.51), channel_id=1, source_target_pairs={{0,1},{1,0},{2,3},{3,2},{4,5},{5,4},{6,7},{7,6},{8,9},{9,8},{10,11... | collective-permute-start | bytes 1572872 | tf_op jit(solution)/shard_map/ppermute | solution.py:255
  47.9 0.0 collective-permute-done.11.refs_11_
  47.9 4.8 %attend.3 = (bf16[256,1024]{1,0:T(8,128)(2,1)S(1)}, bf16[256,1024]{1,0:T(8,128)(2,1)S(1)}) custom-call(bf16[1296,128]{1,0:T(8,128)(2,1)S(1)} %copy-done.1, bf16[1296,128]{1,0:T(8,128)(2,1)S(1)} %collective-permute-done.refs_1_, bf16[1296,128]{1,0:T(8,128)(2,1)S(1)} %collective-permute-done.1.refs_2_, bf16[1296,128]{1,0:T(8,128)(2,1)S(1)} %collective-permute-done.5.refs_3_, ...), custom_call_target="tpu_custom_call" | custom-call | flops 8000000000 | bytes 4194304 | tf_op jit(solution)/shard_map/attend/pallas_call | solution.py:238
  52.8 0.1 collective-permute-start.12
  52.9 0.0 collective-permute-done.10.refs_1_
  52.9 1.8 %collective-permute-done.12.refs_3_ = bf16[256,1024]{1,0:T(8,128)(2,1)S(1)} collective-permute-done((bf16[256,1024]{1,0:T(8,128)(2,1)S(1)}, bf16[256,1024]{1,0:T(8,128)(2,1)S(1)}, u32[]{:S(2)}, u32[]{:S(2)}) %collective-permute-start.12) | collective-permute-done | bytes 524320 | tf_op jit(solution)/shard_map/ppermute | solution.py:255
  54.8 0.0 collective-permute-done.13.refs_5_
  54.8 0.0 copy-done
  54.8 2.4 %project.1 = (bf16[128,1024]{1,0:T(8,128)(2,1)S(1)}, bf16[128,1024]{1,0:T(8,128)(2,1)S(1)}, bf16[128,1024]{1,0:T(8,128)(2,1)S(1)}, bf16[128,1024]{1,0:T(8,128)(2,1)S(1)}) custom-call(bf16[256,1024]{1,0:T(8,128)(2,1)S(1)} %get-tuple-element.50.refs_0_, bf16[256,1024]{1,0:T(8,128)(2,1)S(1)} %collective-permute-done.10.refs_1_, ...), custom_call_target="tpu_custom_call" | custom-call | tf_op jit(solution)/shard_map/project/pallas_call | solution.py:256
  57.2 5.2 %collective-permute-start.14 = (bf16[128,1024]{1,0:T(8,128)(2,1)S(1)}, bf16[128,1024]{1,0:T(8,128)(2,1)S(1)}, u32[]{:S(2)}, u32[]{:S(2)}) collective-permute-start(bf16[128,1024]{1,0:T(8,128)(2,1)S(1)} %get-tuple-element.57), channel_id=1, source_target_pairs={{0,0},{1,4},{2,8},{3,12},{4,16},{5,20},{6,24},{7,28},{8,1},{9,5},{... | collective-permute-start | bytes 786440 | tf_op jit(solution)/shard_map/ppermute | solution.py:271
  62.3 1.7 %collective-permute-start.15 = (bf16[128,1024]{1,0:T(8,128)(2,1)S(1)}, bf16[128,1024]{1,0:T(8,128)(2,1)S(1)}, u32[]{:S(2)}, u32[]{:S(2)}) collective-permute-start(bf16[128,1024]{1,0:T(8,128)(2,1)S(1)} %get-tuple-element.58), channel_id=1, source_target_pairs={{0,8},{1,12},{2,0},{3,4},{4,24},{5,28},{6,16},{7,20},{8,9},{9,13},... | collective-permute-start | bytes 786440 | tf_op jit(solution)/shard_map/ppermute | solution.py:271
  64.0 0.0 collective-permute-start.16
  64.0 3.0 %collective-permute-start.17 = (bf16[128,1024]{1,0:T(8,128)(2,1)S(1)}, bf16[128,1024]{1,0:T(8,128)(2,1)S(1)}, u32[]{:S(2)}, u32[]{:S(2)}) collective-permute-start(bf16[128,1024]{1,0:T(8,128)(2,1)S(1)} %get-tuple-element.60), channel_id=1, source_target_pairs={{0,24},{1,28},{2,16},{3,20},{4,8},{5,12},{6,0},{7,4},{8,25},{9,29}... | collective-permute-start | bytes 786440 | tf_op jit(solution)/shard_map/ppermute | solution.py:271
  67.0 12.7 %collective-permute-done.14.refs_0_ = bf16[128,1024]{1,0:T(8,128)(2,1)S(1)} collective-permute-done((bf16[128,1024]{1,0:T(8,128)(2,1)S(1)}, bf16[128,1024]{1,0:T(8,128)(2,1)S(1)}, u32[]{:S(2)}, u32[]{:S(2)}) %collective-permute-start.14) | collective-permute-done | bytes 262176 | tf_op jit(solution)/shard_map/ppermute | solution.py:271
  79.7 7.3 %collective-permute-done.15.refs_1_ = bf16[128,1024]{1,0:T(8,128)(2,1)S(1)} collective-permute-done((bf16[128,1024]{1,0:T(8,128)(2,1)S(1)}, bf16[128,1024]{1,0:T(8,128)(2,1)S(1)}, u32[]{:S(2)}, u32[]{:S(2)}) %collective-permute-start.15) | collective-permute-done | bytes 262176 | tf_op jit(solution)/shard_map/ppermute | solution.py:271
  87.0 0.0 collective-permute-done.16.refs_2_
  87.0 1.0 %collective-permute-done.17.refs_3_ = bf16[128,1024]{1,0:T(8,128)(2,1)S(1)} collective-permute-done((bf16[128,1024]{1,0:T(8,128)(2,1)S(1)}, bf16[128,1024]{1,0:T(8,128)(2,1)S(1)}, u32[]{:S(2)}, u32[]{:S(2)}) %collective-permute-start.17) | collective-permute-done | bytes 262176 | tf_op jit(solution)/shard_map/ppermute | solution.py:271
  88.0 0.9 %final_sum.1 = bf16[128,2048]{1,0:T(8,128)(2,1)} custom-call(bf16[128,1024]{1,0:T(8,128)(2,1)S(1)} %collective-permute-done.14.refs_0_, bf16[128,1024]{1,0:T(8,128)(2,1)S(1)} %collective-permute-done.15.refs_1_, bf16[128,1024]{1,0:T(8,128)(2,1)S(1)} %collective-permute-done.16.refs_2_, bf16[128,1024]{1,0:T(8,128)(2,1)S(1)} %collective-permute-done.17.refs_3_), custom_call_target="tpu_custom_call" | custom-call | tf_op jit(solution)/shard_map/final_sum/pallas_call | solution.py:272
Async XLA Ops:
  1.9 19.0 %collective-permute-start.1 = (bf16[1296,128]{1,0:T(8,128)(2,1)}, bf16[1296,128]{1,0:T(8,128)(2,1)S(1)}, u32[]{:S(2)}, u32[]{:S(2)}) collective-permute-start(bf16[1296,128]{1,0:T(8,128)(2,1)} %get-tuple-element.42.refs_0_), channel_id=1, source_target_pairs={{0,8},{4,12},{8,0},{12,4},{16,24},{20,28},{24,16},{28,20},{1,9},{5... | collective-permute-start | bytes 995336 | tf_op jit(solution)/shard_map/ppermute | solution.py:183
  3.2 17.7 %collective-permute-start = (bf16[1296,128]{1,0:T(8,128)(2,1)}, bf16[1296,128]{1,0:T(8,128)(2,1)S(1)}, u32[]{:S(2)}, u32[]{:S(2)}) collective-permute-start(bf16[1296,128]{1,0:T(8,128)(2,1)} %get-tuple-element.42.refs_0_), channel_id=1, source_target_pairs={{0,4},{4,0},{8,12},{12,8},{16,20},{20,16},{24,28},{28,24},{1,5},{5... | collective-permute-start | bytes 995336 | tf_op jit(solution)/shard_map/ppermute | solution.py:183
  4.5 16.4 %collective-permute-start.2 = (bf16[1024,128]{1,0:T(8,128)(2,1)}, bf16[1024,128]{1,0:T(8,128)(2,1)S(1)}, u32[]{:S(2)}, u32[]{:S(2)}) collective-permute-start(bf16[1024,128]{1,0:T(8,128)(2,1)} %get-tuple-element.34), channel_id=1, source_target_pairs={{0,16},{4,20},{8,24},{12,28},{16,0},{20,4},{24,8},{28,12},{1,17},{... | collective-permute-start | bytes 786440 | tf_op jit(solution)/shard_map/ppermute | solution.py:183
  4.5 14.0 %collective-permute-start.4 = (bf16[272,128]{1,0:T(8,128)(2,1)}, bf16[272,128]{1,0:T(8,128)(2,1)S(1)}, u32[]{:S(2)}, u32[]{:S(2)}) collective-permute-start(bf16[272,128]{1,0:T(8,128)(2,1)} %get-tuple-element.35), channel_id=1, source_target_pairs={{0,20},{4,16},{8,28},{12,24},{16,4},{20,0},{24,12},{28,8},{1,21},{... | collective-permute-start | bytes 208904 | tf_op jit(solution)/shard_map/ppermute | solution.py:183
  6.8 14.1 %collective-permute-start.3 = (bf16[272,128]{1,0:T(8,128)(2,1)}, bf16[272,128]{1,0:T(8,128)(2,1)S(1)}, u32[]{:S(2)}, u32[]{:S(2)}) collective-permute-start(bf16[272,128]{1,0:T(8,128)(2,1)} %get-tuple-element.35), channel_id=1, source_target_pairs={{0,16},{4,20},{8,24},{12,28},{16,0},{20,4},{24,8},{28,12},{1,17},{... | collective-permute-start | bytes 208904 | tf_op jit(solution)/shard_map/ppermute | solution.py:183
  20.9 12.9 %collective-permute-start.5 = (bf16[1296,128]{1,0:T(8,128)(2,1)S(1)}, bf16[1296,128]{1,0:T(8,128)(2,1)S(1)}, u32[]{:S(2)}, u32[]{:S(2)}) collective-permute-start(bf16[1296,128]{1,0:T(8,128)(2,1)S(1)} %collective-permute-done.1.refs_2_), channel_id=1, source_target_pairs={{0,4},{4,0},{8,12},{12,8},{16,20},{20,16},{24,28},{28,24},{1,5},{5... | collective-permute-start | bytes 995336 | tf_op jit(solution)/shard_map/ppermute | solution.py:183
  21.0 12.4 %collective-permute-start.7 = (bf16[1024,128]{1,0:T(8,128)(2,1)S(1)}, bf16[1024,128]{1,0:T(8,128)(2,1)S(1)}, u32[]{:S(2)}, u32[]{:S(2)}) collective-permute-start(bf16[1024,128]{1,0:T(8,128)(2,1)S(1)} %collective-permute-done.2.refs_8_), channel_id=1, source_target_pairs={{0,8},{4,12},{8,0},{12,4},{16,24},{20,28},{24,16},{28,20},{1,9},{5... | collective-permute-start | bytes 786440 | tf_op jit(solution)/shard_map/ppermute | solution.py:183
  24.3 9.5 %collective-permute-start.6 = (bf16[1024,128]{1,0:T(8,128)(2,1)S(1)}, bf16[1024,128]{1,0:T(8,128)(2,1)S(1)}, u32[]{:S(2)}, u32[]{:S(2)}) collective-permute-start(bf16[1024,128]{1,0:T(8,128)(2,1)S(1)} %collective-permute-done.2.refs_8_), channel_id=1, source_target_pairs={{0,4},{4,0},{8,12},{12,8},{16,20},{20,16},{24,28},{28,24},{1,5},{5... | collective-permute-start | bytes 786440 | tf_op jit(solution)/shard_map/ppermute | solution.py:183
  25.5 4.3 %collective-permute-start.8 = (bf16[272,128]{1,0:T(8,128)(2,1)S(1)}, bf16[272,128]{1,0:T(8,128)(2,1)S(1)}, u32[]{:S(2)}, u32[]{:S(2)}) collective-permute-start(bf16[272,128]{1,0:T(8,128)(2,1)S(1)} %collective-permute-done.3.refs_4_), channel_id=1, source_target_pairs={{0,8},{4,12},{8,0},{12,4},{16,24},{20,28},{24,16},{28,20},{1,9},{5... | collective-permute-start | bytes 208904 | tf_op jit(solution)/shard_map/ppermute | solution.py:183
  25.5 29.2 %collective-permute-start.13 = (bf16[1024,1024]{1,0:T(8,128)(2,1)}, bf16[1024,1024]{1,0:T(8,128)(2,1)S(1)}, u32[]{:S(2)}, u32[]{:S(2)}) collective-permute-start(bf16[1024,1024]{1,0:T(8,128)(2,1)} %refs_4_.1), channel_id=1, source_target_pairs={{0,1},{1,0},{2,3},{3,2},{4,5},{5,4},{6,7},{7,6},{8,9},{9,8},{10,11... | collective-permute-start | bytes 6291464 | tf_op jit(solution)/shard_map/ppermute | solution.py:217
  29.8 3.6 %collective-permute-start.9 = (bf16[272,128]{1,0:T(8,128)(2,1)S(1)}, bf16[272,128]{1,0:T(8,128)(2,1)S(1)}, u32[]{:S(2)}, u32[]{:S(2)}) collective-permute-start(bf16[272,128]{1,0:T(8,128)(2,1)S(1)} %collective-permute-done.4.refs_5_), channel_id=1, source_target_pairs={{0,8},{4,12},{8,0},{12,4},{16,24},{20,28},{24,16},{28,20},{1,9},{5... | collective-permute-start | bytes 208904 | tf_op jit(solution)/shard_map/ppermute | solution.py:183
  33.8 14.2 %collective-permute-start.11 = (bf16[1024,128]{1,0:T(8,128)(2,1)S(1)}, bf16[1024,128]{1,0:T(8,128)(2,1)S(1)}, u32[]{:S(2)}, u32[]{:S(2)}) collective-permute-start(bf16[1024,128]{1,0:T(8,128)(2,1)S(1)} %collective-permute-done.7.refs_10_), channel_id=1, source_target_pairs={{0,4},{4,0},{8,12},{12,8},{16,20},{20,16},{24,28},{28,24},{1,5},{5... | collective-permute-start | bytes 786440 | tf_op jit(solution)/shard_map/ppermute | solution.py:183
  34.8 1.0 %copy-start.1 = (bf16[1296,128]{1,0:T(8,128)(2,1)S(1)}, bf16[1296,128]{1,0:T(8,128)(2,1)}, u32[]{:S(2)}) copy-start(bf16[1296,128]{1,0:T(8,128)(2,1)} %get-tuple-element.42.refs_0_) | copy-start | bytes 995332
  43.7 11.1 %copy-start = (bf16[1024,1024]{1,0:T(8,128)(2,1)S(1)}, bf16[1024,1024]{1,0:T(8,128)(2,1)}, u32[]{:S(2)}) copy-start(bf16[1024,1024]{1,0:T(8,128)(2,1)} %refs_4_.1) | copy-start | bytes 6291460
  43.7 9.2 %collective-permute-start.10 = (bf16[256,1024]{1,0:T(8,128)(2,1)S(1)}, bf16[256,1024]{1,0:T(8,128)(2,1)S(1)}, u32[]{:S(2)}, u32[]{:S(2)}) collective-permute-start(bf16[256,1024]{1,0:T(8,128)(2,1)S(1)} %get-tuple-element.51), channel_id=1, source_target_pairs={{0,1},{1,0},{2,3},{3,2},{4,5},{5,4},{6,7},{7,6},{8,9},{9,8},{10,11... | collective-permute-start | bytes 1572872 | tf_op jit(solution)/shard_map/ppermute | solution.py:255
  52.8 2.0 %collective-permute-start.12 = (bf16[256,1024]{1,0:T(8,128)(2,1)S(1)}, bf16[256,1024]{1,0:T(8,128)(2,1)S(1)}, u32[]{:S(2)}, u32[]{:S(2)}) collective-permute-start(bf16[256,1024]{1,0:T(8,128)(2,1)S(1)} %get-tuple-element.56), channel_id=1, source_target_pairs={{0,1},{1,0},{2,3},{3,2},{4,5},{5,4},{6,7},{7,6},{8,9},{9,8},{10,11... | collective-permute-start | bytes 1572872 | tf_op jit(solution)/shard_map/ppermute | solution.py:255
  57.2 22.6 %collective-permute-start.14 = (bf16[128,1024]{1,0:T(8,128)(2,1)S(1)}, bf16[128,1024]{1,0:T(8,128)(2,1)S(1)}, u32[]{:S(2)}, u32[]{:S(2)}) collective-permute-start(bf16[128,1024]{1,0:T(8,128)(2,1)S(1)} %get-tuple-element.57), channel_id=1, source_target_pairs={{0,0},{1,4},{2,8},{3,12},{4,16},{5,20},{6,24},{7,28},{8,1},{9,5},{... | collective-permute-start | bytes 786440 | tf_op jit(solution)/shard_map/ppermute | solution.py:271
  62.3 24.7 %collective-permute-start.15 = (bf16[128,1024]{1,0:T(8,128)(2,1)S(1)}, bf16[128,1024]{1,0:T(8,128)(2,1)S(1)}, u32[]{:S(2)}, u32[]{:S(2)}) collective-permute-start(bf16[128,1024]{1,0:T(8,128)(2,1)S(1)} %get-tuple-element.58), channel_id=1, source_target_pairs={{0,8},{1,12},{2,0},{3,4},{4,24},{5,28},{6,16},{7,20},{8,9},{9,13},... | collective-permute-start | bytes 786440 | tf_op jit(solution)/shard_map/ppermute | solution.py:271
  64.0 23.0 %collective-permute-start.16 = (bf16[128,1024]{1,0:T(8,128)(2,1)S(1)}, bf16[128,1024]{1,0:T(8,128)(2,1)S(1)}, u32[]{:S(2)}, u32[]{:S(2)}) collective-permute-start(bf16[128,1024]{1,0:T(8,128)(2,1)S(1)} %get-tuple-element.59), channel_id=1, source_target_pairs={{0,16},{1,20},{2,24},{3,28},{4,0},{5,4},{6,8},{7,12},{8,17},{9,21}... | collective-permute-start | bytes 786440 | tf_op jit(solution)/shard_map/ppermute | solution.py:271
  64.0 24.0 %collective-permute-start.17 = (bf16[128,1024]{1,0:T(8,128)(2,1)S(1)}, bf16[128,1024]{1,0:T(8,128)(2,1)S(1)}, u32[]{:S(2)}, u32[]{:S(2)}) collective-permute-start(bf16[128,1024]{1,0:T(8,128)(2,1)S(1)} %get-tuple-element.60), channel_id=1, source_target_pairs={{0,24},{1,28},{2,16},{3,20},{4,8},{5,12},{6,0},{7,4},{8,25},{9,29}... | collective-permute-start | bytes 786440 | tf_op jit(solution)/shard_map/ppermute | solution.py:271

commit v4 on v3

--- a/solution.py
+++ b/solution.py
@@ -50,20 +50,19 @@
         out_ref[base + 2 * rows :, :] = meta.astype(jnp.bfloat16)
 
 
-def attend_kernel(parts, heads, scale, wave, *refs):
-    half = parts // 2
+def attend_kernel(parts, heads, scale, slots, *refs):
+    half, many = parts // 2, len(slots)
     near, far, refs = refs[:half], refs[half : 2 * half], refs[2 * half :]
-    q_blocks = near
-    if wave:
-        q_blocks, refs = refs[:half], refs[half:]
-    send_ref, keep_ref, q_held, kv_held, vals_ref, rows_ref, ends, sems = refs
+    q_blocks = [near[k] for k in slots if k < half]
+    if not q_blocks:
+        q_blocks, refs = refs[:many], refs[many:]
+    send_ref, keep_ref, q_held, kv_held, rows_ref, ends, sems = refs
     rows = q_held.shape[1] // heads
     piece = rows // parts
     me = lax.axis_index("ctx")
     other = 1 - lax.rem(lax.axis_index("head"), 2)
-    first_block = half * lax.rem(lax.div(me, half) + wave, 2)
     q_rows = heads * rows
-    kv_copies = [
+    copies = [
         pltpu.make_async_copy(
             near[k].at[q_rows:], kv_held.at[jnp.bitwise_xor(me, k)], sems.at[half + k]
         )
@@ -73,33 +72,25 @@
             far[k], kv_held.at[jnp.bitwise_xor(me, half + k)], sems.at[2 * half + k]
         )
         for k in range(half)
+    ] + [
+        pltpu.make_async_copy(q_blocks[i].at[:q_rows], q_held.at[i], sems.at[i])
+        for i in range(many)
     ]
-    copies = [
-        pltpu.make_async_copy(
-            q_blocks[k].at[:q_rows], q_held.at[jnp.bitwise_xor(lax.rem(me, half), k)], sems.at[k]
-        )
-        for k in range(half)
-    ]
-    for copy in kv_copies + copies:
+    for copy in copies:
         copy.start()
-    for copy in kv_copies:
+    for copy in copies:
         copy.wait()
 
     def ids_of(block):
         return kv_held[block, 2 * rows :, :].astype(jnp.float32)
 
     for b in range(parts):
-        vals_ref[b, :, :HEAD_DIM] = kv_held[b, rows : 2 * rows, :]
-        vals_ref[b, :, HEAD_DIM:] = jnp.ones((rows, HEAD_DIM), jnp.bfloat16)
         ids = ids_of(b)[0:1]
         ends[0, b] = jnp.min(ids)
         ends[1, b] = jnp.max(ids)
 
-    for copy in copies:
-        copy.wait()
-
     def one_block(i, carry):
-        d = first_block + i
+        d = jnp.bitwise_xor(me, slots[0] + i)
         turned = ids_of(d).T
         q_ids, q_pos = turned[:, 1:2], turned[:, 2:3]
         start = jnp.int32(0)
@@ -117,7 +108,8 @@
                 allowed = (k_ids == q_ids) & (k_pos.astype(jnp.float32) <= q_pos)
                 bias = jnp.where(allowed, 0.0, NEG_FILL)
                 keys = kv_held[pl.ds(b0, 2 * w), :rows, :].reshape(span, HEAD_DIM)
-                vals = vals_ref[pl.ds(b0, 2 * w), :, :].reshape(span, 2 * HEAD_DIM)
+                vals = kv_held[pl.ds(b0, 2 * w), rows : 2 * rows, :].reshape(span, HEAD_DIM)
+                vals = jnp.concatenate([vals, jnp.ones((span, HEAD_DIM), jnp.bfloat16)], axis=1)
                 for h in range(heads):
                     q = q_held[i, h * rows : (h + 1) * rows, :]
                     s = lax.dot_general(
@@ -129,7 +121,7 @@
                     o = jnp.dot(e.astype(jnp.bfloat16), vals, preferred_element_type=jnp.float32)
                     o = (o[:, :HEAD_DIM] / o[:, HEAD_DIM:]).astype(jnp.bfloat16)
                     for j in range(parts):
-                        at = pl.multiple_of((j // 2) * half * piece + i * piece, piece)
+                        at = pl.multiple_of((j // 2) * many * piece + i * piece, piece)
                         rows_ref[
                             jnp.bitwise_xor(other, j % 2),
                             pl.ds(at, piece),
@@ -138,7 +130,7 @@
 
         return carry
 
-    lax.fori_loop(0, half, one_block, 0)
+    lax.fori_loop(0, many, one_block, 0)
     out = [
         pltpu.make_async_copy(rows_ref.at[0], send_ref, sems.at[0]),
         pltpu.make_async_copy(rows_ref.at[1], keep_ref, sems.at[1]),
@@ -149,22 +141,29 @@
         copy.wait()
 
 
-def project_kernel(group, half, *refs):
-    (keep_0, got_0, keep_1, got_1, w_ref, w_pair_ref), refs = refs[:6], refs[6:]
-    out_refs, total = refs[:-1], refs[-1]
+def project_kernel(group, half, parts, groups_of_slots, *refs):
+    halves, refs = refs[: 2 * len(groups_of_slots)], refs[2 * len(groups_of_slots) :]
+    w_ref, w_pair_ref, refs = refs[0], refs[1], refs[2:]
+    out_refs, (x_keep, x_got, total) = refs[:-3], refs[-3:]
     count = len(out_refs)
-    rows = keep_0.shape[0] // count
+    rows = out_refs[0].shape[0]
+    piece = rows // parts
     me = lax.axis_index("ctx")
-    upper = lax.div(me, count)
+    for n, slots in enumerate(groups_of_slots):
+        for held, part in ((x_keep, halves[2 * n]), (x_got, halves[2 * n + 1])):
+            for i, slot in enumerate(slots):
+                d = jnp.bitwise_xor(me, slot)
+                for a in range(count):
+                    at = pl.ds(pl.multiple_of(a * rows + d * piece, piece), piece)
+                    first = (a * len(slots) + i) * piece
+                    held[at, :] = part[first : first + piece, :]
+    total[...] = jnp.dot(x_keep[...], w_ref[...], preferred_element_type=jnp.float32) + jnp.dot(
+        x_got[...], w_pair_ref[...], preferred_element_type=jnp.float32
+    )
     mine = lax.rem(me, group) * half + lax.div(lax.axis_index("head"), 2)
-    for wave, keep_ref, got_ref in ((0, keep_0, got_0), (1, keep_1, got_1)):
-        total[...] = jnp.dot(
-            keep_ref[...], w_ref[...], preferred_element_type=jnp.float32
-        ) + jnp.dot(got_ref[...], w_pair_ref[...], preferred_element_type=jnp.float32)
-        place = pl.ds(pl.multiple_of(lax.rem(upper + wave, 2) * rows, rows), rows)
-        for k, out_ref in enumerate(out_refs):
-            at = pl.ds(pl.multiple_of(jnp.bitwise_xor(mine, k) * rows, rows), rows)
-            out_ref[place, :] = total[at, :].astype(jnp.bfloat16)
+    for k, out_ref in enumerate(out_refs):
+        at = pl.ds(pl.multiple_of(jnp.bitwise_xor(mine, k) * rows, rows), rows)
+        out_ref[...] = total[at, :].astype(jnp.bfloat16)
 
 
 def final_kernel(group, half, *refs):
@@ -183,25 +182,33 @@
     return lax.ppermute(x, "ctx", [(i, i ^ k) for i in range(parts)])
 
 
-def spread_over_ctx(block, q_block, kv_block, parts):
+def spread_first(block, q_block, kv_block, parts):
     half = parts // 2
-    near, far_q, far_kv = {0: block}, {}, {}
-    far_q[0] = along_ctx(q_block, parts, half)
+    near, far_kv = {0: block}, {}
+    far_kv[0] = along_ctx(kv_block, parts, half)
+    far_kv[1] = along_ctx(kv_block, parts, half + 1)
     for k in [*range(2, half, 2), 1]:
         near[k] = along_ctx(block, parts, k)
-    far_kv[0] = along_ctx(kv_block, parts, half)
-    far_kv[1] = along_ctx(kv_block, parts, half + 1)
-    near, far_q, far_kv = lax.optimization_barrier((near, far_q, far_kv))
+    far_q = along_ctx(q_block, parts, half)
+    near, far_kv = lax.optimization_barrier((near, far_kv))
     for k in range(2, half, 2):
         near[k + 1] = along_ctx(near[k], parts, 1)
-        far_q[k] = along_ctx(far_q[0], parts, k)
         far_kv[k] = along_ctx(far_kv[0], parts, k)
         far_kv[k + 1] = along_ctx(far_kv[1], parts, k)
-    far_q[1] = along_ctx(far_q[0], parts, 1)
-    near, far_q, far_kv = lax.optimization_barrier((near, far_q, far_kv))
+    return [near[k] for k in range(half)], [far_kv[k] for k in range(half)], far_q
+
+
+def spread_second(far_q, parts):
+    half = parts // 2
+    got = {k: along_ctx(far_q, parts, k) for k in [*range(2, half, 2), 1]}
+    return lax.optimization_barrier(got)
+
+
+def spread_third(far_q, got, parts):
+    half = parts // 2
     for k in range(2, half, 2):
-        far_q[k + 1] = along_ctx(far_q[k], parts, 1)
-    return [[some[k] for k in range(half)] for some in (near, far_q, far_kv)]
+        got[k + 1] = along_ctx(got[k], parts, 1)
+    return [far_q] + [got[k] for k in range(1, half)]
 
 
 def packed_body(groups, queries, keys, values, doc_ids, plan, w_out):
@@ -227,38 +234,50 @@
         compiler_params=pltpu.CompilerParams(vmem_limit_bytes=PACK_LIMIT),
         name="pack",
     )(plan, queries, keys, values, doc_ids.reshape(1, rows))
-    near, far_q, far_kv = spread_over_ctx(block, q_block, kv_block, parts)
-    wave_rows = parts * rows // 4
+    near, far_kv, far_q = spread_first(block, q_block, kv_block, parts)
     count = parts // 2
     arrived, halves = [], []
-    for wave in range(2):
+    last = parts - 1
+    slot_groups = [range(count), range(count, count + 1), range(count + 1, last), range(last, parts)]
+    for slots in slot_groups:
         inputs = [*near, *far_kv]
-        if wave:
-            inputs = inputs + far_q
+        if slots[0] >= count:
+            inputs += far_q[slots[0] - count : slots[-1] + 1 - count]
+        many = len(slots)
+        out_rows = count * many * rows // parts
         send, keep = pl.pallas_call(
-            functools.partial(attend_kernel, parts, heads, 1.0 / math.sqrt(HEAD_DIM), wave),
-            out_shape=[jax.ShapeDtypeStruct((wave_rows, heads * HEAD_DIM), bf16)] * 2,
+            functools.partial(attend_kernel, parts, heads, 1.0 / math.sqrt(HEAD_DIM), tuple(slots)),
+            out_shape=[jax.ShapeDtypeStruct((out_rows, heads * HEAD_DIM), bf16)] * 2,
             in_specs=[ANY] * len(inputs),
             out_specs=[ANY, ANY],
             scratch_shapes=[
-                pltpu.VMEM((count, heads * rows, HEAD_DIM), bf16),
+                pltpu.VMEM((many, heads * rows, HEAD_DIM), bf16),
                 pltpu.VMEM((parts, kv_rows, HEAD_DIM), bf16),
-                pltpu.VMEM((parts, rows, 2 * HEAD_DIM), bf16),
-                pltpu.VMEM((2, wave_rows, heads * HEAD_DIM), bf16),
+                pltpu.VMEM((2, out_rows, heads * HEAD_DIM), bf16),
                 pltpu.SMEM((2, parts), jnp.float32),
                 pltpu.SemaphoreType.DMA((count + parts,)),
             ],
             compiler_params=params,
-            cost_estimate=pl.CostEstimate(flops=8 * 10**9, bytes_accessed=2**22, transcendentals=0),
             name="attend",
         )(*inputs)
+        if slots[0] == 0:
+            send, far_q = lax.optimization_barrier((send, far_q))
+            second = spread_second(far_q, parts)
+            far_q = [far_q]
+        if slots[0] == count:
+            send, second = lax.optimization_barrier((send, second))
+            far_q = spread_third(far_q[0], second, parts)
         halves += [keep, lax.ppermute(send, "head", pair)]
     sums = pl.pallas_call(
-        functools.partial(project_kernel, group, half),
+        functools.partial(project_kernel, group, half, parts, slot_groups),
         out_shape=[jax.ShapeDtypeStruct((rows, width), bf16)] * count,
-        in_specs=[VMEM] * 6,
+        in_specs=[VMEM] * (2 * len(slot_groups) + 2),
         out_specs=[VMEM] * count,
-        scratch_shapes=[pltpu.VMEM((wave_rows, width), jnp.float32)],
+        scratch_shapes=[
+            pltpu.VMEM((count * rows, heads * HEAD_DIM), bf16),
+            pltpu.VMEM((count * rows, heads * HEAD_DIM), bf16),
+            pltpu.VMEM((count * rows, width), jnp.float32),
+        ],
         compiler_params=params,
         name="project",
     )(*halves, w_out, w_pair)

time: 89.1 us -> 87.8 us (0.985)
  waiting for transfers between devices: 41 us -> 38.2 us
  Pallas kernels: 18 us -> 20.3 us
    ppermute x2 -> x4, starting transfers between devices: 4.37 us -> 8.56 us  [packed_body(): halves += [keep, lax.ppermute(send, 'head', pair)]]
    ppermute x11, starting transfers between devices: 11.7 us -> 9.19 us  [along_ctx(): return lax.ppermute(x, 'ctx', [(i, i ^ k) for i in range(parts)])]
    ppermute x1, starting transfers between devices: 2.96 us -> 0.68 us  [packed_body(): w_pair = lax.ppermute(w_out, 'head', pair)]
    pallas_call x2 -> x4, Pallas kernels: 12.8 us -> 15 us  [packed_body(): pl.pallas_call(functools.partial(attend_kernel, parts, heads, 1.0 / math....]
    ppermute x4, waiting for transfers between devices: 21 us -> 20 us  [packed_body(): arrived.append(lax.ppermute(sums[k], ('ctx', 'head'), pairs))]
    ppermute x2 -> x4, waiting for transfers between devices: 1.85 us -> 0.98 us  [packed_body(): halves += [keep, lax.ppermute(send, 'head', pair)]]
  transfers between devices with their start and end apart: 18 -> 20, of which waited for: 9 -> 10; matrix products, arithmetic and copies ran while one was open for 0% -> 0% of each run, Pallas kernels for 14% -> 19%
where the time goes in v4:
time: 87.8 us; the launch traced here: 88 us
  waiting for transfers between devices  38.2 us (44%)
  starting transfers between devices  28.4 us (32%)
  Pallas kernels  20.3 us (23%)
  local copies, waits for them, and re-layouts  0.98 us (1%)
    ppermute x4, waiting for transfers between devices, packed_body(): arrived.append(lax.ppermute(sums[k], ('ctx', 'head'), pairs))  20 us
    ppermute x11, waiting for transfers between devices, along_ctx(): return lax.ppermute(x, 'ctx', [(i, i ^ k) for i in range(parts)])  17.3 us
    pallas_call x4, Pallas kernels, packed_body(): pl.pallas_call(functools.partial(attend_kernel, parts, heads, 1.0 / math....  15 us
    ppermute x4, starting transfers between devices, packed_body(): arrived.append(lax.ppermute(sums[k], ('ctx', 'head'), pairs))  9.96 us
    ppermute x11, starting transfers between devices, along_ctx(): return lax.ppermute(x, 'ctx', [(i, i ^ k) for i in range(parts)])  9.19 us
    ppermute x4, starting transfers between devices, packed_body(): halves += [keep, lax.ppermute(send, 'head', pair)]  8.56 us
    pallas_call x1, Pallas kernels, packed_body(): pl.pallas_call(functools.partial(project_kernel, group, half, parts, slot...  2.51 us
    pallas_call x1, Pallas kernels, packed_body(): pl.pallas_call(functools.partial(pack_kernel, parts, heads), out_shape=[j...  1.92 us
  transfers between devices with their start and end apart: 20, of which 10 were waited for; matrix products, arithmetic and copies ran while one was open for 0% of the time, Pallas kernels for 19%

profile of v4, /device:TPU:17, one launch (start us, length us, event | category | flops | bytes accessed | tf_op | source)
XLA Modules:
  0.0 88.0 jit_solution(418137952568195321)
XLA Ops:
  0.0 0.7 collective-permute-start.15
  0.7 1.9 %pack.1 = (bf16[1296,128]{1,0:T(8,128)(2,1)}, bf16[1024,128]{1,0:T(8,128)(2,1)}, bf16[272,128]{1,0:T(8,128)(2,1)}) custom-call(s32[1,8]{1,0:T(1,128)} %plan_ref.1, bf16[128,1024]{1,0:T(8,128)(2,1)} %q_ref.1, bf16[128,128]{1,0:T(8,128)(2,1)} %k_ref.1, bf16[128,128]{1,0:T(8,128)(2,1)} %v_ref.1, s32[1,128]{1,0:T(1,128)} %bitcast.1), custom_call_target="tpu_custom_call" | custom-call | tf_op jit(solution)/shard_map/pack/pallas_call | solution.py:225
  2.6 1.3 %collective-permute-start.1 = (bf16[1296,128]{1,0:T(8,128)(2,1)}, bf16[1296,128]{1,0:T(8,128)(2,1)S(1)}, u32[]{:S(2)}, u32[]{:S(2)}) collective-permute-start(bf16[1296,128]{1,0:T(8,128)(2,1)} %get-tuple-element.34.refs_0_), channel_id=1, source_target_pairs={{0,8},{4,12},{8,0},{12,4},{16,24},{20,28},{24,16},{28,20},{1,9},{5... | collective-permute-start | bytes 995336 | tf_op jit(solution)/shard_map/ppermute | solution.py:182
  3.9 1.2 %collective-permute-start = (bf16[1296,128]{1,0:T(8,128)(2,1)}, bf16[1296,128]{1,0:T(8,128)(2,1)S(1)}, u32[]{:S(2)}, u32[]{:S(2)}) collective-permute-start(bf16[1296,128]{1,0:T(8,128)(2,1)} %get-tuple-element.34.refs_0_), channel_id=1, source_target_pairs={{0,4},{4,0},{8,12},{12,8},{16,20},{20,16},{24,28},{28,24},{1,5},{5... | collective-permute-start | bytes 995336 | tf_op jit(solution)/shard_map/ppermute | solution.py:182
  5.1 0.0 collective-permute-start.3
  5.1 2.3 %collective-permute-start.2 = (bf16[272,128]{1,0:T(8,128)(2,1)}, bf16[272,128]{1,0:T(8,128)(2,1)S(1)}, u32[]{:S(2)}, u32[]{:S(2)}) collective-permute-start(bf16[272,128]{1,0:T(8,128)(2,1)} %get-tuple-element.33), channel_id=1, source_target_pairs={{0,16},{4,20},{8,24},{12,28},{16,0},{20,4},{24,8},{28,12},{1,17},{... | collective-permute-start | bytes 208904 | tf_op jit(solution)/shard_map/ppermute | solution.py:182
  7.4 7.1 %collective-permute-done.3.refs_5_ = bf16[272,128]{1,0:T(8,128)(2,1)S(1)} collective-permute-done((bf16[272,128]{1,0:T(8,128)(2,1)}, bf16[272,128]{1,0:T(8,128)(2,1)S(1)}, u32[]{:S(2)}, u32[]{:S(2)}) %collective-permute-start.3) | collective-permute-done | bytes 69664 | tf_op jit(solution)/shard_map/ppermute | solution.py:182
  14.6 0.5 collective-permute-done.2.refs_4_
  15.1 0.0 collective-permute-done.1.refs_2_
  15.1 0.0 collective-permute-done.refs_1_
  15.1 1.2 %collective-permute-start.4 = (bf16[1296,128]{1,0:T(8,128)(2,1)S(1)}, bf16[1296,128]{1,0:T(8,128)(2,1)S(1)}, u32[]{:S(2)}, u32[]{:S(2)}) collective-permute-start(bf16[1296,128]{1,0:T(8,128)(2,1)S(1)} %collective-permute-done.1.refs_2_), channel_id=1, source_target_pairs={{0,4},{4,0},{8,12},{12,8},{16,20},{20,16},{24,28},{28,24},{1,5},{5... | collective-permute-start | bytes 995336 | tf_op jit(solution)/shard_map/ppermute | solution.py:182
  16.4 0.2 collective-permute-start.7
  16.5 2.3 %collective-permute-start.5 = (bf16[272,128]{1,0:T(8,128)(2,1)S(1)}, bf16[272,128]{1,0:T(8,128)(2,1)S(1)}, u32[]{:S(2)}, u32[]{:S(2)}) collective-permute-start(bf16[272,128]{1,0:T(8,128)(2,1)S(1)} %collective-permute-done.2.refs_4_), channel_id=1, source_target_pairs={{0,8},{4,12},{8,0},{12,4},{16,24},{20,28},{24,16},{28,20},{1,9},{5... | collective-permute-start | bytes 208904 | tf_op jit(solution)/shard_map/ppermute | solution.py:182
  18.8 0.0 collective-permute-start.6
  18.9 7.0 %collective-permute-done.5.refs_6_ = bf16[272,128]{1,0:T(8,128)(2,1)S(1)} collective-permute-done((bf16[272,128]{1,0:T(8,128)(2,1)S(1)}, bf16[272,128]{1,0:T(8,128)(2,1)S(1)}, u32[]{:S(2)}, u32[]{:S(2)}) %collective-permute-start.5) | collective-permute-done | bytes 69664 | tf_op jit(solution)/shard_map/ppermute | solution.py:182
  25.9 1.4 %collective-permute-done.6.refs_7_ = bf16[272,128]{1,0:T(8,128)(2,1)S(1)} collective-permute-done((bf16[272,128]{1,0:T(8,128)(2,1)S(1)}, bf16[272,128]{1,0:T(8,128)(2,1)S(1)}, u32[]{:S(2)}, u32[]{:S(2)}) %collective-permute-start.6) | collective-permute-done | bytes 69664 | tf_op jit(solution)/shard_map/ppermute | solution.py:182
  27.3 0.0 collective-permute-done.4.refs_3_
  27.3 1.0 %copy-done = bf16[1296,128]{1,0:T(8,128)(2,1)S(1)} copy-done((bf16[1296,128]{1,0:T(8,128)(2,1)S(1)}, bf16[1296,128]{1,0:T(8,128)(2,1)}, u32[]{:S(2)}) %copy-start) | copy-done | bytes 331800
  28.3 7.7 %attend.4 = (bf16[256,1024]{1,0:T(8,128)(2,1)S(1)}, bf16[256,1024]{1,0:T(8,128)(2,1)S(1)}) custom-call(bf16[1296,128]{1,0:T(8,128)(2,1)S(1)} %copy-done, bf16[1296,128]{1,0:T(8,128)(2,1)S(1)} %collective-permute-done.refs_1_, bf16[1296,128]{1,0:T(8,128)(2,1)S(1)} %collective-permute-done.1.refs_2_, bf16[1296,128]{1,0:T(8,128)(2,1)S(1)} %collective-permute-done.4.refs_3_, ...), custom_call_target="tpu_custom_call" | custom-call | tf_op jit(solution)/shard_map/attend/pallas_call | solution.py:248
  36.0 0.0 collective-permute-done.7.refs_8_
  36.0 0.1 collective-permute-start.10
  36.1 0.3 collective-permute-start.9
  36.4 2.3 %collective-permute-start.8 = (bf16[256,1024]{1,0:T(8,128)(2,1)S(1)}, bf16[256,1024]{1,0:T(8,128)(2,1)S(1)}, u32[]{:S(2)}, u32[]{:S(2)}) collective-permute-start(bf16[256,1024]{1,0:T(8,128)(2,1)S(1)} %get-tuple-element.42), channel_id=1, source_target_pairs={{0,1},{1,0},{2,3},{3,2},{4,5},{5,4},{6,7},{7,6},{8,9},{9,8},{10,11... | collective-permute-start | bytes 1572872 | tf_op jit(solution)/shard_map/ppermute | solution.py:270
  38.7 2.1 %attend.5 = (bf16[64,1024]{1,0:T(8,128)(2,1)S(1)}, bf16[64,1024]{1,0:T(8,128)(2,1)S(1)}) custom-call(bf16[1296,128]{1,0:T(8,128)(2,1)S(1)} %copy-done, bf16[1296,128]{1,0:T(8,128)(2,1)S(1)} %collective-permute-done.refs_1_, bf16[1296,128]{1,0:T(8,128)(2,1)S(1)} %collective-permute-done.1.refs_2_, bf16[1296,128]{1,0:T(8,128)(2,1)S(1)} %collective-permute-done.4.refs_3_, ...), custom_call_target="tpu_custom_call" | custom-call | tf_op jit(solution)/shard_map/attend/pallas_call | solution.py:248
  40.8 0.0 copy-start.1
  40.8 1.0 %collective-permute-done.10.refs_9_ = bf16[1024,128]{1,0:T(8,128)(2,1)S(1)} collective-permute-done((bf16[1024,128]{1,0:T(8,128)(2,1)S(1)}, bf16[1024,128]{1,0:T(8,128)(2,1)S(1)}, u32[]{:S(2)}, u32[]{:S(2)}) %collective-permute-start.10) | collective-permute-done | bytes 262176 | tf_op jit(solution)/shard_map/ppermute | solution.py:182
  41.9 0.1 collective-permute-done.9.refs_8_
  42.0 0.2 collective-permute-start.13
  42.2 2.8 %attend.6 = (bf16[128,1024]{1,0:T(8,128)(2,1)S(1)}, bf16[128,1024]{1,0:T(8,128)(2,1)S(1)}) custom-call(bf16[1296,128]{1,0:T(8,128)(2,1)S(1)} %copy-done, bf16[1296,128]{1,0:T(8,128)(2,1)S(1)} %collective-permute-done.refs_1_, bf16[1296,128]{1,0:T(8,128)(2,1)S(1)} %collective-permute-done.1.refs_2_, bf16[1296,128]{1,0:T(8,128)(2,1)S(1)} %collective-permute-done.4.refs_3_, ...), custom_call_target="tpu_custom_call" | custom-call | tf_op jit(solution)/shard_map/attend/pallas_call | solution.py:248
  45.0 3.3 %collective-permute-start.12 = (bf16[128,1024]{1,0:T(8,128)(2,1)S(1)}, bf16[128,1024]{1,0:T(8,128)(2,1)S(1)}, u32[]{:S(2)}, u32[]{:S(2)}) collective-permute-start(bf16[128,1024]{1,0:T(8,128)(2,1)S(1)} %get-tuple-element.52), channel_id=1, source_target_pairs={{0,1},{1,0},{2,3},{3,2},{4,5},{5,4},{6,7},{7,6},{8,9},{9,8},{10,11... | collective-permute-start | bytes 786440 | tf_op jit(solution)/shard_map/ppermute | solution.py:270
  48.3 0.1 collective-permute-start.11
  48.4 0.0 collective-permute-done.13.refs_8_
  48.4 2.3 %attend.7 = (bf16[64,1024]{1,0:T(8,128)(2,1)S(1)}, bf16[64,1024]{1,0:T(8,128)(2,1)S(1)}) custom-call(bf16[1296,128]{1,0:T(8,128)(2,1)S(1)} %copy-done, bf16[1296,128]{1,0:T(8,128)(2,1)S(1)} %collective-permute-done.refs_1_, bf16[1296,128]{1,0:T(8,128)(2,1)S(1)} %collective-permute-done.1.refs_2_, bf16[1296,128]{1,0:T(8,128)(2,1)S(1)} %collective-permute-done.4.refs_3_, ...), custom_call_target="tpu_custom_call" | custom-call | tf_op jit(solution)/shard_map/attend/pallas_call | solution.py:248
  50.7 2.9 %collective-permute-start.14 = (bf16[64,1024]{1,0:T(8,128)(2,1)S(1)}, bf16[64,1024]{1,0:T(8,128)(2,1)S(1)}, u32[]{:S(2)}, u32[]{:S(2)}) collective-permute-start(bf16[64,1024]{1,0:T(8,128)(2,1)S(1)} %get-tuple-element.54), channel_id=1, source_target_pairs={{0,1},{1,0},{2,3},{3,2},{4,5},{5,4},{6,7},{7,6},{8,9},{9,8},{10,11... | collective-permute-start | bytes 393224 | tf_op jit(solution)/shard_map/ppermute | solution.py:270
  53.6 0.0 collective-permute-done.11.refs_3_
  53.6 0.0 collective-permute-done.12.refs_5_
  53.6 0.0 collective-permute-done.8.refs_1_
  53.6 1.0 %collective-permute-done.14.refs_7_ = bf16[64,1024]{1,0:T(8,128)(2,1)S(1)} collective-permute-done((bf16[64,1024]{1,0:T(8,128)(2,1)S(1)}, bf16[64,1024]{1,0:T(8,128)(2,1)S(1)}, u32[]{:S(2)}, u32[]{:S(2)}) %collective-permute-start.14) | collective-permute-done | bytes 131104 | tf_op jit(solution)/shard_map/ppermute | solution.py:270
  54.6 0.0 collective-permute-done.15.refs_9_
  54.6 2.5 %project.1 = (bf16[128,1024]{1,0:T(8,128)(2,1)S(1)}, bf16[128,1024]{1,0:T(8,128)(2,1)S(1)}, bf16[128,1024]{1,0:T(8,128)(2,1)S(1)}, bf16[128,1024]{1,0:T(8,128)(2,1)S(1)}) custom-call(bf16[256,1024]{1,0:T(8,128)(2,1)S(1)} %get-tuple-element.39.refs_0_, bf16[256,1024]{1,0:T(8,128)(2,1)S(1)} %collective-permute-done.8.refs_1_, ...), custom_call_target="tpu_custom_call" | custom-call | tf_op jit(solution)/shard_map/project/pallas_call | solution.py:271
  57.1 2.5 %collective-permute-start.16 = (bf16[128,1024]{1,0:T(8,128)(2,1)S(1)}, bf16[128,1024]{1,0:T(8,128)(2,1)S(1)}, u32[]{:S(2)}, u32[]{:S(2)}) collective-permute-start(bf16[128,1024]{1,0:T(8,128)(2,1)S(1)} %get-tuple-element.55), channel_id=1, source_target_pairs={{0,0},{1,4},{2,8},{3,12},{4,16},{5,20},{6,24},{7,28},{8,1},{9,5},{... | collective-permute-start | bytes 786440 | tf_op jit(solution)/shard_map/ppermute | solution.py:290
  59.7 3.8 %collective-permute-start.17 = (bf16[128,1024]{1,0:T(8,128)(2,1)S(1)}, bf16[128,1024]{1,0:T(8,128)(2,1)S(1)}, u32[]{:S(2)}, u32[]{:S(2)}) collective-permute-start(bf16[128,1024]{1,0:T(8,128)(2,1)S(1)} %get-tuple-element.56), channel_id=1, source_target_pairs={{0,8},{1,12},{2,0},{3,4},{4,24},{5,28},{6,16},{7,20},{8,9},{9,13},... | collective-permute-start | bytes 786440 | tf_op jit(solution)/shard_map/ppermute | solution.py:290
  63.5 0.0 collective-permute-start.18
  63.5 3.6 %collective-permute-start.19 = (bf16[128,1024]{1,0:T(8,128)(2,1)S(1)}, bf16[128,1024]{1,0:T(8,128)(2,1)S(1)}, u32[]{:S(2)}, u32[]{:S(2)}) collective-permute-start(bf16[128,1024]{1,0:T(8,128)(2,1)S(1)} %get-tuple-element.58), channel_id=1, source_target_pairs={{0,24},{1,28},{2,16},{3,20},{4,8},{5,12},{6,0},{7,4},{8,25},{9,29}... | collective-permute-start | bytes 786440 | tf_op jit(solution)/shard_map/ppermute | solution.py:290
  67.1 12.4 %collective-permute-done.16.refs_0_ = bf16[128,1024]{1,0:T(8,128)(2,1)S(1)} collective-permute-done((bf16[128,1024]{1,0:T(8,128)(2,1)S(1)}, bf16[128,1024]{1,0:T(8,128)(2,1)S(1)}, u32[]{:S(2)}, u32[]{:S(2)}) %collective-permute-start.16) | collective-permute-done | bytes 262176 | tf_op jit(solution)/shard_map/ppermute | solution.py:290
  79.5 6.0 %collective-permute-done.17.refs_1_ = bf16[128,1024]{1,0:T(8,128)(2,1)S(1)} collective-permute-done((bf16[128,1024]{1,0:T(8,128)(2,1)S(1)}, bf16[128,1024]{1,0:T(8,128)(2,1)S(1)}, u32[]{:S(2)}, u32[]{:S(2)}) %collective-permute-start.17) | collective-permute-done | bytes 262176 | tf_op jit(solution)/shard_map/ppermute | solution.py:290
  85.6 1.5 %collective-permute-done.19.refs_3_ = bf16[128,1024]{1,0:T(8,128)(2,1)S(1)} collective-permute-done((bf16[128,1024]{1,0:T(8,128)(2,1)S(1)}, bf16[128,1024]{1,0:T(8,128)(2,1)S(1)}, u32[]{:S(2)}, u32[]{:S(2)}) %collective-permute-start.19) | collective-permute-done | bytes 262176 | tf_op jit(solution)/shard_map/ppermute | solution.py:290
  87.1 0.9 %final_sum.1 = bf16[128,2048]{1,0:T(8,128)(2,1)} custom-call(bf16[128,1024]{1,0:T(8,128)(2,1)S(1)} %collective-permute-done.16.refs_0_, bf16[128,1024]{1,0:T(8,128)(2,1)S(1)} %collective-permute-done.17.refs_1_, bf16[128,1024]{1,0:T(8,128)(2,1)S(1)} %collective-permute-done.18.refs_2_, bf16[128,1024]{1,0:T(8,128)(2,1)S(1)} %collective-permute-done.19.refs_3_), custom_call_target="tpu_custom_call" | custom-call | tf_op jit(solution)/shard_map/final_sum/pallas_call | solution.py:291
  (3 shorter events, 0.0 us)
Async XLA Ops:
  0.0 54.6 %collective-permute-start.15 = (bf16[1024,1024]{1,0:T(8,128)(2,1)}, bf16[1024,1024]{1,0:T(8,128)(2,1)S(1)}, u32[]{:S(2)}, u32[]{:S(2)}) collective-permute-start(bf16[1024,1024]{1,0:T(8,128)(2,1)} %refs_8_.1), channel_id=1, source_target_pairs={{0,1},{1,0},{2,3},{3,2},{4,5},{5,4},{6,7},{7,6},{8,9},{9,8},{10,11... | collective-permute-start | bytes 6291464 | tf_op jit(solution)/shard_map/ppermute | solution.py:224
  2.6 12.5 %collective-permute-start.1 = (bf16[1296,128]{1,0:T(8,128)(2,1)}, bf16[1296,128]{1,0:T(8,128)(2,1)S(1)}, u32[]{:S(2)}, u32[]{:S(2)}) collective-permute-start(bf16[1296,128]{1,0:T(8,128)(2,1)} %get-tuple-element.34.refs_0_), channel_id=1, source_target_pairs={{0,8},{4,12},{8,0},{12,4},{16,24},{20,28},{24,16},{28,20},{1,9},{5... | collective-permute-start | bytes 995336 | tf_op jit(solution)/shard_map/ppermute | solution.py:182
  3.9 11.2 %collective-permute-start = (bf16[1296,128]{1,0:T(8,128)(2,1)}, bf16[1296,128]{1,0:T(8,128)(2,1)S(1)}, u32[]{:S(2)}, u32[]{:S(2)}) collective-permute-start(bf16[1296,128]{1,0:T(8,128)(2,1)} %get-tuple-element.34.refs_0_), channel_id=1, source_target_pairs={{0,4},{4,0},{8,12},{12,8},{16,20},{20,16},{24,28},{28,24},{1,5},{5... | collective-permute-start | bytes 995336 | tf_op jit(solution)/shard_map/ppermute | solution.py:182
  5.1 9.4 %collective-permute-start.3 = (bf16[272,128]{1,0:T(8,128)(2,1)}, bf16[272,128]{1,0:T(8,128)(2,1)S(1)}, u32[]{:S(2)}, u32[]{:S(2)}) collective-permute-start(bf16[272,128]{1,0:T(8,128)(2,1)} %get-tuple-element.33), channel_id=1, source_target_pairs={{0,20},{4,16},{8,28},{12,24},{16,4},{20,0},{24,12},{28,8},{1,21},{... | collective-permute-start | bytes 208904 | tf_op jit(solution)/shard_map/ppermute | solution.py:182
  5.1 10.0 %collective-permute-start.2 = (bf16[272,128]{1,0:T(8,128)(2,1)}, bf16[272,128]{1,0:T(8,128)(2,1)S(1)}, u32[]{:S(2)}, u32[]{:S(2)}) collective-permute-start(bf16[272,128]{1,0:T(8,128)(2,1)} %get-tuple-element.33), channel_id=1, source_target_pairs={{0,16},{4,20},{8,24},{12,28},{16,0},{20,4},{24,8},{28,12},{1,17},{... | collective-permute-start | bytes 208904 | tf_op jit(solution)/shard_map/ppermute | solution.py:182
  15.1 12.2 %collective-permute-start.4 = (bf16[1296,128]{1,0:T(8,128)(2,1)S(1)}, bf16[1296,128]{1,0:T(8,128)(2,1)S(1)}, u32[]{:S(2)}, u32[]{:S(2)}) collective-permute-start(bf16[1296,128]{1,0:T(8,128)(2,1)S(1)} %collective-permute-done.1.refs_2_), channel_id=1, source_target_pairs={{0,4},{4,0},{8,12},{12,8},{16,20},{20,16},{24,28},{28,24},{1,5},{5... | collective-permute-start | bytes 995336 | tf_op jit(solution)/shard_map/ppermute | solution.py:182
  16.4 19.7 %collective-permute-start.7 = (bf16[1024,128]{1,0:T(8,128)(2,1)}, bf16[1024,128]{1,0:T(8,128)(2,1)S(1)}, u32[]{:S(2)}, u32[]{:S(2)}) collective-permute-start(bf16[1024,128]{1,0:T(8,128)(2,1)} %get-tuple-element.41), channel_id=1, source_target_pairs={{0,16},{4,20},{8,24},{12,28},{16,0},{20,4},{24,8},{28,12},{1,17},{... | collective-permute-start | bytes 786440 | tf_op jit(solution)/shard_map/ppermute | solution.py:182
  16.5 9.4 %collective-permute-start.5 = (bf16[272,128]{1,0:T(8,128)(2,1)S(1)}, bf16[272,128]{1,0:T(8,128)(2,1)S(1)}, u32[]{:S(2)}, u32[]{:S(2)}) collective-permute-start(bf16[272,128]{1,0:T(8,128)(2,1)S(1)} %collective-permute-done.2.refs_4_), channel_id=1, source_target_pairs={{0,8},{4,12},{8,0},{12,4},{16,24},{20,28},{24,16},{28,20},{1,9},{5... | collective-permute-start | bytes 208904 | tf_op jit(solution)/shard_map/ppermute | solution.py:182
  18.8 8.5 %collective-permute-start.6 = (bf16[272,128]{1,0:T(8,128)(2,1)S(1)}, bf16[272,128]{1,0:T(8,128)(2,1)S(1)}, u32[]{:S(2)}, u32[]{:S(2)}) collective-permute-start(bf16[272,128]{1,0:T(8,128)(2,1)S(1)} %collective-permute-done.3.refs_5_), channel_id=1, source_target_pairs={{0,8},{4,12},{8,0},{12,4},{16,24},{20,28},{24,16},{28,20},{1,9},{5... | collective-permute-start | bytes 208904 | tf_op jit(solution)/shard_map/ppermute | solution.py:182
  27.3 1.0 %copy-start = (bf16[1296,128]{1,0:T(8,128)(2,1)S(1)}, bf16[1296,128]{1,0:T(8,128)(2,1)}, u32[]{:S(2)}) copy-start(bf16[1296,128]{1,0:T(8,128)(2,1)} %get-tuple-element.34.refs_0_) | copy-start | bytes 995332
  36.0 5.9 %collective-permute-start.10 = (bf16[1024,128]{1,0:T(8,128)(2,1)S(1)}, bf16[1024,128]{1,0:T(8,128)(2,1)S(1)}, u32[]{:S(2)}, u32[]{:S(2)}) collective-permute-start(bf16[1024,128]{1,0:T(8,128)(2,1)S(1)} %collective-permute-done.7.refs_8_), channel_id=1, source_target_pairs={{0,8},{4,12},{8,0},{12,4},{16,24},{20,28},{24,16},{28,20},{1,9},{5... | collective-permute-start | bytes 786440 | tf_op jit(solution)/shard_map/ppermute | solution.py:182
  36.1 5.9 %collective-permute-start.9 = (bf16[1024,128]{1,0:T(8,128)(2,1)S(1)}, bf16[1024,128]{1,0:T(8,128)(2,1)S(1)}, u32[]{:S(2)}, u32[]{:S(2)}) collective-permute-start(bf16[1024,128]{1,0:T(8,128)(2,1)S(1)} %collective-permute-done.7.refs_8_), channel_id=1, source_target_pairs={{0,4},{4,0},{8,12},{12,8},{16,20},{20,16},{24,28},{28,24},{1,5},{5... | collective-permute-start | bytes 786440 | tf_op jit(solution)/shard_map/ppermute | solution.py:182
  36.4 17.2 %collective-permute-start.8 = (bf16[256,1024]{1,0:T(8,128)(2,1)S(1)}, bf16[256,1024]{1,0:T(8,128)(2,1)S(1)}, u32[]{:S(2)}, u32[]{:S(2)}) collective-permute-start(bf16[256,1024]{1,0:T(8,128)(2,1)S(1)} %get-tuple-element.42), channel_id=1, source_target_pairs={{0,1},{1,0},{2,3},{3,2},{4,5},{5,4},{6,7},{7,6},{8,9},{9,8},{10,11... | collective-permute-start | bytes 1572872 | tf_op jit(solution)/shard_map/ppermute | solution.py:270
  40.8 13.8 %copy-start.1 = (bf16[1024,1024]{1,0:T(8,128)(2,1)S(1)}, bf16[1024,1024]{1,0:T(8,128)(2,1)}, u32[]{:S(2)}) copy-start(bf16[1024,1024]{1,0:T(8,128)(2,1)} %refs_8_.1) | copy-start | bytes 6291460
  42.0 6.4 %collective-permute-start.13 = (bf16[1024,128]{1,0:T(8,128)(2,1)S(1)}, bf16[1024,128]{1,0:T(8,128)(2,1)S(1)}, u32[]{:S(2)}, u32[]{:S(2)}) collective-permute-start(bf16[1024,128]{1,0:T(8,128)(2,1)S(1)} %collective-permute-done.10.refs_9_), channel_id=1, source_target_pairs={{0,4},{4,0},{8,12},{12,8},{16,20},{20,16},{24,28},{28,24},{1,5},{5... | collective-permute-start | bytes 786440 | tf_op jit(solution)/shard_map/ppermute | solution.py:182
  45.0 8.6 %collective-permute-start.12 = (bf16[128,1024]{1,0:T(8,128)(2,1)S(1)}, bf16[128,1024]{1,0:T(8,128)(2,1)S(1)}, u32[]{:S(2)}, u32[]{:S(2)}) collective-permute-start(bf16[128,1024]{1,0:T(8,128)(2,1)S(1)} %get-tuple-element.52), channel_id=1, source_target_pairs={{0,1},{1,0},{2,3},{3,2},{4,5},{5,4},{6,7},{7,6},{8,9},{9,8},{10,11... | collective-permute-start | bytes 786440 | tf_op jit(solution)/shard_map/ppermute | solution.py:270
  48.3 5.3 %collective-permute-start.11 = (bf16[64,1024]{1,0:T(8,128)(2,1)S(1)}, bf16[64,1024]{1,0:T(8,128)(2,1)S(1)}, u32[]{:S(2)}, u32[]{:S(2)}) collective-permute-start(bf16[64,1024]{1,0:T(8,128)(2,1)S(1)} %get-tuple-element.48), channel_id=1, source_target_pairs={{0,1},{1,0},{2,3},{3,2},{4,5},{5,4},{6,7},{7,6},{8,9},{9,8},{10,11... | collective-permute-start | bytes 393224 | tf_op jit(solution)/shard_map/ppermute | solution.py:270
  50.7 3.9 %collective-permute-start.14 = (bf16[64,1024]{1,0:T(8,128)(2,1)S(1)}, bf16[64,1024]{1,0:T(8,128)(2,1)S(1)}, u32[]{:S(2)}, u32[]{:S(2)}) collective-permute-start(bf16[64,1024]{1,0:T(8,128)(2,1)S(1)} %get-tuple-element.54), channel_id=1, source_target_pairs={{0,1},{1,0},{2,3},{3,2},{4,5},{5,4},{6,7},{7,6},{8,9},{9,8},{10,11... | collective-permute-start | bytes 393224 | tf_op jit(solution)/shard_map/ppermute | solution.py:270
  57.1 22.4 %collective-permute-start.16 = (bf16[128,1024]{1,0:T(8,128)(2,1)S(1)}, bf16[128,1024]{1,0:T(8,128)(2,1)S(1)}, u32[]{:S(2)}, u32[]{:S(2)}) collective-permute-start(bf16[128,1024]{1,0:T(8,128)(2,1)S(1)} %get-tuple-element.55), channel_id=1, source_target_pairs={{0,0},{1,4},{2,8},{3,12},{4,16},{5,20},{6,24},{7,28},{8,1},{9,5},{... | collective-permute-start | bytes 786440 | tf_op jit(solution)/shard_map/ppermute | solution.py:290
  59.7 25.9 %collective-permute-start.17 = (bf16[128,1024]{1,0:T(8,128)(2,1)S(1)}, bf16[128,1024]{1,0:T(8,128)(2,1)S(1)}, u32[]{:S(2)}, u32[]{:S(2)}) collective-permute-start(bf16[128,1024]{1,0:T(8,128)(2,1)S(1)} %get-tuple-element.56), channel_id=1, source_target_pairs={{0,8},{1,12},{2,0},{3,4},{4,24},{5,28},{6,16},{7,20},{8,9},{9,13},... | collective-permute-start | bytes 786440 | tf_op jit(solution)/shard_map/ppermute | solution.py:290
  63.5 22.1 %collective-permute-start.18 = (bf16[128,1024]{1,0:T(8,128)(2,1)S(1)}, bf16[128,1024]{1,0:T(8,128)(2,1)S(1)}, u32[]{:S(2)}, u32[]{:S(2)}) collective-permute-start(bf16[128,1024]{1,0:T(8,128)(2,1)S(1)} %get-tuple-element.57), channel_id=1, source_target_pairs={{0,16},{1,20},{2,24},{3,28},{4,0},{5,4},{6,8},{7,12},{8,17},{9,21}... | collective-permute-start | bytes 786440 | tf_op jit(solution)/shard_map/ppermute | solution.py:290
  63.5 23.6 %collective-permute-start.19 = (bf16[128,1024]{1,0:T(8,128)(2,1)S(1)}, bf16[128,1024]{1,0:T(8,128)(2,1)S(1)}, u32[]{:S(2)}, u32[]{:S(2)}) collective-permute-start(bf16[128,1024]{1,0:T(8,128)(2,1)S(1)} %get-tuple-element.58), channel_id=1, source_target_pairs={{0,24},{1,28},{2,16},{3,20},{4,8},{5,12},{6,0},{7,4},{8,25},{9,29}... | collective-permute-start | bytes 786440 | tf_op jit(solution)/shard_map/ppermute | solution.py:290

commit v5 on v4

--- a/solution.py
+++ b/solution.py
@@ -141,6 +141,10 @@
         copy.wait()
 
 
+def turn_of(plane, count):
+    return (1 - (plane ^ (plane >> 1)) % 2) * (count - 1)
+
+
 def project_kernel(group, half, parts, groups_of_slots, *refs):
     halves, refs = refs[: 2 * len(groups_of_slots)], refs[2 * len(groups_of_slots) :]
     w_ref, w_pair_ref, refs = refs[0], refs[1], refs[2:]
@@ -161,6 +165,7 @@
         x_got[...], w_pair_ref[...], preferred_element_type=jnp.float32
     )
     mine = lax.rem(me, group) * half + lax.div(lax.axis_index("head"), 2)
+    mine = jnp.bitwise_xor(mine, turn_of(lax.div(me, group), count))
     for k, out_ref in enumerate(out_refs):
         at = pl.ds(pl.multiple_of(jnp.bitwise_xor(mine, k) * rows, rows), rows)
         out_ref[...] = total[at, :].astype(jnp.bfloat16)
@@ -170,6 +175,7 @@
     blocks, out_ref = refs[:-1], refs[-1]
     cols = blocks[0].shape[1]
     high = lax.div(lax.axis_index("ctx"), 2)
+    high = jnp.bitwise_xor(high, turn_of(lax.axis_index("head"), len(blocks)))
     for first in range(0, len(blocks), half):
         part = lax.div(jnp.bitwise_xor(high, first), half)
         total = blocks[first][...].astype(jnp.float32)
@@ -285,7 +291,7 @@
         pairs = []
         for c in range(parts):
             for g in range(groups):
-                high = ((c % group) * half + g // 2) ^ k
+                high = ((c % group) * half + g // 2) ^ k ^ turn_of(c // group, count)
                 pairs.append((c * groups + g, (high * 2 + g % 2) * groups + c // group))
         arrived.append(lax.ppermute(sums[k], ("ctx", "head"), pairs))
     return pl.pallas_call(

time: 87.8 us -> 84.3 us (0.960)
  starting transfers between devices: 28.4 us -> 24.8 us
  Pallas kernels: 20.3 us -> 19.3 us
    ppermute x4, starting transfers between devices: 9.96 us -> 6.33 us  [packed_body(): arrived.append(lax.ppermute(sums[k], ('ctx', 'head'), pairs))]
    pallas_call x4, Pallas kernels: 15 us -> 13.9 us  [packed_body(): pl.pallas_call(functools.partial(attend_kernel, parts, heads, 1.0 / math....]
where the time goes in v5:
time: 84.3 us; the launch traced here: 83.9 us
  waiting for transfers between devices  38.8 us (46%)
  starting transfers between devices  24.8 us (29%)
  Pallas kernels  19.3 us (23%)
  local copies, waits for them, and re-layouts  0.98 us (1%)
    ppermute x4, waiting for transfers between devices, packed_body(): arrived.append(lax.ppermute(sums[k], ('ctx', 'head'), pairs))  20.6 us
    ppermute x11, waiting for transfers between devices, along_ctx(): return lax.ppermute(x, 'ctx', [(i, i ^ k) for i in range(parts)])  17.2 us
    pallas_call x4, Pallas kernels, packed_body(): pl.pallas_call(functools.partial(attend_kernel, parts, heads, 1.0 / math....  13.9 us
    ppermute x11, starting transfers between devices, along_ctx(): return lax.ppermute(x, 'ctx', [(i, i ^ k) for i in range(parts)])  9.19 us
    ppermute x4, starting transfers between devices, packed_body(): halves += [keep, lax.ppermute(send, 'head', pair)]  8.56 us
    ppermute x4, starting transfers between devices, packed_body(): arrived.append(lax.ppermute(sums[k], ('ctx', 'head'), pairs))  6.33 us
    pallas_call x1, Pallas kernels, packed_body(): pl.pallas_call(functools.partial(project_kernel, group, half, parts, slot...  2.51 us
    pallas_call x1, Pallas kernels, packed_body(): pl.pallas_call(functools.partial(pack_kernel, parts, heads), out_shape=[j...  1.92 us
  transfers between devices with their start and end apart: 20, of which 10 were waited for; matrix products, arithmetic and copies ran while one was open for 0% of the time, Pallas kernels for 19%

profile of v5, /device:TPU:17, one launch (start us, length us, event | category | flops | bytes accessed | tf_op | source)
XLA Modules:
  0.0 83.9 jit_solution(13892075107300444605)
XLA Ops:
  0.0 0.7 collective-permute-start.15
  0.7 1.9 %pack.1 = (bf16[1296,128]{1,0:T(8,128)(2,1)}, bf16[1024,128]{1,0:T(8,128)(2,1)}, bf16[272,128]{1,0:T(8,128)(2,1)}) custom-call(s32[1,8]{1,0:T(1,128)} %plan_ref.1, bf16[128,1024]{1,0:T(8,128)(2,1)} %q_ref.1, bf16[128,128]{1,0:T(8,128)(2,1)} %k_ref.1, bf16[128,128]{1,0:T(8,128)(2,1)} %v_ref.1, s32[1,128]{1,0:T(1,128)} %bitcast.1), custom_call_target="tpu_custom_call" | custom-call | tf_op jit(solution)/shard_map/pack/pallas_call | solution.py:231
  2.6 1.3 %collective-permute-start.1 = (bf16[1296,128]{1,0:T(8,128)(2,1)}, bf16[1296,128]{1,0:T(8,128)(2,1)S(1)}, u32[]{:S(2)}, u32[]{:S(2)}) collective-permute-start(bf16[1296,128]{1,0:T(8,128)(2,1)} %get-tuple-element.34.refs_0_), channel_id=1, source_target_pairs={{0,8},{4,12},{8,0},{12,4},{16,24},{20,28},{24,16},{28,20},{1,9},{5... | collective-permute-start | bytes 995336 | tf_op jit(solution)/shard_map/ppermute | solution.py:188
  3.9 1.2 %collective-permute-start = (bf16[1296,128]{1,0:T(8,128)(2,1)}, bf16[1296,128]{1,0:T(8,128)(2,1)S(1)}, u32[]{:S(2)}, u32[]{:S(2)}) collective-permute-start(bf16[1296,128]{1,0:T(8,128)(2,1)} %get-tuple-element.34.refs_0_), channel_id=1, source_target_pairs={{0,4},{4,0},{8,12},{12,8},{16,20},{20,16},{24,28},{28,24},{1,5},{5... | collective-permute-start | bytes 995336 | tf_op jit(solution)/shard_map/ppermute | solution.py:188
  5.1 0.0 collective-permute-start.3
  5.1 2.3 %collective-permute-start.2 = (bf16[272,128]{1,0:T(8,128)(2,1)}, bf16[272,128]{1,0:T(8,128)(2,1)S(1)}, u32[]{:S(2)}, u32[]{:S(2)}) collective-permute-start(bf16[272,128]{1,0:T(8,128)(2,1)} %get-tuple-element.33), channel_id=1, source_target_pairs={{0,16},{4,20},{8,24},{12,28},{16,0},{20,4},{24,8},{28,12},{1,17},{... | collective-permute-start | bytes 208904 | tf_op jit(solution)/shard_map/ppermute | solution.py:188
  7.4 7.1 %collective-permute-done.3.refs_5_ = bf16[272,128]{1,0:T(8,128)(2,1)S(1)} collective-permute-done((bf16[272,128]{1,0:T(8,128)(2,1)}, bf16[272,128]{1,0:T(8,128)(2,1)S(1)}, u32[]{:S(2)}, u32[]{:S(2)}) %collective-permute-start.3) | collective-permute-done | bytes 69664 | tf_op jit(solution)/shard_map/ppermute | solution.py:188
  14.6 0.5 collective-permute-done.2.refs_4_
  15.1 0.0 collective-permute-done.1.refs_2_
  15.1 0.0 collective-permute-done.refs_1_
  15.1 1.2 %collective-permute-start.4 = (bf16[1296,128]{1,0:T(8,128)(2,1)S(1)}, bf16[1296,128]{1,0:T(8,128)(2,1)S(1)}, u32[]{:S(2)}, u32[]{:S(2)}) collective-permute-start(bf16[1296,128]{1,0:T(8,128)(2,1)S(1)} %collective-permute-done.1.refs_2_), channel_id=1, source_target_pairs={{0,4},{4,0},{8,12},{12,8},{16,20},{20,16},{24,28},{28,24},{1,5},{5... | collective-permute-start | bytes 995336 | tf_op jit(solution)/shard_map/ppermute | solution.py:188
  16.4 0.2 collective-permute-start.7
  16.5 2.3 %collective-permute-start.5 = (bf16[272,128]{1,0:T(8,128)(2,1)S(1)}, bf16[272,128]{1,0:T(8,128)(2,1)S(1)}, u32[]{:S(2)}, u32[]{:S(2)}) collective-permute-start(bf16[272,128]{1,0:T(8,128)(2,1)S(1)} %collective-permute-done.2.refs_4_), channel_id=1, source_target_pairs={{0,8},{4,12},{8,0},{12,4},{16,24},{20,28},{24,16},{28,20},{1,9},{5... | collective-permute-start | bytes 208904 | tf_op jit(solution)/shard_map/ppermute | solution.py:188
  18.8 0.0 collective-permute-start.6
  18.9 7.0 %collective-permute-done.5.refs_6_ = bf16[272,128]{1,0:T(8,128)(2,1)S(1)} collective-permute-done((bf16[272,128]{1,0:T(8,128)(2,1)S(1)}, bf16[272,128]{1,0:T(8,128)(2,1)S(1)}, u32[]{:S(2)}, u32[]{:S(2)}) %collective-permute-start.5) | collective-permute-done | bytes 69664 | tf_op jit(solution)/shard_map/ppermute | solution.py:188
  25.9 1.4 %collective-permute-done.6.refs_7_ = bf16[272,128]{1,0:T(8,128)(2,1)S(1)} collective-permute-done((bf16[272,128]{1,0:T(8,128)(2,1)S(1)}, bf16[272,128]{1,0:T(8,128)(2,1)S(1)}, u32[]{:S(2)}, u32[]{:S(2)}) %collective-permute-start.6) | collective-permute-done | bytes 69664 | tf_op jit(solution)/shard_map/ppermute | solution.py:188
  27.3 0.0 collective-permute-done.4.refs_3_
  27.3 1.0 %copy-done = bf16[1296,128]{1,0:T(8,128)(2,1)S(1)} copy-done((bf16[1296,128]{1,0:T(8,128)(2,1)S(1)}, bf16[1296,128]{1,0:T(8,128)(2,1)}, u32[]{:S(2)}) %copy-start) | copy-done | bytes 331800
  28.3 6.7 %attend.4 = (bf16[256,1024]{1,0:T(8,128)(2,1)S(1)}, bf16[256,1024]{1,0:T(8,128)(2,1)S(1)}) custom-call(bf16[1296,128]{1,0:T(8,128)(2,1)S(1)} %copy-done, bf16[1296,128]{1,0:T(8,128)(2,1)S(1)} %collective-permute-done.refs_1_, bf16[1296,128]{1,0:T(8,128)(2,1)S(1)} %collective-permute-done.1.refs_2_, bf16[1296,128]{1,0:T(8,128)(2,1)S(1)} %collective-permute-done.4.refs_3_, ...), custom_call_target="tpu_custom_call" | custom-call | tf_op jit(solution)/shard_map/attend/pallas_call | solution.py:254
  35.0 0.0 collective-permute-done.7.refs_8_
  35.0 0.1 collective-permute-start.10
  35.1 0.3 collective-permute-start.9
  35.4 2.3 %collective-permute-start.8 = (bf16[256,1024]{1,0:T(8,128)(2,1)S(1)}, bf16[256,1024]{1,0:T(8,128)(2,1)S(1)}, u32[]{:S(2)}, u32[]{:S(2)}) collective-permute-start(bf16[256,1024]{1,0:T(8,128)(2,1)S(1)} %get-tuple-element.42), channel_id=1, source_target_pairs={{0,1},{1,0},{2,3},{3,2},{4,5},{5,4},{6,7},{7,6},{8,9},{9,8},{10,11... | collective-permute-start | bytes 1572872 | tf_op jit(solution)/shard_map/ppermute | solution.py:276
  37.6 2.1 %attend.5 = (bf16[64,1024]{1,0:T(8,128)(2,1)S(1)}, bf16[64,1024]{1,0:T(8,128)(2,1)S(1)}) custom-call(bf16[1296,128]{1,0:T(8,128)(2,1)S(1)} %copy-done, bf16[1296,128]{1,0:T(8,128)(2,1)S(1)} %collective-permute-done.refs_1_, bf16[1296,128]{1,0:T(8,128)(2,1)S(1)} %collective-permute-done.1.refs_2_, bf16[1296,128]{1,0:T(8,128)(2,1)S(1)} %collective-permute-done.4.refs_3_, ...), custom_call_target="tpu_custom_call" | custom-call | tf_op jit(solution)/shard_map/attend/pallas_call | solution.py:254
  39.8 0.0 copy-start.1
  39.8 1.0 %collective-permute-done.10.refs_9_ = bf16[1024,128]{1,0:T(8,128)(2,1)S(1)} collective-permute-done((bf16[1024,128]{1,0:T(8,128)(2,1)S(1)}, bf16[1024,128]{1,0:T(8,128)(2,1)S(1)}, u32[]{:S(2)}, u32[]{:S(2)}) %collective-permute-start.10) | collective-permute-done | bytes 262176 | tf_op jit(solution)/shard_map/ppermute | solution.py:188
  40.8 0.1 collective-permute-done.9.refs_8_
  40.9 0.2 collective-permute-start.13
  41.1 2.8 %attend.6 = (bf16[128,1024]{1,0:T(8,128)(2,1)S(1)}, bf16[128,1024]{1,0:T(8,128)(2,1)S(1)}) custom-call(bf16[1296,128]{1,0:T(8,128)(2,1)S(1)} %copy-done, bf16[1296,128]{1,0:T(8,128)(2,1)S(1)} %collective-permute-done.refs_1_, bf16[1296,128]{1,0:T(8,128)(2,1)S(1)} %collective-permute-done.1.refs_2_, bf16[1296,128]{1,0:T(8,128)(2,1)S(1)} %collective-permute-done.4.refs_3_, ...), custom_call_target="tpu_custom_call" | custom-call | tf_op jit(solution)/shard_map/attend/pallas_call | solution.py:254
  44.0 3.3 %collective-permute-start.12 = (bf16[128,1024]{1,0:T(8,128)(2,1)S(1)}, bf16[128,1024]{1,0:T(8,128)(2,1)S(1)}, u32[]{:S(2)}, u32[]{:S(2)}) collective-permute-start(bf16[128,1024]{1,0:T(8,128)(2,1)S(1)} %get-tuple-element.52), channel_id=1, source_target_pairs={{0,1},{1,0},{2,3},{3,2},{4,5},{5,4},{6,7},{7,6},{8,9},{9,8},{10,11... | collective-permute-start | bytes 786440 | tf_op jit(solution)/shard_map/ppermute | solution.py:276
  47.3 0.1 collective-permute-start.11
  47.4 0.0 collective-permute-done.13.refs_8_
  47.4 2.3 %attend.7 = (bf16[64,1024]{1,0:T(8,128)(2,1)S(1)}, bf16[64,1024]{1,0:T(8,128)(2,1)S(1)}) custom-call(bf16[1296,128]{1,0:T(8,128)(2,1)S(1)} %copy-done, bf16[1296,128]{1,0:T(8,128)(2,1)S(1)} %collective-permute-done.refs_1_, bf16[1296,128]{1,0:T(8,128)(2,1)S(1)} %collective-permute-done.1.refs_2_, bf16[1296,128]{1,0:T(8,128)(2,1)S(1)} %collective-permute-done.4.refs_3_, ...), custom_call_target="tpu_custom_call" | custom-call | tf_op jit(solution)/shard_map/attend/pallas_call | solution.py:254
  49.7 2.9 %collective-permute-start.14 = (bf16[64,1024]{1,0:T(8,128)(2,1)S(1)}, bf16[64,1024]{1,0:T(8,128)(2,1)S(1)}, u32[]{:S(2)}, u32[]{:S(2)}) collective-permute-start(bf16[64,1024]{1,0:T(8,128)(2,1)S(1)} %get-tuple-element.54), channel_id=1, source_target_pairs={{0,1},{1,0},{2,3},{3,2},{4,5},{5,4},{6,7},{7,6},{8,9},{9,8},{10,11... | collective-permute-start | bytes 393224 | tf_op jit(solution)/shard_map/ppermute | solution.py:276
  52.6 0.0 collective-permute-done.11.refs_3_
  52.6 0.0 collective-permute-done.12.refs_5_
  52.6 0.0 collective-permute-done.8.refs_1_
  52.6 1.0 %collective-permute-done.14.refs_7_ = bf16[64,1024]{1,0:T(8,128)(2,1)S(1)} collective-permute-done((bf16[64,1024]{1,0:T(8,128)(2,1)S(1)}, bf16[64,1024]{1,0:T(8,128)(2,1)S(1)}, u32[]{:S(2)}, u32[]{:S(2)}) %collective-permute-start.14) | collective-permute-done | bytes 131104 | tf_op jit(solution)/shard_map/ppermute | solution.py:276
  53.6 0.0 collective-permute-done.15.refs_9_
  53.6 2.5 %project.1 = (bf16[128,1024]{1,0:T(8,128)(2,1)S(1)}, bf16[128,1024]{1,0:T(8,128)(2,1)S(1)}, bf16[128,1024]{1,0:T(8,128)(2,1)S(1)}, bf16[128,1024]{1,0:T(8,128)(2,1)S(1)}) custom-call(bf16[256,1024]{1,0:T(8,128)(2,1)S(1)} %get-tuple-element.39.refs_0_, bf16[256,1024]{1,0:T(8,128)(2,1)S(1)} %collective-permute-done.8.refs_1_, ...), custom_call_target="tpu_custom_call" | custom-call | tf_op jit(solution)/shard_map/project/pallas_call | solution.py:277
  56.1 1.7 %collective-permute-start.16 = (bf16[128,1024]{1,0:T(8,128)(2,1)S(1)}, bf16[128,1024]{1,0:T(8,128)(2,1)S(1)}, u32[]{:S(2)}, u32[]{:S(2)}) collective-permute-start(bf16[128,1024]{1,0:T(8,128)(2,1)S(1)} %get-tuple-element.55), channel_id=1, source_target_pairs={{0,24},{1,28},{2,16},{3,20},{4,8},{5,12},{6,0},{7,4},{8,1},{9,5},{... | collective-permute-start | bytes 786440 | tf_op jit(solution)/shard_map/ppermute | solution.py:296
  57.8 2.7 %collective-permute-start.17 = (bf16[128,1024]{1,0:T(8,128)(2,1)S(1)}, bf16[128,1024]{1,0:T(8,128)(2,1)S(1)}, u32[]{:S(2)}, u32[]{:S(2)}) collective-permute-start(bf16[128,1024]{1,0:T(8,128)(2,1)S(1)} %get-tuple-element.56), channel_id=1, source_target_pairs={{0,16},{1,20},{2,24},{3,28},{4,0},{5,4},{6,8},{7,12},{8,9},{9,13},... | collective-permute-start | bytes 786440 | tf_op jit(solution)/shard_map/ppermute | solution.py:296
  60.5 0.0 collective-permute-start.18
  60.5 1.9 %collective-permute-start.19 = (bf16[128,1024]{1,0:T(8,128)(2,1)S(1)}, bf16[128,1024]{1,0:T(8,128)(2,1)S(1)}, u32[]{:S(2)}, u32[]{:S(2)}) collective-permute-start(bf16[128,1024]{1,0:T(8,128)(2,1)S(1)} %get-tuple-element.58), channel_id=1, source_target_pairs={{0,0},{1,4},{2,8},{3,12},{4,16},{5,20},{6,24},{7,28},{8,25},{9,29}... | collective-permute-start | bytes 786440 | tf_op jit(solution)/shard_map/ppermute | solution.py:296
  62.4 14.5 %collective-permute-done.16.refs_0_ = bf16[128,1024]{1,0:T(8,128)(2,1)S(1)} collective-permute-done((bf16[128,1024]{1,0:T(8,128)(2,1)S(1)}, bf16[128,1024]{1,0:T(8,128)(2,1)S(1)}, u32[]{:S(2)}, u32[]{:S(2)}) %collective-permute-start.16) | collective-permute-done | bytes 262176 | tf_op jit(solution)/shard_map/ppermute | solution.py:296
  77.0 5.8 %collective-permute-done.17.refs_1_ = bf16[128,1024]{1,0:T(8,128)(2,1)S(1)} collective-permute-done((bf16[128,1024]{1,0:T(8,128)(2,1)S(1)}, bf16[128,1024]{1,0:T(8,128)(2,1)S(1)}, u32[]{:S(2)}, u32[]{:S(2)}) %collective-permute-start.17) | collective-permute-done | bytes 262176 | tf_op jit(solution)/shard_map/ppermute | solution.py:296
  82.7 0.3 collective-permute-done.19.refs_3_
  83.0 0.9 %final_sum.1 = bf16[128,2048]{1,0:T(8,128)(2,1)} custom-call(bf16[128,1024]{1,0:T(8,128)(2,1)S(1)} %collective-permute-done.16.refs_0_, bf16[128,1024]{1,0:T(8,128)(2,1)S(1)} %collective-permute-done.17.refs_1_, bf16[128,1024]{1,0:T(8,128)(2,1)S(1)} %collective-permute-done.18.refs_2_, bf16[128,1024]{1,0:T(8,128)(2,1)S(1)} %collective-permute-done.19.refs_3_), custom_call_target="tpu_custom_call" | custom-call | tf_op jit(solution)/shard_map/final_sum/pallas_call | solution.py:297
  (3 shorter events, 0.0 us)
Async XLA Ops:
  0.0 53.6 %collective-permute-start.15 = (bf16[1024,1024]{1,0:T(8,128)(2,1)}, bf16[1024,1024]{1,0:T(8,128)(2,1)S(1)}, u32[]{:S(2)}, u32[]{:S(2)}) collective-permute-start(bf16[1024,1024]{1,0:T(8,128)(2,1)} %refs_8_.1), channel_id=1, source_target_pairs={{0,1},{1,0},{2,3},{3,2},{4,5},{5,4},{6,7},{7,6},{8,9},{9,8},{10,11... | collective-permute-start | bytes 6291464 | tf_op jit(solution)/shard_map/ppermute | solution.py:230
  2.6 12.5 %collective-permute-start.1 = (bf16[1296,128]{1,0:T(8,128)(2,1)}, bf16[1296,128]{1,0:T(8,128)(2,1)S(1)}, u32[]{:S(2)}, u32[]{:S(2)}) collective-permute-start(bf16[1296,128]{1,0:T(8,128)(2,1)} %get-tuple-element.34.refs_0_), channel_id=1, source_target_pairs={{0,8},{4,12},{8,0},{12,4},{16,24},{20,28},{24,16},{28,20},{1,9},{5... | collective-permute-start | bytes 995336 | tf_op jit(solution)/shard_map/ppermute | solution.py:188
  3.9 11.2 %collective-permute-start = (bf16[1296,128]{1,0:T(8,128)(2,1)}, bf16[1296,128]{1,0:T(8,128)(2,1)S(1)}, u32[]{:S(2)}, u32[]{:S(2)}) collective-permute-start(bf16[1296,128]{1,0:T(8,128)(2,1)} %get-tuple-element.34.refs_0_), channel_id=1, source_target_pairs={{0,4},{4,0},{8,12},{12,8},{16,20},{20,16},{24,28},{28,24},{1,5},{5... | collective-permute-start | bytes 995336 | tf_op jit(solution)/shard_map/ppermute | solution.py:188
  5.1 9.4 %collective-permute-start.3 = (bf16[272,128]{1,0:T(8,128)(2,1)}, bf16[272,128]{1,0:T(8,128)(2,1)S(1)}, u32[]{:S(2)}, u32[]{:S(2)}) collective-permute-start(bf16[272,128]{1,0:T(8,128)(2,1)} %get-tuple-element.33), channel_id=1, source_target_pairs={{0,20},{4,16},{8,28},{12,24},{16,4},{20,0},{24,12},{28,8},{1,21},{... | collective-permute-start | bytes 208904 | tf_op jit(solution)/shard_map/ppermute | solution.py:188
  5.1 10.0 %collective-permute-start.2 = (bf16[272,128]{1,0:T(8,128)(2,1)}, bf16[272,128]{1,0:T(8,128)(2,1)S(1)}, u32[]{:S(2)}, u32[]{:S(2)}) collective-permute-start(bf16[272,128]{1,0:T(8,128)(2,1)} %get-tuple-element.33), channel_id=1, source_target_pairs={{0,16},{4,20},{8,24},{12,28},{16,0},{20,4},{24,8},{28,12},{1,17},{... | collective-permute-start | bytes 208904 | tf_op jit(solution)/shard_map/ppermute | solution.py:188
  15.1 12.2 %collective-permute-start.4 = (bf16[1296,128]{1,0:T(8,128)(2,1)S(1)}, bf16[1296,128]{1,0:T(8,128)(2,1)S(1)}, u32[]{:S(2)}, u32[]{:S(2)}) collective-permute-start(bf16[1296,128]{1,0:T(8,128)(2,1)S(1)} %collective-permute-done.1.refs_2_), channel_id=1, source_target_pairs={{0,4},{4,0},{8,12},{12,8},{16,20},{20,16},{24,28},{28,24},{1,5},{5... | collective-permute-start | bytes 995336 | tf_op jit(solution)/shard_map/ppermute | solution.py:188
  16.4 18.6 %collective-permute-start.7 = (bf16[1024,128]{1,0:T(8,128)(2,1)}, bf16[1024,128]{1,0:T(8,128)(2,1)S(1)}, u32[]{:S(2)}, u32[]{:S(2)}) collective-permute-start(bf16[1024,128]{1,0:T(8,128)(2,1)} %get-tuple-element.41), channel_id=1, source_target_pairs={{0,16},{4,20},{8,24},{12,28},{16,0},{20,4},{24,8},{28,12},{1,17},{... | collective-permute-start | bytes 786440 | tf_op jit(solution)/shard_map/ppermute | solution.py:188
  16.5 9.4 %collective-permute-start.5 = (bf16[272,128]{1,0:T(8,128)(2,1)S(1)}, bf16[272,128]{1,0:T(8,128)(2,1)S(1)}, u32[]{:S(2)}, u32[]{:S(2)}) collective-permute-start(bf16[272,128]{1,0:T(8,128)(2,1)S(1)} %collective-permute-done.2.refs_4_), channel_id=1, source_target_pairs={{0,8},{4,12},{8,0},{12,4},{16,24},{20,28},{24,16},{28,20},{1,9},{5... | collective-permute-start | bytes 208904 | tf_op jit(solution)/shard_map/ppermute | solution.py:188
  18.8 8.5 %collective-permute-start.6 = (bf16[272,128]{1,0:T(8,128)(2,1)S(1)}, bf16[272,128]{1,0:T(8,128)(2,1)S(1)}, u32[]{:S(2)}, u32[]{:S(2)}) collective-permute-start(bf16[272,128]{1,0:T(8,128)(2,1)S(1)} %collective-permute-done.3.refs_5_), channel_id=1, source_target_pairs={{0,8},{4,12},{8,0},{12,4},{16,24},{20,28},{24,16},{28,20},{1,9},{5... | collective-permute-start | bytes 208904 | tf_op jit(solution)/shard_map/ppermute | solution.py:188
  27.3 1.0 %copy-start = (bf16[1296,128]{1,0:T(8,128)(2,1)S(1)}, bf16[1296,128]{1,0:T(8,128)(2,1)}, u32[]{:S(2)}) copy-start(bf16[1296,128]{1,0:T(8,128)(2,1)} %get-tuple-element.34.refs_0_) | copy-start | bytes 995332
  35.0 5.9 %collective-permute-start.10 = (bf16[1024,128]{1,0:T(8,128)(2,1)S(1)}, bf16[1024,128]{1,0:T(8,128)(2,1)S(1)}, u32[]{:S(2)}, u32[]{:S(2)}) collective-permute-start(bf16[1024,128]{1,0:T(8,128)(2,1)S(1)} %collective-permute-done.7.refs_8_), channel_id=1, source_target_pairs={{0,8},{4,12},{8,0},{12,4},{16,24},{20,28},{24,16},{28,20},{1,9},{5... | collective-permute-start | bytes 786440 | tf_op jit(solution)/shard_map/ppermute | solution.py:188
  35.1 5.9 %collective-permute-start.9 = (bf16[1024,128]{1,0:T(8,128)(2,1)S(1)}, bf16[1024,128]{1,0:T(8,128)(2,1)S(1)}, u32[]{:S(2)}, u32[]{:S(2)}) collective-permute-start(bf16[1024,128]{1,0:T(8,128)(2,1)S(1)} %collective-permute-done.7.refs_8_), channel_id=1, source_target_pairs={{0,4},{4,0},{8,12},{12,8},{16,20},{20,16},{24,28},{28,24},{1,5},{5... | collective-permute-start | bytes 786440 | tf_op jit(solution)/shard_map/ppermute | solution.py:188
  35.4 17.2 %collective-permute-start.8 = (bf16[256,1024]{1,0:T(8,128)(2,1)S(1)}, bf16[256,1024]{1,0:T(8,128)(2,1)S(1)}, u32[]{:S(2)}, u32[]{:S(2)}) collective-permute-start(bf16[256,1024]{1,0:T(8,128)(2,1)S(1)} %get-tuple-element.42), channel_id=1, source_target_pairs={{0,1},{1,0},{2,3},{3,2},{4,5},{5,4},{6,7},{7,6},{8,9},{9,8},{10,11... | collective-permute-start | bytes 1572872 | tf_op jit(solution)/shard_map/ppermute | solution.py:276
  39.8 13.8 %copy-start.1 = (bf16[1024,1024]{1,0:T(8,128)(2,1)S(1)}, bf16[1024,1024]{1,0:T(8,128)(2,1)}, u32[]{:S(2)}) copy-start(bf16[1024,1024]{1,0:T(8,128)(2,1)} %refs_8_.1) | copy-start | bytes 6291460
  40.9 6.4 %collective-permute-start.13 = (bf16[1024,128]{1,0:T(8,128)(2,1)S(1)}, bf16[1024,128]{1,0:T(8,128)(2,1)S(1)}, u32[]{:S(2)}, u32[]{:S(2)}) collective-permute-start(bf16[1024,128]{1,0:T(8,128)(2,1)S(1)} %collective-permute-done.10.refs_9_), channel_id=1, source_target_pairs={{0,4},{4,0},{8,12},{12,8},{16,20},{20,16},{24,28},{28,24},{1,5},{5... | collective-permute-start | bytes 786440 | tf_op jit(solution)/shard_map/ppermute | solution.py:188
  44.0 8.6 %collective-permute-start.12 = (bf16[128,1024]{1,0:T(8,128)(2,1)S(1)}, bf16[128,1024]{1,0:T(8,128)(2,1)S(1)}, u32[]{:S(2)}, u32[]{:S(2)}) collective-permute-start(bf16[128,1024]{1,0:T(8,128)(2,1)S(1)} %get-tuple-element.52), channel_id=1, source_target_pairs={{0,1},{1,0},{2,3},{3,2},{4,5},{5,4},{6,7},{7,6},{8,9},{9,8},{10,11... | collective-permute-start | bytes 786440 | tf_op jit(solution)/shard_map/ppermute | solution.py:276
  47.3 5.3 %collective-permute-start.11 = (bf16[64,1024]{1,0:T(8,128)(2,1)S(1)}, bf16[64,1024]{1,0:T(8,128)(2,1)S(1)}, u32[]{:S(2)}, u32[]{:S(2)}) collective-permute-start(bf16[64,1024]{1,0:T(8,128)(2,1)S(1)} %get-tuple-element.48), channel_id=1, source_target_pairs={{0,1},{1,0},{2,3},{3,2},{4,5},{5,4},{6,7},{7,6},{8,9},{9,8},{10,11... | collective-permute-start | bytes 393224 | tf_op jit(solution)/shard_map/ppermute | solution.py:276
  49.7 3.9 %collective-permute-start.14 = (bf16[64,1024]{1,0:T(8,128)(2,1)S(1)}, bf16[64,1024]{1,0:T(8,128)(2,1)S(1)}, u32[]{:S(2)}, u32[]{:S(2)}) collective-permute-start(bf16[64,1024]{1,0:T(8,128)(2,1)S(1)} %get-tuple-element.54), channel_id=1, source_target_pairs={{0,1},{1,0},{2,3},{3,2},{4,5},{5,4},{6,7},{7,6},{8,9},{9,8},{10,11... | collective-permute-start | bytes 393224 | tf_op jit(solution)/shard_map/ppermute | solution.py:276
  56.1 20.9 %collective-permute-start.16 = (bf16[128,1024]{1,0:T(8,128)(2,1)S(1)}, bf16[128,1024]{1,0:T(8,128)(2,1)S(1)}, u32[]{:S(2)}, u32[]{:S(2)}) collective-permute-start(bf16[128,1024]{1,0:T(8,128)(2,1)S(1)} %get-tuple-element.55), channel_id=1, source_target_pairs={{0,24},{1,28},{2,16},{3,20},{4,8},{5,12},{6,0},{7,4},{8,1},{9,5},{... | collective-permute-start | bytes 786440 | tf_op jit(solution)/shard_map/ppermute | solution.py:296
  57.8 24.9 %collective-permute-start.17 = (bf16[128,1024]{1,0:T(8,128)(2,1)S(1)}, bf16[128,1024]{1,0:T(8,128)(2,1)S(1)}, u32[]{:S(2)}, u32[]{:S(2)}) collective-permute-start(bf16[128,1024]{1,0:T(8,128)(2,1)S(1)} %get-tuple-element.56), channel_id=1, source_target_pairs={{0,16},{1,20},{2,24},{3,28},{4,0},{5,4},{6,8},{7,12},{8,9},{9,13},... | collective-permute-start | bytes 786440 | tf_op jit(solution)/shard_map/ppermute | solution.py:296
  60.5 22.2 %collective-permute-start.18 = (bf16[128,1024]{1,0:T(8,128)(2,1)S(1)}, bf16[128,1024]{1,0:T(8,128)(2,1)S(1)}, u32[]{:S(2)}, u32[]{:S(2)}) collective-permute-start(bf16[128,1024]{1,0:T(8,128)(2,1)S(1)} %get-tuple-element.57), channel_id=1, source_target_pairs={{0,8},{1,12},{2,0},{3,4},{4,24},{5,28},{6,16},{7,20},{8,17},{9,21}... | collective-permute-start | bytes 786440 | tf_op jit(solution)/shard_map/ppermute | solution.py:296
  60.5 22.5 %collective-permute-start.19 = (bf16[128,1024]{1,0:T(8,128)(2,1)S(1)}, bf16[128,1024]{1,0:T(8,128)(2,1)S(1)}, u32[]{:S(2)}, u32[]{:S(2)}) collective-permute-start(bf16[128,1024]{1,0:T(8,128)(2,1)S(1)} %get-tuple-element.58), channel_id=1, source_target_pairs={{0,0},{1,4},{2,8},{3,12},{4,16},{5,20},{6,24},{7,28},{8,25},{9,29}... | collective-permute-start | bytes 786440 | tf_op jit(solution)/shard_map/ppermute | solution.py:296

commit v6 on v5

--- a/solution.py
+++ b/solution.py
@@ -56,30 +56,17 @@
     q_blocks = [near[k] for k in slots if k < half]
     if not q_blocks:
         q_blocks, refs = refs[:many], refs[many:]
-    send_ref, keep_ref, q_held, kv_held, rows_ref, ends, sems = refs
+    send_ref, keep_ref, q_held, kv_held, rows_ref, ends = refs
     rows = q_held.shape[1] // heads
     piece = rows // parts
     me = lax.axis_index("ctx")
     other = 1 - lax.rem(lax.axis_index("head"), 2)
     q_rows = heads * rows
-    copies = [
-        pltpu.make_async_copy(
-            near[k].at[q_rows:], kv_held.at[jnp.bitwise_xor(me, k)], sems.at[half + k]
-        )
-        for k in range(half)
-    ] + [
-        pltpu.make_async_copy(
-            far[k], kv_held.at[jnp.bitwise_xor(me, half + k)], sems.at[2 * half + k]
-        )
-        for k in range(half)
-    ] + [
-        pltpu.make_async_copy(q_blocks[i].at[:q_rows], q_held.at[i], sems.at[i])
-        for i in range(many)
-    ]
-    for copy in copies:
-        copy.start()
-    for copy in copies:
-        copy.wait()
+    for k in range(half):
+        kv_held[jnp.bitwise_xor(me, k)] = near[k][q_rows:, :]
+        kv_held[jnp.bitwise_xor(me, half + k)] = far[k][...]
+    for i in range(many):
+        q_held[i] = q_blocks[i][:q_rows, :]
 
     def ids_of(block):
         return kv_held[block, 2 * rows :, :].astype(jnp.float32)
@@ -131,14 +118,8 @@
         return carry
 
     lax.fori_loop(0, many, one_block, 0)
-    out = [
-        pltpu.make_async_copy(rows_ref.at[0], send_ref, sems.at[0]),
-        pltpu.make_async_copy(rows_ref.at[1], keep_ref, sems.at[1]),
-    ]
-    for copy in out:
-        copy.start()
-    for copy in out:
-        copy.wait()
+    send_ref[...] = rows_ref[0]
+    keep_ref[...] = rows_ref[1]
 
 
 def turn_of(plane, count):
@@ -254,14 +235,13 @@
         send, keep = pl.pallas_call(
             functools.partial(attend_kernel, parts, heads, 1.0 / math.sqrt(HEAD_DIM), tuple(slots)),
             out_shape=[jax.ShapeDtypeStruct((out_rows, heads * HEAD_DIM), bf16)] * 2,
-            in_specs=[ANY] * len(inputs),
-            out_specs=[ANY, ANY],
+            in_specs=[VMEM] * len(inputs),
+            out_specs=[VMEM, VMEM],
             scratch_shapes=[
                 pltpu.VMEM((many, heads * rows, HEAD_DIM), bf16),
                 pltpu.VMEM((parts, kv_rows, HEAD_DIM), bf16),
                 pltpu.VMEM((2, out_rows, heads * HEAD_DIM), bf16),
                 pltpu.SMEM((2, parts), jnp.float32),
-                pltpu.SemaphoreType.DMA((count + parts,)),
             ],
             compiler_params=params,
             name="attend",

time: 84.3 us -> 82.2 us (0.975)
  Pallas kernels: 19.3 us -> 14.4 us
  starting transfers between devices: 24.8 us -> 26.5 us
    pallas_call x4, Pallas kernels: 13.9 us -> 9.05 us  [packed_body(): pl.pallas_call(functools.partial(attend_kernel, parts, heads, 1.0 / math....]
    ppermute x11, waiting for transfers between devices: 17.2 us -> 18.3 us  [along_ctx(): return lax.ppermute(x, 'ctx', [(i, i ^ k) for i in range(parts)])]
    ppermute x4, starting transfers between devices: 6.33 us -> 7.31 us  [packed_body(): arrived.append(lax.ppermute(sums[k], ('ctx', 'head'), pairs))]
    ppermute x4, waiting for transfers between devices: 20.6 us -> 19.7 us  [packed_body(): arrived.append(lax.ppermute(sums[k], ('ctx', 'head'), pairs))]
  transfers between devices with their start and end apart: 20 -> 20, of which waited for: 10 -> 10; matrix products, arithmetic and copies ran while one was open for 0% -> 0% of each run, Pallas kernels for 19% -> 14%
where the time goes in v6:
time: 82.2 us; the launch traced here: 81 us
  waiting for transfers between devices  39 us (47%)
  starting transfers between devices  26.5 us (32%)
  Pallas kernels  14.4 us (18%)
  local copies, waits for them, and re-layouts  0.98 us (1%)
    ppermute x4, waiting for transfers between devices, packed_body(): arrived.append(lax.ppermute(sums[k], ('ctx', 'head'), pairs))  19.7 us
    ppermute x11, waiting for transfers between devices, along_ctx(): return lax.ppermute(x, 'ctx', [(i, i ^ k) for i in range(parts)])  18.3 us
    ppermute x4, starting transfers between devices, packed_body(): halves += [keep, lax.ppermute(send, 'head', pair)]  9.37 us
    ppermute x11, starting transfers between devices, along_ctx(): return lax.ppermute(x, 'ctx', [(i, i ^ k) for i in range(parts)])  9.19 us
    pallas_call x4, Pallas kernels, packed_body(): pl.pallas_call(functools.partial(attend_kernel, parts, heads, 1.0 / math....  9.05 us
    ppermute x4, starting transfers between devices, packed_body(): arrived.append(lax.ppermute(sums[k], ('ctx', 'head'), pairs))  7.31 us
    pallas_call x1, Pallas kernels, packed_body(): pl.pallas_call(functools.partial(project_kernel, group, half, parts, slot...  2.51 us
    pallas_call x1, Pallas kernels, packed_body(): pl.pallas_call(functools.partial(pack_kernel, parts, heads), out_shape=[j...  1.92 us
  transfers between devices with their start and end apart: 20, of which 10 were waited for; matrix products, arithmetic and copies ran while one was open for 0% of the time, Pallas kernels for 14%

profile of v6, /device:TPU:17, one launch (start us, length us, event | category | flops | bytes accessed | tf_op | source)
XLA Modules:
  0.0 81.0 jit_solution(14743543036805020284)
XLA Ops:
  0.0 0.7 collective-permute-start.15
  0.7 1.9 %pack.1 = (bf16[1296,128]{1,0:T(8,128)(2,1)}, bf16[1024,128]{1,0:T(8,128)(2,1)}, bf16[272,128]{1,0:T(8,128)(2,1)}) custom-call(s32[1,8]{1,0:T(1,128)} %plan_ref.1, bf16[128,1024]{1,0:T(8,128)(2,1)} %q_ref.1, bf16[128,128]{1,0:T(8,128)(2,1)} %k_ref.1, bf16[128,128]{1,0:T(8,128)(2,1)} %v_ref.1, s32[1,128]{1,0:T(1,128)} %bitcast.1), custom_call_target="tpu_custom_call" | custom-call | tf_op jit(solution)/shard_map/pack/pallas_call | solution.py:212
  2.6 1.3 %collective-permute-start.1 = (bf16[1296,128]{1,0:T(8,128)(2,1)}, bf16[1296,128]{1,0:T(8,128)(2,1)S(1)}, u32[]{:S(2)}, u32[]{:S(2)}) collective-permute-start(bf16[1296,128]{1,0:T(8,128)(2,1)} %get-tuple-element.34.refs_0_), channel_id=1, source_target_pairs={{0,8},{4,12},{8,0},{12,4},{16,24},{20,28},{24,16},{28,20},{1,9},{5... | collective-permute-start | bytes 995336 | tf_op jit(solution)/shard_map/ppermute | solution.py:169
  3.9 1.2 %collective-permute-start = (bf16[1296,128]{1,0:T(8,128)(2,1)}, bf16[1296,128]{1,0:T(8,128)(2,1)S(1)}, u32[]{:S(2)}, u32[]{:S(2)}) collective-permute-start(bf16[1296,128]{1,0:T(8,128)(2,1)} %get-tuple-element.34.refs_0_), channel_id=1, source_target_pairs={{0,4},{4,0},{8,12},{12,8},{16,20},{20,16},{24,28},{28,24},{1,5},{5... | collective-permute-start | bytes 995336 | tf_op jit(solution)/shard_map/ppermute | solution.py:169
  5.1 0.0 collective-permute-start.3
  5.1 2.3 %collective-permute-start.2 = (bf16[272,128]{1,0:T(8,128)(2,1)}, bf16[272,128]{1,0:T(8,128)(2,1)S(1)}, u32[]{:S(2)}, u32[]{:S(2)}) collective-permute-start(bf16[272,128]{1,0:T(8,128)(2,1)} %get-tuple-element.33), channel_id=1, source_target_pairs={{0,16},{4,20},{8,24},{12,28},{16,0},{20,4},{24,8},{28,12},{1,17},{... | collective-permute-start | bytes 208904 | tf_op jit(solution)/shard_map/ppermute | solution.py:169
  7.4 7.1 %collective-permute-done.3.refs_5_ = bf16[272,128]{1,0:T(8,128)(2,1)S(1)} collective-permute-done((bf16[272,128]{1,0:T(8,128)(2,1)}, bf16[272,128]{1,0:T(8,128)(2,1)S(1)}, u32[]{:S(2)}, u32[]{:S(2)}) %collective-permute-start.3) | collective-permute-done | bytes 69664 | tf_op jit(solution)/shard_map/ppermute | solution.py:169
  14.6 0.5 collective-permute-done.2.refs_4_
  15.1 0.0 collective-permute-done.1.refs_2_
  15.1 0.0 collective-permute-done.refs_1_
  15.1 1.2 %collective-permute-start.4 = (bf16[1296,128]{1,0:T(8,128)(2,1)S(1)}, bf16[1296,128]{1,0:T(8,128)(2,1)S(1)}, u32[]{:S(2)}, u32[]{:S(2)}) collective-permute-start(bf16[1296,128]{1,0:T(8,128)(2,1)S(1)} %collective-permute-done.1.refs_2_), channel_id=1, source_target_pairs={{0,4},{4,0},{8,12},{12,8},{16,20},{20,16},{24,28},{28,24},{1,5},{5... | collective-permute-start | bytes 995336 | tf_op jit(solution)/shard_map/ppermute | solution.py:169
  16.4 0.2 collective-permute-start.7
  16.5 2.3 %collective-permute-start.5 = (bf16[272,128]{1,0:T(8,128)(2,1)S(1)}, bf16[272,128]{1,0:T(8,128)(2,1)S(1)}, u32[]{:S(2)}, u32[]{:S(2)}) collective-permute-start(bf16[272,128]{1,0:T(8,128)(2,1)S(1)} %collective-permute-done.2.refs_4_), channel_id=1, source_target_pairs={{0,8},{4,12},{8,0},{12,4},{16,24},{20,28},{24,16},{28,20},{1,9},{5... | collective-permute-start | bytes 208904 | tf_op jit(solution)/shard_map/ppermute | solution.py:169
  18.8 0.0 collective-permute-start.6
  18.9 7.0 %collective-permute-done.5.refs_6_ = bf16[272,128]{1,0:T(8,128)(2,1)S(1)} collective-permute-done((bf16[272,128]{1,0:T(8,128)(2,1)S(1)}, bf16[272,128]{1,0:T(8,128)(2,1)S(1)}, u32[]{:S(2)}, u32[]{:S(2)}) %collective-permute-start.5) | collective-permute-done | bytes 69664 | tf_op jit(solution)/shard_map/ppermute | solution.py:169
  25.9 1.4 %collective-permute-done.6.refs_7_ = bf16[272,128]{1,0:T(8,128)(2,1)S(1)} collective-permute-done((bf16[272,128]{1,0:T(8,128)(2,1)S(1)}, bf16[272,128]{1,0:T(8,128)(2,1)S(1)}, u32[]{:S(2)}, u32[]{:S(2)}) %collective-permute-start.6) | collective-permute-done | bytes 69664 | tf_op jit(solution)/shard_map/ppermute | solution.py:169
  27.3 0.0 collective-permute-done.4.refs_3_
  27.3 1.0 %copy-done = bf16[1296,128]{1,0:T(8,128)(2,1)S(1)} copy-done((bf16[1296,128]{1,0:T(8,128)(2,1)S(1)}, bf16[1296,128]{1,0:T(8,128)(2,1)}, u32[]{:S(2)}) %copy-start) | copy-done | bytes 331800
  28.3 4.8 %attend.4 = (bf16[256,1024]{1,0:T(8,128)(2,1)S(1)}, bf16[256,1024]{1,0:T(8,128)(2,1)S(1)}) custom-call(bf16[1296,128]{1,0:T(8,128)(2,1)S(1)} %copy-done, bf16[1296,128]{1,0:T(8,128)(2,1)S(1)} %collective-permute-done.refs_1_, bf16[1296,128]{1,0:T(8,128)(2,1)S(1)} %collective-permute-done.1.refs_2_, bf16[1296,128]{1,0:T(8,128)(2,1)S(1)} %collective-permute-done.4.refs_3_, ...), custom_call_target="tpu_custom_call" | custom-call | tf_op jit(solution)/shard_map/attend/pallas_call | solution.py:235
  33.1 0.0 collective-permute-done.7.refs_8_
  33.1 0.1 collective-permute-start.10
  33.2 0.3 collective-permute-start.9
  33.5 2.3 %collective-permute-start.8 = (bf16[256,1024]{1,0:T(8,128)(2,1)S(1)}, bf16[256,1024]{1,0:T(8,128)(2,1)S(1)}, u32[]{:S(2)}, u32[]{:S(2)}) collective-permute-start(bf16[256,1024]{1,0:T(8,128)(2,1)S(1)} %get-tuple-element.42), channel_id=1, source_target_pairs={{0,1},{1,0},{2,3},{3,2},{4,5},{5,4},{6,7},{7,6},{8,9},{9,8},{10,11... | collective-permute-start | bytes 1572872 | tf_op jit(solution)/shard_map/ppermute | solution.py:256
  35.8 1.0 %attend.5 = (bf16[64,1024]{1,0:T(8,128)(2,1)S(1)}, bf16[64,1024]{1,0:T(8,128)(2,1)S(1)}) custom-call(bf16[1296,128]{1,0:T(8,128)(2,1)S(1)} %copy-done, bf16[1296,128]{1,0:T(8,128)(2,1)S(1)} %collective-permute-done.refs_1_, bf16[1296,128]{1,0:T(8,128)(2,1)S(1)} %collective-permute-done.1.refs_2_, bf16[1296,128]{1,0:T(8,128)(2,1)S(1)} %collective-permute-done.4.refs_3_, ...), custom_call_target="tpu_custom_call" | custom-call | tf_op jit(solution)/shard_map/attend/pallas_call | solution.py:235
  36.8 0.0 copy-start.1
  36.8 2.1 %collective-permute-done.10.refs_9_ = bf16[1024,128]{1,0:T(8,128)(2,1)S(1)} collective-permute-done((bf16[1024,128]{1,0:T(8,128)(2,1)S(1)}, bf16[1024,128]{1,0:T(8,128)(2,1)S(1)}, u32[]{:S(2)}, u32[]{:S(2)}) %collective-permute-start.10) | collective-permute-done | bytes 262176 | tf_op jit(solution)/shard_map/ppermute | solution.py:169
  39.0 0.1 collective-permute-done.9.refs_8_
  39.0 0.2 collective-permute-start.13
  39.3 2.0 %attend.6 = (bf16[128,1024]{1,0:T(8,128)(2,1)S(1)}, bf16[128,1024]{1,0:T(8,128)(2,1)S(1)}) custom-call(bf16[1296,128]{1,0:T(8,128)(2,1)S(1)} %copy-done, bf16[1296,128]{1,0:T(8,128)(2,1)S(1)} %collective-permute-done.refs_1_, bf16[1296,128]{1,0:T(8,128)(2,1)S(1)} %collective-permute-done.1.refs_2_, bf16[1296,128]{1,0:T(8,128)(2,1)S(1)} %collective-permute-done.4.refs_3_, ...), custom_call_target="tpu_custom_call" | custom-call | tf_op jit(solution)/shard_map/attend/pallas_call | solution.py:235
  41.3 3.3 %collective-permute-start.12 = (bf16[128,1024]{1,0:T(8,128)(2,1)S(1)}, bf16[128,1024]{1,0:T(8,128)(2,1)S(1)}, u32[]{:S(2)}, u32[]{:S(2)}) collective-permute-start(bf16[128,1024]{1,0:T(8,128)(2,1)S(1)} %get-tuple-element.52), channel_id=1, source_target_pairs={{0,1},{1,0},{2,3},{3,2},{4,5},{5,4},{6,7},{7,6},{8,9},{9,8},{10,11... | collective-permute-start | bytes 786440 | tf_op jit(solution)/shard_map/ppermute | solution.py:256
  44.6 0.1 collective-permute-start.11
  44.7 0.0 collective-permute-done.13.refs_8_
  44.7 1.2 %attend.7 = (bf16[64,1024]{1,0:T(8,128)(2,1)S(1)}, bf16[64,1024]{1,0:T(8,128)(2,1)S(1)}) custom-call(bf16[1296,128]{1,0:T(8,128)(2,1)S(1)} %copy-done, bf16[1296,128]{1,0:T(8,128)(2,1)S(1)} %collective-permute-done.refs_1_, bf16[1296,128]{1,0:T(8,128)(2,1)S(1)} %collective-permute-done.1.refs_2_, bf16[1296,128]{1,0:T(8,128)(2,1)S(1)} %collective-permute-done.4.refs_3_, ...), custom_call_target="tpu_custom_call" | custom-call | tf_op jit(solution)/shard_map/attend/pallas_call | solution.py:235
  45.9 3.7 %collective-permute-start.14 = (bf16[64,1024]{1,0:T(8,128)(2,1)S(1)}, bf16[64,1024]{1,0:T(8,128)(2,1)S(1)}, u32[]{:S(2)}, u32[]{:S(2)}) collective-permute-start(bf16[64,1024]{1,0:T(8,128)(2,1)S(1)} %get-tuple-element.54), channel_id=1, source_target_pairs={{0,1},{1,0},{2,3},{3,2},{4,5},{5,4},{6,7},{7,6},{8,9},{9,8},{10,11... | collective-permute-start | bytes 393224 | tf_op jit(solution)/shard_map/ppermute | solution.py:256
  49.6 0.0 collective-permute-done.11.refs_3_
  49.6 0.0 collective-permute-done.12.refs_5_
  49.6 0.0 collective-permute-done.8.refs_1_
  49.6 1.0 %collective-permute-done.14.refs_7_ = bf16[64,1024]{1,0:T(8,128)(2,1)S(1)} collective-permute-done((bf16[64,1024]{1,0:T(8,128)(2,1)S(1)}, bf16[64,1024]{1,0:T(8,128)(2,1)S(1)}, u32[]{:S(2)}, u32[]{:S(2)}) %collective-permute-start.14) | collective-permute-done | bytes 131104 | tf_op jit(solution)/shard_map/ppermute | solution.py:256
  50.6 0.0 collective-permute-done.15.refs_9_
  50.6 2.5 %project.1 = (bf16[128,1024]{1,0:T(8,128)(2,1)S(1)}, bf16[128,1024]{1,0:T(8,128)(2,1)S(1)}, bf16[128,1024]{1,0:T(8,128)(2,1)S(1)}, bf16[128,1024]{1,0:T(8,128)(2,1)S(1)}) custom-call(bf16[256,1024]{1,0:T(8,128)(2,1)S(1)} %get-tuple-element.39.refs_0_, bf16[256,1024]{1,0:T(8,128)(2,1)S(1)} %collective-permute-done.8.refs_1_, ...), custom_call_target="tpu_custom_call" | custom-call | tf_op jit(solution)/shard_map/project/pallas_call | solution.py:257
  53.1 1.3 %collective-permute-start.16 = (bf16[128,1024]{1,0:T(8,128)(2,1)S(1)}, bf16[128,1024]{1,0:T(8,128)(2,1)S(1)}, u32[]{:S(2)}, u32[]{:S(2)}) collective-permute-start(bf16[128,1024]{1,0:T(8,128)(2,1)S(1)} %get-tuple-element.55), channel_id=1, source_target_pairs={{0,24},{1,28},{2,16},{3,20},{4,8},{5,12},{6,0},{7,4},{8,1},{9,5},{... | collective-permute-start | bytes 786440 | tf_op jit(solution)/shard_map/ppermute | solution.py:276
  54.4 3.2 %collective-permute-start.17 = (bf16[128,1024]{1,0:T(8,128)(2,1)S(1)}, bf16[128,1024]{1,0:T(8,128)(2,1)S(1)}, u32[]{:S(2)}, u32[]{:S(2)}) collective-permute-start(bf16[128,1024]{1,0:T(8,128)(2,1)S(1)} %get-tuple-element.56), channel_id=1, source_target_pairs={{0,16},{1,20},{2,24},{3,28},{4,0},{5,4},{6,8},{7,12},{8,9},{9,13},... | collective-permute-start | bytes 786440 | tf_op jit(solution)/shard_map/ppermute | solution.py:276
  57.5 0.0 collective-permute-start.18
  57.5 2.9 %collective-permute-start.19 = (bf16[128,1024]{1,0:T(8,128)(2,1)S(1)}, bf16[128,1024]{1,0:T(8,128)(2,1)S(1)}, u32[]{:S(2)}, u32[]{:S(2)}) collective-permute-start(bf16[128,1024]{1,0:T(8,128)(2,1)S(1)} %get-tuple-element.58), channel_id=1, source_target_pairs={{0,0},{1,4},{2,8},{3,12},{4,16},{5,20},{6,24},{7,28},{8,25},{9,29}... | collective-permute-start | bytes 786440 | tf_op jit(solution)/shard_map/ppermute | solution.py:276
  60.4 13.5 %collective-permute-done.16.refs_0_ = bf16[128,1024]{1,0:T(8,128)(2,1)S(1)} collective-permute-done((bf16[128,1024]{1,0:T(8,128)(2,1)S(1)}, bf16[128,1024]{1,0:T(8,128)(2,1)S(1)}, u32[]{:S(2)}, u32[]{:S(2)}) %collective-permute-start.16) | collective-permute-done | bytes 262176 | tf_op jit(solution)/shard_map/ppermute | solution.py:276
  74.0 5.8 %collective-permute-done.17.refs_1_ = bf16[128,1024]{1,0:T(8,128)(2,1)S(1)} collective-permute-done((bf16[128,1024]{1,0:T(8,128)(2,1)S(1)}, bf16[128,1024]{1,0:T(8,128)(2,1)S(1)}, u32[]{:S(2)}, u32[]{:S(2)}) %collective-permute-start.17) | collective-permute-done | bytes 262176 | tf_op jit(solution)/shard_map/ppermute | solution.py:276
  79.8 0.3 collective-permute-done.19.refs_3_
  80.1 0.9 %final_sum.1 = bf16[128,2048]{1,0:T(8,128)(2,1)} custom-call(bf16[128,1024]{1,0:T(8,128)(2,1)S(1)} %collective-permute-done.16.refs_0_, bf16[128,1024]{1,0:T(8,128)(2,1)S(1)} %collective-permute-done.17.refs_1_, bf16[128,1024]{1,0:T(8,128)(2,1)S(1)} %collective-permute-done.18.refs_2_, bf16[128,1024]{1,0:T(8,128)(2,1)S(1)} %collective-permute-done.19.refs_3_), custom_call_target="tpu_custom_call" | custom-call | tf_op jit(solution)/shard_map/final_sum/pallas_call | solution.py:277
  (3 shorter events, 0.0 us)
Async XLA Ops:
  0.0 50.6 %collective-permute-start.15 = (bf16[1024,1024]{1,0:T(8,128)(2,1)}, bf16[1024,1024]{1,0:T(8,128)(2,1)S(1)}, u32[]{:S(2)}, u32[]{:S(2)}) collective-permute-start(bf16[1024,1024]{1,0:T(8,128)(2,1)} %refs_8_.1), channel_id=1, source_target_pairs={{0,1},{1,0},{2,3},{3,2},{4,5},{5,4},{6,7},{7,6},{8,9},{9,8},{10,11... | collective-permute-start | bytes 6291464 | tf_op jit(solution)/shard_map/ppermute | solution.py:211
  2.6 12.5 %collective-permute-start.1 = (bf16[1296,128]{1,0:T(8,128)(2,1)}, bf16[1296,128]{1,0:T(8,128)(2,1)S(1)}, u32[]{:S(2)}, u32[]{:S(2)}) collective-permute-start(bf16[1296,128]{1,0:T(8,128)(2,1)} %get-tuple-element.34.refs_0_), channel_id=1, source_target_pairs={{0,8},{4,12},{8,0},{12,4},{16,24},{20,28},{24,16},{28,20},{1,9},{5... | collective-permute-start | bytes 995336 | tf_op jit(solution)/shard_map/ppermute | solution.py:169
  3.9 11.2 %collective-permute-start = (bf16[1296,128]{1,0:T(8,128)(2,1)}, bf16[1296,128]{1,0:T(8,128)(2,1)S(1)}, u32[]{:S(2)}, u32[]{:S(2)}) collective-permute-start(bf16[1296,128]{1,0:T(8,128)(2,1)} %get-tuple-element.34.refs_0_), channel_id=1, source_target_pairs={{0,4},{4,0},{8,12},{12,8},{16,20},{20,16},{24,28},{28,24},{1,5},{5... | collective-permute-start | bytes 995336 | tf_op jit(solution)/shard_map/ppermute | solution.py:169
  5.1 9.4 %collective-permute-start.3 = (bf16[272,128]{1,0:T(8,128)(2,1)}, bf16[272,128]{1,0:T(8,128)(2,1)S(1)}, u32[]{:S(2)}, u32[]{:S(2)}) collective-permute-start(bf16[272,128]{1,0:T(8,128)(2,1)} %get-tuple-element.33), channel_id=1, source_target_pairs={{0,20},{4,16},{8,28},{12,24},{16,4},{20,0},{24,12},{28,8},{1,21},{... | collective-permute-start | bytes 208904 | tf_op jit(solution)/shard_map/ppermute | solution.py:169
  5.1 10.0 %collective-permute-start.2 = (bf16[272,128]{1,0:T(8,128)(2,1)}, bf16[272,128]{1,0:T(8,128)(2,1)S(1)}, u32[]{:S(2)}, u32[]{:S(2)}) collective-permute-start(bf16[272,128]{1,0:T(8,128)(2,1)} %get-tuple-element.33), channel_id=1, source_target_pairs={{0,16},{4,20},{8,24},{12,28},{16,0},{20,4},{24,8},{28,12},{1,17},{... | collective-permute-start | bytes 208904 | tf_op jit(solution)/shard_map/ppermute | solution.py:169
  15.1 12.2 %collective-permute-start.4 = (bf16[1296,128]{1,0:T(8,128)(2,1)S(1)}, bf16[1296,128]{1,0:T(8,128)(2,1)S(1)}, u32[]{:S(2)}, u32[]{:S(2)}) collective-permute-start(bf16[1296,128]{1,0:T(8,128)(2,1)S(1)} %collective-permute-done.1.refs_2_), channel_id=1, source_target_pairs={{0,4},{4,0},{8,12},{12,8},{16,20},{20,16},{24,28},{28,24},{1,5},{5... | collective-permute-start | bytes 995336 | tf_op jit(solution)/shard_map/ppermute | solution.py:169
  16.4 16.7 %collective-permute-start.7 = (bf16[1024,128]{1,0:T(8,128)(2,1)}, bf16[1024,128]{1,0:T(8,128)(2,1)S(1)}, u32[]{:S(2)}, u32[]{:S(2)}) collective-permute-start(bf16[1024,128]{1,0:T(8,128)(2,1)} %get-tuple-element.41), channel_id=1, source_target_pairs={{0,16},{4,20},{8,24},{12,28},{16,0},{20,4},{24,8},{28,12},{1,17},{... | collective-permute-start | bytes 786440 | tf_op jit(solution)/shard_map/ppermute | solution.py:169
  16.5 9.4 %collective-permute-start.5 = (bf16[272,128]{1,0:T(8,128)(2,1)S(1)}, bf16[272,128]{1,0:T(8,128)(2,1)S(1)}, u32[]{:S(2)}, u32[]{:S(2)}) collective-permute-start(bf16[272,128]{1,0:T(8,128)(2,1)S(1)} %collective-permute-done.2.refs_4_), channel_id=1, source_target_pairs={{0,8},{4,12},{8,0},{12,4},{16,24},{20,28},{24,16},{28,20},{1,9},{5... | collective-permute-start | bytes 208904 | tf_op jit(solution)/shard_map/ppermute | solution.py:169
  18.8 8.5 %collective-permute-start.6 = (bf16[272,128]{1,0:T(8,128)(2,1)S(1)}, bf16[272,128]{1,0:T(8,128)(2,1)S(1)}, u32[]{:S(2)}, u32[]{:S(2)}) collective-permute-start(bf16[272,128]{1,0:T(8,128)(2,1)S(1)} %collective-permute-done.3.refs_5_), channel_id=1, source_target_pairs={{0,8},{4,12},{8,0},{12,4},{16,24},{20,28},{24,16},{28,20},{1,9},{5... | collective-permute-start | bytes 208904 | tf_op jit(solution)/shard_map/ppermute | solution.py:169
  27.3 1.0 %copy-start = (bf16[1296,128]{1,0:T(8,128)(2,1)S(1)}, bf16[1296,128]{1,0:T(8,128)(2,1)}, u32[]{:S(2)}) copy-start(bf16[1296,128]{1,0:T(8,128)(2,1)} %get-tuple-element.34.refs_0_) | copy-start | bytes 995332
  33.1 5.9 %collective-permute-start.10 = (bf16[1024,128]{1,0:T(8,128)(2,1)S(1)}, bf16[1024,128]{1,0:T(8,128)(2,1)S(1)}, u32[]{:S(2)}, u32[]{:S(2)}) collective-permute-start(bf16[1024,128]{1,0:T(8,128)(2,1)S(1)} %collective-permute-done.7.refs_8_), channel_id=1, source_target_pairs={{0,8},{4,12},{8,0},{12,4},{16,24},{20,28},{24,16},{28,20},{1,9},{5... | collective-permute-start | bytes 786440 | tf_op jit(solution)/shard_map/ppermute | solution.py:169
  33.2 5.9 %collective-permute-start.9 = (bf16[1024,128]{1,0:T(8,128)(2,1)S(1)}, bf16[1024,128]{1,0:T(8,128)(2,1)S(1)}, u32[]{:S(2)}, u32[]{:S(2)}) collective-permute-start(bf16[1024,128]{1,0:T(8,128)(2,1)S(1)} %collective-permute-done.7.refs_8_), channel_id=1, source_target_pairs={{0,4},{4,0},{8,12},{12,8},{16,20},{20,16},{24,28},{28,24},{1,5},{5... | collective-permute-start | bytes 786440 | tf_op jit(solution)/shard_map/ppermute | solution.py:169
  33.5 16.1 %collective-permute-start.8 = (bf16[256,1024]{1,0:T(8,128)(2,1)S(1)}, bf16[256,1024]{1,0:T(8,128)(2,1)S(1)}, u32[]{:S(2)}, u32[]{:S(2)}) collective-permute-start(bf16[256,1024]{1,0:T(8,128)(2,1)S(1)} %get-tuple-element.42), channel_id=1, source_target_pairs={{0,1},{1,0},{2,3},{3,2},{4,5},{5,4},{6,7},{7,6},{8,9},{9,8},{10,11... | collective-permute-start | bytes 1572872 | tf_op jit(solution)/shard_map/ppermute | solution.py:256
  36.8 13.8 %copy-start.1 = (bf16[1024,1024]{1,0:T(8,128)(2,1)S(1)}, bf16[1024,1024]{1,0:T(8,128)(2,1)}, u32[]{:S(2)}) copy-start(bf16[1024,1024]{1,0:T(8,128)(2,1)} %refs_8_.1) | copy-start | bytes 6291460
  39.0 5.6 %collective-permute-start.13 = (bf16[1024,128]{1,0:T(8,128)(2,1)S(1)}, bf16[1024,128]{1,0:T(8,128)(2,1)S(1)}, u32[]{:S(2)}, u32[]{:S(2)}) collective-permute-start(bf16[1024,128]{1,0:T(8,128)(2,1)S(1)} %collective-permute-done.10.refs_9_), channel_id=1, source_target_pairs={{0,4},{4,0},{8,12},{12,8},{16,20},{20,16},{24,28},{28,24},{1,5},{5... | collective-permute-start | bytes 786440 | tf_op jit(solution)/shard_map/ppermute | solution.py:169
  41.3 8.3 %collective-permute-start.12 = (bf16[128,1024]{1,0:T(8,128)(2,1)S(1)}, bf16[128,1024]{1,0:T(8,128)(2,1)S(1)}, u32[]{:S(2)}, u32[]{:S(2)}) collective-permute-start(bf16[128,1024]{1,0:T(8,128)(2,1)S(1)} %get-tuple-element.52), channel_id=1, source_target_pairs={{0,1},{1,0},{2,3},{3,2},{4,5},{5,4},{6,7},{7,6},{8,9},{9,8},{10,11... | collective-permute-start | bytes 786440 | tf_op jit(solution)/shard_map/ppermute | solution.py:256
  44.6 5.0 %collective-permute-start.11 = (bf16[64,1024]{1,0:T(8,128)(2,1)S(1)}, bf16[64,1024]{1,0:T(8,128)(2,1)S(1)}, u32[]{:S(2)}, u32[]{:S(2)}) collective-permute-start(bf16[64,1024]{1,0:T(8,128)(2,1)S(1)} %get-tuple-element.48), channel_id=1, source_target_pairs={{0,1},{1,0},{2,3},{3,2},{4,5},{5,4},{6,7},{7,6},{8,9},{9,8},{10,11... | collective-permute-start | bytes 393224 | tf_op jit(solution)/shard_map/ppermute | solution.py:256
  45.9 4.7 %collective-permute-start.14 = (bf16[64,1024]{1,0:T(8,128)(2,1)S(1)}, bf16[64,1024]{1,0:T(8,128)(2,1)S(1)}, u32[]{:S(2)}, u32[]{:S(2)}) collective-permute-start(bf16[64,1024]{1,0:T(8,128)(2,1)S(1)} %get-tuple-element.54), channel_id=1, source_target_pairs={{0,1},{1,0},{2,3},{3,2},{4,5},{5,4},{6,7},{7,6},{8,9},{9,8},{10,11... | collective-permute-start | bytes 393224 | tf_op jit(solution)/shard_map/ppermute | solution.py:256
  53.1 20.9 %collective-permute-start.16 = (bf16[128,1024]{1,0:T(8,128)(2,1)S(1)}, bf16[128,1024]{1,0:T(8,128)(2,1)S(1)}, u32[]{:S(2)}, u32[]{:S(2)}) collective-permute-start(bf16[128,1024]{1,0:T(8,128)(2,1)S(1)} %get-tuple-element.55), channel_id=1, source_target_pairs={{0,24},{1,28},{2,16},{3,20},{4,8},{5,12},{6,0},{7,4},{8,1},{9,5},{... | collective-permute-start | bytes 786440 | tf_op jit(solution)/shard_map/ppermute | solution.py:276
  54.4 25.4 %collective-permute-start.17 = (bf16[128,1024]{1,0:T(8,128)(2,1)S(1)}, bf16[128,1024]{1,0:T(8,128)(2,1)S(1)}, u32[]{:S(2)}, u32[]{:S(2)}) collective-permute-start(bf16[128,1024]{1,0:T(8,128)(2,1)S(1)} %get-tuple-element.56), channel_id=1, source_target_pairs={{0,16},{1,20},{2,24},{3,28},{4,0},{5,4},{6,8},{7,12},{8,9},{9,13},... | collective-permute-start | bytes 786440 | tf_op jit(solution)/shard_map/ppermute | solution.py:276
  57.5 22.2 %collective-permute-start.18 = (bf16[128,1024]{1,0:T(8,128)(2,1)S(1)}, bf16[128,1024]{1,0:T(8,128)(2,1)S(1)}, u32[]{:S(2)}, u32[]{:S(2)}) collective-permute-start(bf16[128,1024]{1,0:T(8,128)(2,1)S(1)} %get-tuple-element.57), channel_id=1, source_target_pairs={{0,8},{1,12},{2,0},{3,4},{4,24},{5,28},{6,16},{7,20},{8,17},{9,21}... | collective-permute-start | bytes 786440 | tf_op jit(solution)/shard_map/ppermute | solution.py:276
  57.5 22.6 %collective-permute-start.19 = (bf16[128,1024]{1,0:T(8,128)(2,1)S(1)}, bf16[128,1024]{1,0:T(8,128)(2,1)S(1)}, u32[]{:S(2)}, u32[]{:S(2)}) collective-permute-start(bf16[128,1024]{1,0:T(8,128)(2,1)S(1)} %get-tuple-element.58), channel_id=1, source_target_pairs={{0,0},{1,4},{2,8},{3,12},{4,16},{5,20},{6,24},{7,28},{8,25},{9,29}... | collective-permute-start | bytes 786440 | tf_op jit(solution)/shard_map/ppermute | solution.py:276

commit v7 on v6

--- a/solution.py
+++ b/solution.py
@@ -126,30 +126,47 @@
     return (1 - (plane ^ (plane >> 1)) % 2) * (count - 1)
 
 
-def project_kernel(group, half, parts, groups_of_slots, *refs):
-    halves, refs = refs[: 2 * len(groups_of_slots)], refs[2 * len(groups_of_slots) :]
-    w_ref, w_pair_ref, refs = refs[0], refs[1], refs[2:]
-    out_refs, (x_keep, x_got, total) = refs[:-3], refs[-3:]
+def project_rows(slot_groups, halves, w_ref, w_pair_ref, x_keep, x_got, piece):
+    many = sum(len(slots) for slots in slot_groups)
+    count = x_keep.shape[0] // (many * piece)
+    before = 0
+    for n, slots in enumerate(slot_groups):
+        each = len(slots) * piece
+        for a in range(count):
+            at = (a * many + before) * piece
+            x_keep[at : at + each, :] = halves[2 * n][a * each : (a + 1) * each, :]
+            x_got[at : at + each, :] = halves[2 * n + 1][a * each : (a + 1) * each, :]
+        before += len(slots)
+    return jnp.dot(x_keep[...], w_ref[...], preferred_element_type=jnp.float32) + jnp.dot(
+        x_got[...], w_pair_ref[...], preferred_element_type=jnp.float32
+    )
+
+
+def project_early_kernel(piece, slot_groups, *refs):
+    halves, (w_ref, w_pair_ref, out_ref, x_keep, x_got) = refs[:-5], refs[-5:]
+    total = project_rows(slot_groups, halves, w_ref, w_pair_ref, x_keep, x_got, piece)
+    out_ref[...] = total.astype(jnp.bfloat16)
+
+
+def project_kernel(group, half, parts, early_groups, late_groups, *refs):
+    halves, refs = refs[: 2 * len(late_groups)], refs[2 * len(late_groups) :]
+    early_ref, w_ref, w_pair_ref, refs = refs[0], refs[1], refs[2], refs[3:]
+    out_refs, (x_keep, x_got, late_ref) = refs[:-3], refs[-3:]
     count = len(out_refs)
-    rows = out_refs[0].shape[0]
-    piece = rows // parts
+    piece = out_refs[0].shape[0] // parts
     me = lax.axis_index("ctx")
-    for n, slots in enumerate(groups_of_slots):
-        for held, part in ((x_keep, halves[2 * n]), (x_got, halves[2 * n + 1])):
-            for i, slot in enumerate(slots):
-                d = jnp.bitwise_xor(me, slot)
-                for a in range(count):
-                    at = pl.ds(pl.multiple_of(a * rows + d * piece, piece), piece)
-                    first = (a * len(slots) + i) * piece
-                    held[at, :] = part[first : first + piece, :]
-    total[...] = jnp.dot(x_keep[...], w_ref[...], preferred_element_type=jnp.float32) + jnp.dot(
-        x_got[...], w_pair_ref[...], preferred_element_type=jnp.float32
-    )
+    total = project_rows(late_groups, halves, w_ref, w_pair_ref, x_keep, x_got, piece)
+    late_ref[...] = total.astype(jnp.bfloat16)
     mine = lax.rem(me, group) * half + lax.div(lax.axis_index("head"), 2)
     mine = jnp.bitwise_xor(mine, turn_of(lax.div(me, group), count))
     for k, out_ref in enumerate(out_refs):
-        at = pl.ds(pl.multiple_of(jnp.bitwise_xor(mine, k) * rows, rows), rows)
-        out_ref[...] = total[at, :].astype(jnp.bfloat16)
+        a = jnp.bitwise_xor(mine, k)
+        for held, slot_groups in ((early_ref, early_groups), (late_ref, late_groups)):
+            slots = [slot for some in slot_groups for slot in some]
+            for i, slot in enumerate(slots):
+                d = jnp.bitwise_xor(me, slot)
+                at = pl.multiple_of((a * len(slots) + i) * piece, piece)
+                out_ref[pl.ds(pl.multiple_of(d * piece, piece), piece), :] = held[pl.ds(at, piece), :]
 
 
 def final_kernel(group, half, *refs):
@@ -225,7 +242,7 @@
     count = parts // 2
     arrived, halves = [], []
     last = parts - 1
-    slot_groups = [range(count), range(count, count + 1), range(count + 1, last), range(last, parts)]
+    slot_groups = [range(half), range(half, count), range(count, count + 1), range(count + 1, last), range(last, parts)]
     for slots in slot_groups:
         inputs = [*near, *far_kv]
         if slots[0] >= count:
@@ -251,22 +268,36 @@
             second = spread_second(far_q, parts)
             far_q = [far_q]
         if slots[0] == count:
-            send, second = lax.optimization_barrier((send, second))
+            send, halves[-2], second = lax.optimization_barrier((send, halves[-2], second))
             far_q = spread_third(far_q[0], second, parts)
         halves += [keep, lax.ppermute(send, "head", pair)]
+    depth, piece = heads * HEAD_DIM, rows // parts
+    early_groups, late_groups = slot_groups[:3], slot_groups[3:]
+    early_rows, late_rows = [
+        count * piece * sum(len(slots) for slots in some) for some in (early_groups, late_groups)
+    ]
+    early = pl.pallas_call(
+        functools.partial(project_early_kernel, piece, early_groups),
+        out_shape=jax.ShapeDtypeStruct((early_rows, width), bf16),
+        in_specs=[VMEM] * (2 * len(early_groups) + 2),
+        out_specs=VMEM,
+        scratch_shapes=[pltpu.VMEM((early_rows, depth), bf16)] * 2,
+        compiler_params=params,
+        name="project_early",
+    )(*halves[: 2 * len(early_groups)], w_out, w_pair)
     sums = pl.pallas_call(
-        functools.partial(project_kernel, group, half, parts, slot_groups),
+        functools.partial(project_kernel, group, half, parts, early_groups, late_groups),
         out_shape=[jax.ShapeDtypeStruct((rows, width), bf16)] * count,
-        in_specs=[VMEM] * (2 * len(slot_groups) + 2),
+        in_specs=[VMEM] * (2 * len(late_groups) + 3),
         out_specs=[VMEM] * count,
         scratch_shapes=[
-            pltpu.VMEM((count * rows, heads * HEAD_DIM), bf16),
-            pltpu.VMEM((count * rows, heads * HEAD_DIM), bf16),
-            pltpu.VMEM((count * rows, width), jnp.float32),
+            pltpu.VMEM((late_rows, depth), bf16),
+            pltpu.VMEM((late_rows, depth), bf16),
+            pltpu.VMEM((late_rows, width), bf16),
         ],
         compiler_params=params,
         name="project",
-    )(*halves, w_out, w_pair)
+    )(*halves[2 * len(early_groups) :], early, w_out, w_pair)
     for k in range(count):
         pairs = []
         for c in range(parts):

time: 82.2 us -> 80.1 us (0.974); the launches traced: 81 us -> 79.9 us
  starting transfers between devices: 26.5 us -> 23.2 us
  Pallas kernels: 14.4 us -> 15.9 us
    ppermute x4 -> x5, starting transfers between devices: 9.37 us -> 6.13 us  [packed_body(): halves += [keep, lax.ppermute(send, 'head', pair)]]
    pallas_call x4 -> x5, Pallas kernels: 9.05 us -> 10.5 us  [packed_body(): pl.pallas_call(functools.partial(attend_kernel, parts, heads, 1.0 / math....]
    ppermute x4 -> x5, waiting for transfers between devices: 0.98 us -> 0.01 us  [packed_body(): halves += [keep, lax.ppermute(send, 'head', pair)]]
    ppermute x4, waiting for transfers between devices: 19.7 us -> 20.6 us  [packed_body(): arrived.append(lax.ppermute(sums[k], ('ctx', 'head'), pairs))]
    ppermute x4, starting transfers between devices: 7.31 us -> 6.43 us  [packed_body(): arrived.append(lax.ppermute(sums[k], ('ctx', 'head'), pairs))]
    pallas_call x1 -> x2, Pallas kernels: 2.51 us -> 2.54 us  [the longest x1 1.53 us: packed_body(): pl.pallas_call(functools.partial(project_early_kernel, piece, early_group...]
  transfers between devices with their start and end apart: 20 -> 21, of which waited for: 10 -> 10; matrix products, arithmetic and copies ran while one was open for 0% -> 0% of each run, Pallas kernels for 14% -> 17%
where the time goes in v7:
time: 80.1 us; the launch traced here: 79.9 us
  waiting for transfers between devices  39.6 us (49%)
  starting transfers between devices  23.2 us (29%)
  Pallas kernels  15.9 us (20%)
  local copies, waits for them, and re-layouts  0.98 us (1%)
    ppermute x4, waiting for transfers between devices, packed_body(): arrived.append(lax.ppermute(sums[k], ('ctx', 'head'), pairs))  20.6 us
    ppermute x11, waiting for transfers between devices, along_ctx(): return lax.ppermute(x, 'ctx', [(i, i ^ k) for i in range(parts)])  19 us
    pallas_call x5, Pallas kernels, packed_body(): pl.pallas_call(functools.partial(attend_kernel, parts, heads, 1.0 / math....  10.5 us
    ppermute x11, starting transfers between devices, along_ctx(): return lax.ppermute(x, 'ctx', [(i, i ^ k) for i in range(parts)])  9.98 us
    ppermute x4, starting transfers between devices, packed_body(): arrived.append(lax.ppermute(sums[k], ('ctx', 'head'), pairs))  6.43 us
    ppermute x5, starting transfers between devices, packed_body(): halves += [keep, lax.ppermute(send, 'head', pair)]  6.13 us
    pallas_call x1, Pallas kernels, packed_body(): pl.pallas_call(functools.partial(pack_kernel, parts, heads), out_shape=[j...  1.92 us
  transfers between devices with their start and end apart: 21, of which 10 were waited for; matrix products, arithmetic and copies ran while one was open for 0% of the time, Pallas kernels for 17%

profile of v7, /device:TPU:17, one launch (start us, length us, event | category | flops | bytes accessed | tf_op | source)
XLA Modules:
  0.0 79.9 jit_solution(13321866318224327390)
XLA Ops:
  0.0 0.7 collective-permute-start.16
  0.7 1.9 %pack.1 = (bf16[1296,128]{1,0:T(8,128)(2,1)}, bf16[1024,128]{1,0:T(8,128)(2,1)}, bf16[272,128]{1,0:T(8,128)(2,1)}) custom-call(s32[1,8]{1,0:T(1,128)} %plan_ref.1, bf16[128,1024]{1,0:T(8,128)(2,1)} %q_ref.1, bf16[128,128]{1,0:T(8,128)(2,1)} %k_ref.1, bf16[128,128]{1,0:T(8,128)(2,1)} %v_ref.1, s32[1,128]{1,0:T(1,128)} %bitcast.1), custom_call_target="tpu_custom_call" | custom-call | tf_op jit(solution)/shard_map/pack/pallas_call | solution.py:229
  2.6 1.3 %collective-permute-start.1 = (bf16[1296,128]{1,0:T(8,128)(2,1)}, bf16[1296,128]{1,0:T(8,128)(2,1)S(1)}, u32[]{:S(2)}, u32[]{:S(2)}) collective-permute-start(bf16[1296,128]{1,0:T(8,128)(2,1)} %get-tuple-element.37.refs_0_), channel_id=1, source_target_pairs={{0,8},{4,12},{8,0},{12,4},{16,24},{20,28},{24,16},{28,20},{1,9},{5... | collective-permute-start | bytes 995336 | tf_op jit(solution)/shard_map/ppermute | solution.py:186
  3.9 1.2 %collective-permute-start = (bf16[1296,128]{1,0:T(8,128)(2,1)}, bf16[1296,128]{1,0:T(8,128)(2,1)S(1)}, u32[]{:S(2)}, u32[]{:S(2)}) collective-permute-start(bf16[1296,128]{1,0:T(8,128)(2,1)} %get-tuple-element.37.refs_0_), channel_id=1, source_target_pairs={{0,4},{4,0},{8,12},{12,8},{16,20},{20,16},{24,28},{28,24},{1,5},{5... | collective-permute-start | bytes 995336 | tf_op jit(solution)/shard_map/ppermute | solution.py:186
  5.1 2.3 %collective-permute-start.2 = (bf16[272,128]{1,0:T(8,128)(2,1)}, bf16[272,128]{1,0:T(8,128)(2,1)S(1)}, u32[]{:S(2)}, u32[]{:S(2)}) collective-permute-start(bf16[272,128]{1,0:T(8,128)(2,1)} %get-tuple-element.36), channel_id=1, source_target_pairs={{0,16},{4,20},{8,24},{12,28},{16,0},{20,4},{24,8},{28,12},{1,17},{... | collective-permute-start | bytes 208904 | tf_op jit(solution)/shard_map/ppermute | solution.py:186
  7.4 7.1 %collective-permute-done.3.refs_5_ = bf16[272,128]{1,0:T(8,128)(2,1)S(1)} collective-permute-done((bf16[272,128]{1,0:T(8,128)(2,1)}, bf16[272,128]{1,0:T(8,128)(2,1)S(1)}, u32[]{:S(2)}, u32[]{:S(2)}) %collective-permute-start.3) | collective-permute-done | bytes 69664 | tf_op jit(solution)/shard_map/ppermute | solution.py:186
  14.6 0.5 collective-permute-done.2.refs_4_
  15.1 0.0 collective-permute-done.1.refs_2_
  15.1 0.0 collective-permute-done.refs_1_
  15.1 1.2 %collective-permute-start.4 = (bf16[1296,128]{1,0:T(8,128)(2,1)S(1)}, bf16[1296,128]{1,0:T(8,128)(2,1)S(1)}, u32[]{:S(2)}, u32[]{:S(2)}) collective-permute-start(bf16[1296,128]{1,0:T(8,128)(2,1)S(1)} %collective-permute-done.1.refs_2_), channel_id=1, source_target_pairs={{0,4},{4,0},{8,12},{12,8},{16,20},{20,16},{24,28},{28,24},{1,5},{5... | collective-permute-start | bytes 995336 | tf_op jit(solution)/shard_map/ppermute | solution.py:186
  16.4 0.2 collective-permute-start.7
  16.5 2.3 %collective-permute-start.5 = (bf16[272,128]{1,0:T(8,128)(2,1)S(1)}, bf16[272,128]{1,0:T(8,128)(2,1)S(1)}, u32[]{:S(2)}, u32[]{:S(2)}) collective-permute-start(bf16[272,128]{1,0:T(8,128)(2,1)S(1)} %collective-permute-done.2.refs_4_), channel_id=1, source_target_pairs={{0,8},{4,12},{8,0},{12,4},{16,24},{20,28},{24,16},{28,20},{1,9},{5... | collective-permute-start | bytes 208904 | tf_op jit(solution)/shard_map/ppermute | solution.py:186
  18.8 0.0 collective-permute-start.6
  18.9 7.0 %collective-permute-done.5.refs_6_ = bf16[272,128]{1,0:T(8,128)(2,1)S(1)} collective-permute-done((bf16[272,128]{1,0:T(8,128)(2,1)S(1)}, bf16[272,128]{1,0:T(8,128)(2,1)S(1)}, u32[]{:S(2)}, u32[]{:S(2)}) %collective-permute-start.5) | collective-permute-done | bytes 69664 | tf_op jit(solution)/shard_map/ppermute | solution.py:186
  25.9 1.4 %collective-permute-done.6.refs_7_ = bf16[272,128]{1,0:T(8,128)(2,1)S(1)} collective-permute-done((bf16[272,128]{1,0:T(8,128)(2,1)S(1)}, bf16[272,128]{1,0:T(8,128)(2,1)S(1)}, u32[]{:S(2)}, u32[]{:S(2)}) %collective-permute-start.6) | collective-permute-done | bytes 69664 | tf_op jit(solution)/shard_map/ppermute | solution.py:186
  27.3 1.0 %copy-done.1 = bf16[1296,128]{1,0:T(8,128)(2,1)S(1)} copy-done((bf16[1296,128]{1,0:T(8,128)(2,1)S(1)}, bf16[1296,128]{1,0:T(8,128)(2,1)}, u32[]{:S(2)}) %copy-start.1) | copy-done | bytes 331800
  28.3 3.2 %attend.5 = (bf16[128,1024]{1,0:T(8,128)(2,1)S(1)}, bf16[128,1024]{1,0:T(8,128)(2,1)S(1)}) custom-call(bf16[1296,128]{1,0:T(8,128)(2,1)S(1)} %copy-done.1, bf16[1296,128]{1,0:T(8,128)(2,1)S(1)} %collective-permute-done.refs_1_, bf16[1296,128]{1,0:T(8,128)(2,1)S(1)} %collective-permute-done.1.refs_2_, bf16[1296,128]{1,0:T(8,128)(2,1)S(1)} %collective-permute-done.4.refs_3_, ...), custom_call_target="tpu_custom_call" | custom-call | tf_op jit(solution)/shard_map/attend/pallas_call | solution.py:252
  31.5 0.0 collective-permute-done.7.refs_8_
  31.6 0.9 %collective-permute-start.9 = (bf16[1024,128]{1,0:T(8,128)(2,1)S(1)}, bf16[1024,128]{1,0:T(8,128)(2,1)S(1)}, u32[]{:S(2)}, u32[]{:S(2)}) collective-permute-start(bf16[1024,128]{1,0:T(8,128)(2,1)S(1)} %collective-permute-done.7.refs_8_), channel_id=1, source_target_pairs={{0,8},{4,12},{8,0},{12,4},{16,24},{20,28},{24,16},{28,20},{1,9},{5... | collective-permute-start | bytes 786440 | tf_op jit(solution)/shard_map/ppermute | solution.py:186
  32.5 0.2 collective-permute-start.8
  32.7 2.8 %attend.7 = (bf16[128,1024]{1,0:T(8,128)(2,1)S(1)}, bf16[128,1024]{1,0:T(8,128)(2,1)S(1)}) custom-call(bf16[1296,128]{1,0:T(8,128)(2,1)S(1)} %copy-done.1, bf16[1296,128]{1,0:T(8,128)(2,1)S(1)} %collective-permute-done.refs_1_, bf16[1296,128]{1,0:T(8,128)(2,1)S(1)} %collective-permute-done.1.refs_2_, bf16[1296,128]{1,0:T(8,128)(2,1)S(1)} %collective-permute-done.4.refs_3_, ...), custom_call_target="tpu_custom_call" | custom-call | tf_op jit(solution)/shard_map/attend/pallas_call | solution.py:252
  35.5 1.0 %attend.6 = (bf16[64,1024]{1,0:T(8,128)(2,1)S(1)}, bf16[64,1024]{1,0:T(8,128)(2,1)S(1)}) custom-call(bf16[1296,128]{1,0:T(8,128)(2,1)S(1)} %copy-done.1, bf16[1296,128]{1,0:T(8,128)(2,1)S(1)} %collective-permute-done.refs_1_, bf16[1296,128]{1,0:T(8,128)(2,1)S(1)} %collective-permute-done.1.refs_2_, bf16[1296,128]{1,0:T(8,128)(2,1)S(1)} %collective-permute-done.4.refs_3_, ...), custom_call_target="tpu_custom_call" | custom-call | tf_op jit(solution)/shard_map/attend/pallas_call | solution.py:252
  36.6 0.0 copy-start
  36.6 0.8 %collective-permute-done.9.refs_9_ = bf16[1024,128]{1,0:T(8,128)(2,1)S(1)} collective-permute-done((bf16[1024,128]{1,0:T(8,128)(2,1)S(1)}, bf16[1024,128]{1,0:T(8,128)(2,1)S(1)}, u32[]{:S(2)}, u32[]{:S(2)}) %collective-permute-start.9) | collective-permute-done | bytes 262176 | tf_op jit(solution)/shard_map/ppermute | solution.py:186
  37.4 1.7 %collective-permute-done.8.refs_8_ = bf16[1024,128]{1,0:T(8,128)(2,1)S(1)} collective-permute-done((bf16[1024,128]{1,0:T(8,128)(2,1)S(1)}, bf16[1024,128]{1,0:T(8,128)(2,1)S(1)}, u32[]{:S(2)}, u32[]{:S(2)}) %collective-permute-start.8) | collective-permute-done | bytes 262176 | tf_op jit(solution)/shard_map/ppermute | solution.py:186
  39.1 0.2 collective-permute-start.11
  39.3 2.4 %collective-permute-start.14 = (bf16[128,1024]{1,0:T(8,128)(2,1)S(1)}, bf16[128,1024]{1,0:T(8,128)(2,1)S(1)}, u32[]{:S(2)}, u32[]{:S(2)}) collective-permute-start(bf16[128,1024]{1,0:T(8,128)(2,1)S(1)} %get-tuple-element.58), channel_id=1, source_target_pairs={{0,1},{1,0},{2,3},{3,2},{4,5},{5,4},{6,7},{7,6},{8,9},{9,8},{10,11... | collective-permute-start | bytes 786440 | tf_op jit(solution)/shard_map/ppermute | solution.py:273
  41.7 2.0 %attend.8 = (bf16[128,1024]{1,0:T(8,128)(2,1)S(1)}, bf16[128,1024]{1,0:T(8,128)(2,1)S(1)}) custom-call(bf16[1296,128]{1,0:T(8,128)(2,1)S(1)} %copy-done.1, bf16[1296,128]{1,0:T(8,128)(2,1)S(1)} %collective-permute-done.refs_1_, bf16[1296,128]{1,0:T(8,128)(2,1)S(1)} %collective-permute-done.1.refs_2_, bf16[1296,128]{1,0:T(8,128)(2,1)S(1)} %collective-permute-done.4.refs_3_, ...), custom_call_target="tpu_custom_call" | custom-call | tf_op jit(solution)/shard_map/attend/pallas_call | solution.py:252
  43.8 0.6 collective-permute-start.10
  44.3 0.4 collective-permute-done.11.refs_8_
  44.7 3.1 %collective-permute-start.15 = (bf16[64,1024]{1,0:T(8,128)(2,1)S(1)}, bf16[64,1024]{1,0:T(8,128)(2,1)S(1)}, u32[]{:S(2)}, u32[]{:S(2)}) collective-permute-start(bf16[64,1024]{1,0:T(8,128)(2,1)S(1)} %get-tuple-element.60), channel_id=1, source_target_pairs={{0,1},{1,0},{2,3},{3,2},{4,5},{5,4},{6,7},{7,6},{8,9},{9,8},{10,11... | collective-permute-start | bytes 393224 | tf_op jit(solution)/shard_map/ppermute | solution.py:273
  47.8 1.4 %attend.9 = (bf16[64,1024]{1,0:T(8,128)(2,1)S(1)}, bf16[64,1024]{1,0:T(8,128)(2,1)S(1)}) custom-call(bf16[1296,128]{1,0:T(8,128)(2,1)S(1)} %copy-done.1, bf16[1296,128]{1,0:T(8,128)(2,1)S(1)} %collective-permute-done.refs_1_, bf16[1296,128]{1,0:T(8,128)(2,1)S(1)} %collective-permute-done.1.refs_2_, bf16[1296,128]{1,0:T(8,128)(2,1)S(1)} %collective-permute-done.4.refs_3_, ...), custom_call_target="tpu_custom_call" | custom-call | tf_op jit(solution)/shard_map/attend/pallas_call | solution.py:252
  49.2 0.0 collective-permute-done.14.refs_3_
  49.2 0.1 collective-permute-start.12
  49.3 0.0 collective-permute-done.13.refs_1_
  49.3 0.0 collective-permute-done.15.refs_5_
  49.3 1.5 %project_early.1.refs_4_ = bf16[320,1024]{1,0:T(8,128)(2,1)S(1)} custom-call(bf16[128,1024]{1,0:T(8,128)(2,1)S(1)} %get-tuple-element.55.refs_0_, bf16[128,1024]{1,0:T(8,128)(2,1)S(1)} %collective-permute-done.13.refs_1_, bf16[128,1024]{1,0:T(8,128)(2,1)S(1)} %get-tuple-element.57.refs_2_, bf16[128,1024]{1,0:T(8,128)(2,1)S(1)} %collective-permute-done.14.refs_3_, ...), custom_call_target="tpu_custom_call" | custom-call | tf_op jit(solution)/shard_map/project_early/pallas_call | solution.py:279
  50.9 0.0 collective-permute-done.12.refs_3_
  50.9 1.0 %project.1 = (bf16[128,1024]{1,0:T(8,128)(2,1)S(1)}, bf16[128,1024]{1,0:T(8,128)(2,1)S(1)}, bf16[128,1024]{1,0:T(8,128)(2,1)S(1)}, bf16[128,1024]{1,0:T(8,128)(2,1)S(1)}) custom-call(bf16[128,1024]{1,0:T(8,128)(2,1)S(1)} %get-tuple-element.51.refs_0_, bf16[128,1024]{1,0:T(8,128)(2,1)S(1)} %collective-permute-done.10.refs_1_, ...), custom_call_target="tpu_custom_call" | custom-call | tf_op jit(solution)/shard_map/project/pallas_call | solution.py:288
  51.9 1.5 %collective-permute-start.17 = (bf16[128,1024]{1,0:T(8,128)(2,1)S(1)}, bf16[128,1024]{1,0:T(8,128)(2,1)S(1)}, u32[]{:S(2)}, u32[]{:S(2)}) collective-permute-start(bf16[128,1024]{1,0:T(8,128)(2,1)S(1)} %get-tuple-element.61), channel_id=1, source_target_pairs={{0,24},{1,28},{2,16},{3,20},{4,8},{5,12},{6,0},{7,4},{8,1},{9,5},{... | collective-permute-start | bytes 786440 | tf_op jit(solution)/shard_map/ppermute | solution.py:307
  53.4 1.9 %collective-permute-start.18 = (bf16[128,1024]{1,0:T(8,128)(2,1)S(1)}, bf16[128,1024]{1,0:T(8,128)(2,1)S(1)}, u32[]{:S(2)}, u32[]{:S(2)}) collective-permute-start(bf16[128,1024]{1,0:T(8,128)(2,1)S(1)} %get-tuple-element.62), channel_id=1, source_target_pairs={{0,16},{1,20},{2,24},{3,28},{4,0},{5,4},{6,8},{7,12},{8,9},{9,13},... | collective-permute-start | bytes 786440 | tf_op jit(solution)/shard_map/ppermute | solution.py:307
  55.3 0.0 collective-permute-start.19
  55.3 3.0 %collective-permute-start.20 = (bf16[128,1024]{1,0:T(8,128)(2,1)S(1)}, bf16[128,1024]{1,0:T(8,128)(2,1)S(1)}, u32[]{:S(2)}, u32[]{:S(2)}) collective-permute-start(bf16[128,1024]{1,0:T(8,128)(2,1)S(1)} %get-tuple-element.64), channel_id=1, source_target_pairs={{0,0},{1,4},{2,8},{3,12},{4,16},{5,20},{6,24},{7,28},{8,25},{9,29}... | collective-permute-start | bytes 786440 | tf_op jit(solution)/shard_map/ppermute | solution.py:307
  58.4 14.4 %collective-permute-done.17.refs_0_ = bf16[128,1024]{1,0:T(8,128)(2,1)S(1)} collective-permute-done((bf16[128,1024]{1,0:T(8,128)(2,1)S(1)}, bf16[128,1024]{1,0:T(8,128)(2,1)S(1)}, u32[]{:S(2)}, u32[]{:S(2)}) %collective-permute-start.17) | collective-permute-done | bytes 262176 | tf_op jit(solution)/shard_map/ppermute | solution.py:307
  72.8 4.7 %collective-permute-done.18.refs_1_ = bf16[128,1024]{1,0:T(8,128)(2,1)S(1)} collective-permute-done((bf16[128,1024]{1,0:T(8,128)(2,1)S(1)}, bf16[128,1024]{1,0:T(8,128)(2,1)S(1)}, u32[]{:S(2)}, u32[]{:S(2)}) %collective-permute-start.18) | collective-permute-done | bytes 262176 | tf_op jit(solution)/shard_map/ppermute | solution.py:307
  77.5 0.0 collective-permute-done.19.refs_2_
  77.5 1.4 %collective-permute-done.20.refs_3_ = bf16[128,1024]{1,0:T(8,128)(2,1)S(1)} collective-permute-done((bf16[128,1024]{1,0:T(8,128)(2,1)S(1)}, bf16[128,1024]{1,0:T(8,128)(2,1)S(1)}, u32[]{:S(2)}, u32[]{:S(2)}) %collective-permute-start.20) | collective-permute-done | bytes 262176 | tf_op jit(solution)/shard_map/ppermute | solution.py:307
  79.0 0.9 %final_sum.1 = bf16[128,2048]{1,0:T(8,128)(2,1)} custom-call(bf16[128,1024]{1,0:T(8,128)(2,1)S(1)} %collective-permute-done.17.refs_0_, bf16[128,1024]{1,0:T(8,128)(2,1)S(1)} %collective-permute-done.18.refs_1_, bf16[128,1024]{1,0:T(8,128)(2,1)S(1)} %collective-permute-done.19.refs_2_, bf16[128,1024]{1,0:T(8,128)(2,1)S(1)} %collective-permute-done.20.refs_3_), custom_call_target="tpu_custom_call" | custom-call | tf_op jit(solution)/shard_map/final_sum/pallas_call | solution.py:308
  (7 shorter events, 0.0 us)
Async XLA Ops:
  0.0 49.3 %collective-permute-start.16 = (bf16[1024,1024]{1,0:T(8,128)(2,1)}, bf16[1024,1024]{1,0:T(8,128)(2,1)S(1)}, u32[]{:S(2)}, u32[]{:S(2)}) collective-permute-start(bf16[1024,1024]{1,0:T(8,128)(2,1)} %refs_5_.1), channel_id=1, source_target_pairs={{0,1},{1,0},{2,3},{3,2},{4,5},{5,4},{6,7},{7,6},{8,9},{9,8},{10,11... | collective-permute-start | bytes 6291464 | tf_op jit(solution)/shard_map/ppermute | solution.py:228
  2.6 12.5 %collective-permute-start.1 = (bf16[1296,128]{1,0:T(8,128)(2,1)}, bf16[1296,128]{1,0:T(8,128)(2,1)S(1)}, u32[]{:S(2)}, u32[]{:S(2)}) collective-permute-start(bf16[1296,128]{1,0:T(8,128)(2,1)} %get-tuple-element.37.refs_0_), channel_id=1, source_target_pairs={{0,8},{4,12},{8,0},{12,4},{16,24},{20,28},{24,16},{28,20},{1,9},{5... | collective-permute-start | bytes 995336 | tf_op jit(solution)/shard_map/ppermute | solution.py:186
  3.9 11.2 %collective-permute-start = (bf16[1296,128]{1,0:T(8,128)(2,1)}, bf16[1296,128]{1,0:T(8,128)(2,1)S(1)}, u32[]{:S(2)}, u32[]{:S(2)}) collective-permute-start(bf16[1296,128]{1,0:T(8,128)(2,1)} %get-tuple-element.37.refs_0_), channel_id=1, source_target_pairs={{0,4},{4,0},{8,12},{12,8},{16,20},{20,16},{24,28},{28,24},{1,5},{5... | collective-permute-start | bytes 995336 | tf_op jit(solution)/shard_map/ppermute | solution.py:186
  5.1 9.4 %collective-permute-start.3 = (bf16[272,128]{1,0:T(8,128)(2,1)}, bf16[272,128]{1,0:T(8,128)(2,1)S(1)}, u32[]{:S(2)}, u32[]{:S(2)}) collective-permute-start(bf16[272,128]{1,0:T(8,128)(2,1)} %get-tuple-element.36), channel_id=1, source_target_pairs={{0,20},{4,16},{8,28},{12,24},{16,4},{20,0},{24,12},{28,8},{1,21},{... | collective-permute-start | bytes 208904 | tf_op jit(solution)/shard_map/ppermute | solution.py:186
  5.1 10.0 %collective-permute-start.2 = (bf16[272,128]{1,0:T(8,128)(2,1)}, bf16[272,128]{1,0:T(8,128)(2,1)S(1)}, u32[]{:S(2)}, u32[]{:S(2)}) collective-permute-start(bf16[272,128]{1,0:T(8,128)(2,1)} %get-tuple-element.36), channel_id=1, source_target_pairs={{0,16},{4,20},{8,24},{12,28},{16,0},{20,4},{24,8},{28,12},{1,17},{... | collective-permute-start | bytes 208904 | tf_op jit(solution)/shard_map/ppermute | solution.py:186
  15.1 12.2 %collective-permute-start.4 = (bf16[1296,128]{1,0:T(8,128)(2,1)S(1)}, bf16[1296,128]{1,0:T(8,128)(2,1)S(1)}, u32[]{:S(2)}, u32[]{:S(2)}) collective-permute-start(bf16[1296,128]{1,0:T(8,128)(2,1)S(1)} %collective-permute-done.1.refs_2_), channel_id=1, source_target_pairs={{0,4},{4,0},{8,12},{12,8},{16,20},{20,16},{24,28},{28,24},{1,5},{5... | collective-permute-start | bytes 995336 | tf_op jit(solution)/shard_map/ppermute | solution.py:186
  16.4 15.2 %collective-permute-start.7 = (bf16[1024,128]{1,0:T(8,128)(2,1)}, bf16[1024,128]{1,0:T(8,128)(2,1)S(1)}, u32[]{:S(2)}, u32[]{:S(2)}) collective-permute-start(bf16[1024,128]{1,0:T(8,128)(2,1)} %get-tuple-element.43), channel_id=1, source_target_pairs={{0,16},{4,20},{8,24},{12,28},{16,0},{20,4},{24,8},{28,12},{1,17},{... | collective-permute-start | bytes 786440 | tf_op jit(solution)/shard_map/ppermute | solution.py:186
  16.5 9.4 %collective-permute-start.5 = (bf16[272,128]{1,0:T(8,128)(2,1)S(1)}, bf16[272,128]{1,0:T(8,128)(2,1)S(1)}, u32[]{:S(2)}, u32[]{:S(2)}) collective-permute-start(bf16[272,128]{1,0:T(8,128)(2,1)S(1)} %collective-permute-done.2.refs_4_), channel_id=1, source_target_pairs={{0,8},{4,12},{8,0},{12,4},{16,24},{20,28},{24,16},{28,20},{1,9},{5... | collective-permute-start | bytes 208904 | tf_op jit(solution)/shard_map/ppermute | solution.py:186
  18.8 8.5 %collective-permute-start.6 = (bf16[272,128]{1,0:T(8,128)(2,1)S(1)}, bf16[272,128]{1,0:T(8,128)(2,1)S(1)}, u32[]{:S(2)}, u32[]{:S(2)}) collective-permute-start(bf16[272,128]{1,0:T(8,128)(2,1)S(1)} %collective-permute-done.3.refs_5_), channel_id=1, source_target_pairs={{0,8},{4,12},{8,0},{12,4},{16,24},{20,28},{24,16},{28,20},{1,9},{5... | collective-permute-start | bytes 208904 | tf_op jit(solution)/shard_map/ppermute | solution.py:186
  27.3 1.0 %copy-start.1 = (bf16[1296,128]{1,0:T(8,128)(2,1)S(1)}, bf16[1296,128]{1,0:T(8,128)(2,1)}, u32[]{:S(2)}) copy-start(bf16[1296,128]{1,0:T(8,128)(2,1)} %get-tuple-element.37.refs_0_) | copy-start | bytes 995332
  31.6 5.9 %collective-permute-start.9 = (bf16[1024,128]{1,0:T(8,128)(2,1)S(1)}, bf16[1024,128]{1,0:T(8,128)(2,1)S(1)}, u32[]{:S(2)}, u32[]{:S(2)}) collective-permute-start(bf16[1024,128]{1,0:T(8,128)(2,1)S(1)} %collective-permute-done.7.refs_8_), channel_id=1, source_target_pairs={{0,8},{4,12},{8,0},{12,4},{16,24},{20,28},{24,16},{28,20},{1,9},{5... | collective-permute-start | bytes 786440 | tf_op jit(solution)/shard_map/ppermute | solution.py:186
  32.5 6.6 %collective-permute-start.8 = (bf16[1024,128]{1,0:T(8,128)(2,1)S(1)}, bf16[1024,128]{1,0:T(8,128)(2,1)S(1)}, u32[]{:S(2)}, u32[]{:S(2)}) collective-permute-start(bf16[1024,128]{1,0:T(8,128)(2,1)S(1)} %collective-permute-done.7.refs_8_), channel_id=1, source_target_pairs={{0,4},{4,0},{8,12},{12,8},{16,20},{20,16},{24,28},{28,24},{1,5},{5... | collective-permute-start | bytes 786440 | tf_op jit(solution)/shard_map/ppermute | solution.py:186
  36.6 12.8 %copy-start = (bf16[1024,1024]{1,0:T(8,128)(2,1)S(1)}, bf16[1024,1024]{1,0:T(8,128)(2,1)}, u32[]{:S(2)}) copy-start(bf16[1024,1024]{1,0:T(8,128)(2,1)} %refs_5_.1) | copy-start | bytes 6291460
  39.1 5.7 %collective-permute-start.11 = (bf16[1024,128]{1,0:T(8,128)(2,1)S(1)}, bf16[1024,128]{1,0:T(8,128)(2,1)S(1)}, u32[]{:S(2)}, u32[]{:S(2)}) collective-permute-start(bf16[1024,128]{1,0:T(8,128)(2,1)S(1)} %collective-permute-done.9.refs_9_), channel_id=1, source_target_pairs={{0,4},{4,0},{8,12},{12,8},{16,20},{20,16},{24,28},{28,24},{1,5},{5... | collective-permute-start | bytes 786440 | tf_op jit(solution)/shard_map/ppermute | solution.py:186
  39.3 9.9 %collective-permute-start.14 = (bf16[128,1024]{1,0:T(8,128)(2,1)S(1)}, bf16[128,1024]{1,0:T(8,128)(2,1)S(1)}, u32[]{:S(2)}, u32[]{:S(2)}) collective-permute-start(bf16[128,1024]{1,0:T(8,128)(2,1)S(1)} %get-tuple-element.58), channel_id=1, source_target_pairs={{0,1},{1,0},{2,3},{3,2},{4,5},{5,4},{6,7},{7,6},{8,9},{9,8},{10,11... | collective-permute-start | bytes 786440 | tf_op jit(solution)/shard_map/ppermute | solution.py:273
  41.7 7.6 %collective-permute-start.13 = (bf16[128,1024]{1,0:T(8,128)(2,1)S(1)}, bf16[128,1024]{1,0:T(8,128)(2,1)S(1)}, u32[]{:S(2)}, u32[]{:S(2)}) collective-permute-start(bf16[128,1024]{1,0:T(8,128)(2,1)S(1)} %get-tuple-element.56), channel_id=1, source_target_pairs={{0,1},{1,0},{2,3},{3,2},{4,5},{5,4},{6,7},{7,6},{8,9},{9,8},{10,11... | collective-permute-start | bytes 786440 | tf_op jit(solution)/shard_map/ppermute | solution.py:273
  43.8 7.1 %collective-permute-start.10 = (bf16[128,1024]{1,0:T(8,128)(2,1)S(1)}, bf16[128,1024]{1,0:T(8,128)(2,1)S(1)}, u32[]{:S(2)}, u32[]{:S(2)}) collective-permute-start(bf16[128,1024]{1,0:T(8,128)(2,1)S(1)} %get-tuple-element.52), channel_id=1, source_target_pairs={{0,1},{1,0},{2,3},{3,2},{4,5},{5,4},{6,7},{7,6},{8,9},{9,8},{10,11... | collective-permute-start | bytes 786440 | tf_op jit(solution)/shard_map/ppermute | solution.py:273
  44.7 4.6 %collective-permute-start.15 = (bf16[64,1024]{1,0:T(8,128)(2,1)S(1)}, bf16[64,1024]{1,0:T(8,128)(2,1)S(1)}, u32[]{:S(2)}, u32[]{:S(2)}) collective-permute-start(bf16[64,1024]{1,0:T(8,128)(2,1)S(1)} %get-tuple-element.60), channel_id=1, source_target_pairs={{0,1},{1,0},{2,3},{3,2},{4,5},{5,4},{6,7},{7,6},{8,9},{9,8},{10,11... | collective-permute-start | bytes 393224 | tf_op jit(solution)/shard_map/ppermute | solution.py:273
  49.2 1.7 %collective-permute-start.12 = (bf16[64,1024]{1,0:T(8,128)(2,1)S(1)}, bf16[64,1024]{1,0:T(8,128)(2,1)S(1)}, u32[]{:S(2)}, u32[]{:S(2)}) collective-permute-start(bf16[64,1024]{1,0:T(8,128)(2,1)S(1)} %get-tuple-element.54), channel_id=1, source_target_pairs={{0,1},{1,0},{2,3},{3,2},{4,5},{5,4},{6,7},{7,6},{8,9},{9,8},{10,11... | collective-permute-start | bytes 393224 | tf_op jit(solution)/shard_map/ppermute | solution.py:273
  51.9 20.9 %collective-permute-start.17 = (bf16[128,1024]{1,0:T(8,128)(2,1)S(1)}, bf16[128,1024]{1,0:T(8,128)(2,1)S(1)}, u32[]{:S(2)}, u32[]{:S(2)}) collective-permute-start(bf16[128,1024]{1,0:T(8,128)(2,1)S(1)} %get-tuple-element.61), channel_id=1, source_target_pairs={{0,24},{1,28},{2,16},{3,20},{4,8},{5,12},{6,0},{7,4},{8,1},{9,5},{... | collective-permute-start | bytes 786440 | tf_op jit(solution)/shard_map/ppermute | solution.py:307
  53.4 24.2 %collective-permute-start.18 = (bf16[128,1024]{1,0:T(8,128)(2,1)S(1)}, bf16[128,1024]{1,0:T(8,128)(2,1)S(1)}, u32[]{:S(2)}, u32[]{:S(2)}) collective-permute-start(bf16[128,1024]{1,0:T(8,128)(2,1)S(1)} %get-tuple-element.62), channel_id=1, source_target_pairs={{0,16},{1,20},{2,24},{3,28},{4,0},{5,4},{6,8},{7,12},{8,9},{9,13},... | collective-permute-start | bytes 786440 | tf_op jit(solution)/shard_map/ppermute | solution.py:307
  55.3 22.2 %collective-permute-start.19 = (bf16[128,1024]{1,0:T(8,128)(2,1)S(1)}, bf16[128,1024]{1,0:T(8,128)(2,1)S(1)}, u32[]{:S(2)}, u32[]{:S(2)}) collective-permute-start(bf16[128,1024]{1,0:T(8,128)(2,1)S(1)} %get-tuple-element.63), channel_id=1, source_target_pairs={{0,8},{1,12},{2,0},{3,4},{4,24},{5,28},{6,16},{7,20},{8,17},{9,21}... | collective-permute-start | bytes 786440 | tf_op jit(solution)/shard_map/ppermute | solution.py:307
  55.3 23.7 %collective-permute-start.20 = (bf16[128,1024]{1,0:T(8,128)(2,1)S(1)}, bf16[128,1024]{1,0:T(8,128)(2,1)S(1)}, u32[]{:S(2)}, u32[]{:S(2)}) collective-permute-start(bf16[128,1024]{1,0:T(8,128)(2,1)S(1)} %get-tuple-element.64), channel_id=1, source_target_pairs={{0,0},{1,4},{2,8},{3,12},{4,16},{5,20},{6,24},{7,28},{8,25},{9,29}... | collective-permute-start | bytes 786440 | tf_op jit(solution)/shard_map/ppermute | solution.py:307

commit v8 on v7

--- a/solution.py
+++ b/solution.py
@@ -17,37 +17,57 @@
 
 ANY = pl.BlockSpec(memory_space=pl.ANY)
 VMEM = pl.BlockSpec(memory_space=pltpu.VMEM)
-SMEM = pl.BlockSpec(memory_space=pltpu.SMEM)
-
-
-def pack_kernel(parts, heads, plan_ref, q_ref, k_ref, v_ref, ids_ref, all_out, q_out, kv_out):
+
+
+def pack_kernel(
+    parts, heads, plan_ref, q_ref, k_ref, v_ref, ids_ref, all_out, q_out, kv_out,
+    plan_held, q_held, held, ids_held, sems,
+):
     rows = q_ref.shape[0]
     piece = rows // parts
+    base = heads * rows
+    pairs = [
+        (plan_ref, plan_held),
+        (ids_ref, ids_held),
+        (k_ref, held.at[base : base + rows]),
+        (v_ref, held.at[base + rows : base + 2 * rows]),
+        (q_ref, q_held),
+        (held.at[base:], kv_out),
+        (held, all_out),
+        (held.at[:base], q_out),
+    ]
+    copies = [pltpu.make_async_copy(*pair, sems.at[n]) for n, pair in enumerate(pairs)]
+    for copy in copies[:5]:
+        copy.start()
+    copies[0].wait()
     lane = lax.broadcasted_iota(jnp.int32, (1, rows), 1)
     source = jnp.zeros((1, rows), jnp.int32)
     for j in range(parts):
-        p = plan_ref[0, j]
-        for h in range(heads):
-            moved = q_ref[
-                pl.ds(pl.multiple_of(p * piece, piece), piece), h * HEAD_DIM : (h + 1) * HEAD_DIM
-            ]
-            q_out[h * rows + j * piece : h * rows + (j + 1) * piece, :] = moved
-            all_out[h * rows + j * piece : h * rows + (j + 1) * piece, :] = moved
-        source = jnp.where(
-            (lane >= j * piece) & (lane < (j + 1) * piece), (p - j) * piece + lane, source
-        )
-    ids = ids_ref[...].astype(jnp.float32)
+        inside = (lane >= j * piece) & (lane < (j + 1) * piece)
+        source = jnp.where(inside, (plan_held[0, j] - j) * piece + lane, source)
     row = lax.broadcasted_iota(jnp.int32, (META, rows), 0)
     from_row = lax.broadcasted_iota(jnp.int32, (rows, rows), 0)
     chosen = (from_row == source).astype(jnp.float32)
-    ids_rows = jnp.broadcast_to(ids, (META, rows))
+    positions = jnp.broadcast_to(source.astype(jnp.float32), (META, rows))
+    copies[1].wait()
+    ids_rows = jnp.broadcast_to(ids_held[...].astype(jnp.float32), (META, rows))
     ids_moved = jnp.dot(ids_rows, chosen, preferred_element_type=jnp.float32)
-    positions = jnp.broadcast_to(source.astype(jnp.float32), (META, rows))
     meta = jnp.where(row == 0, ids_rows, jnp.where(row == 1, ids_moved, positions))
-    for out_ref, base in ((all_out, heads * rows), (kv_out, 0)):
-        out_ref[base : base + rows, :] = k_ref[...]
-        out_ref[base + rows : base + 2 * rows, :] = v_ref[...]
-        out_ref[base + 2 * rows :, :] = meta.astype(jnp.bfloat16)
+    held[base + 2 * rows :, :] = meta.astype(jnp.bfloat16)
+    copies[2].wait()
+    copies[3].wait()
+    copies[5].start()
+    copies[4].wait()
+    for j in range(parts):
+        p = plan_held[0, j]
+        for h in range(heads):
+            held[h * rows + j * piece : h * rows + (j + 1) * piece, :] = q_held[
+                pl.ds(pl.multiple_of(p * piece, piece), piece), h * HEAD_DIM : (h + 1) * HEAD_DIM
+            ]
+    copies[6].start()
+    copies[7].start()
+    for copy in copies[5:]:
+        copy.wait()
 
 
 def attend_kernel(parts, heads, scale, slots, *refs):
@@ -233,8 +253,15 @@
             jax.ShapeDtypeStruct((heads * rows, HEAD_DIM), bf16),
             jax.ShapeDtypeStruct((kv_rows, HEAD_DIM), bf16),
         ],
-        in_specs=[SMEM, VMEM, VMEM, VMEM, VMEM],
-        out_specs=[VMEM] * 3,
+        in_specs=[ANY] * 5,
+        out_specs=[ANY] * 3,
+        scratch_shapes=[
+            pltpu.SMEM(plan.shape, jnp.int32),
+            pltpu.VMEM(queries.shape, bf16),
+            pltpu.VMEM((heads * rows + kv_rows, HEAD_DIM), bf16),
+            pltpu.VMEM((1, rows), jnp.int32),
+            pltpu.SemaphoreType.DMA((8,)),
+        ],
         compiler_params=pltpu.CompilerParams(vmem_limit_bytes=PACK_LIMIT),
         name="pack",
     )(plan, queries, keys, values, doc_ids.reshape(1, rows))

time: 80.1 us -> 80.1 us (level)
  no operation moved by 1% of the time
where the time goes in v8:
time: 80.1 us; the launch traced here: 80 us
  waiting for transfers between devices  39.7 us (50%)
  starting transfers between devices  23.3 us (29%)
  Pallas kernels  15.9 us (20%)
  local copies, waits for them, and re-layouts  0.98 us (1%)
    ppermute x4, waiting for transfers between devices, packed_body(): arrived.append(lax.ppermute(sums[k], ('ctx', 'head'), pairs))  20.6 us
    ppermute x11, waiting for transfers between devices, along_ctx(): return lax.ppermute(x, 'ctx', [(i, i ^ k) for i in range(parts)])  19 us
    pallas_call x5, Pallas kernels, packed_body(): pl.pallas_call(functools.partial(attend_kernel, parts, heads, 1.0 / math....  10.5 us
    ppermute x11, starting transfers between devices, along_ctx(): return lax.ppermute(x, 'ctx', [(i, i ^ k) for i in range(parts)])  10 us
    ppermute x4, starting transfers between devices, packed_body(): arrived.append(lax.ppermute(sums[k], ('ctx', 'head'), pairs))  6.43 us
    ppermute x5, starting transfers between devices, packed_body(): halves += [keep, lax.ppermute(send, 'head', pair)]  6.12 us
    pallas_call x1, Pallas kernels, packed_body(): pl.pallas_call(functools.partial(pack_kernel, parts, heads), out_shape=[j...  1.93 us
  transfers between devices with their start and end apart: 21, of which 10 were waited for; matrix products, arithmetic and copies ran while one was open for 0% of the time, Pallas kernels for 17%

profile of v8, /device:TPU:17, one launch (start us, length us, event | category | flops | bytes accessed | tf_op | source)
XLA Modules:
  0.0 80.0 jit_solution(9533898113553312387)
XLA Ops:
  0.0 0.7 collective-permute-start.16
  0.7 1.9 %pack.1 = (bf16[1296,128]{1,0:T(8,128)(2,1)}, bf16[1024,128]{1,0:T(8,128)(2,1)}, bf16[272,128]{1,0:T(8,128)(2,1)}) custom-call(s32[1,8]{1,0:T(1,128)} %plan_ref.1, bf16[128,1024]{1,0:T(8,128)(2,1)} %q_ref.1, bf16[128,128]{1,0:T(8,128)(2,1)} %k_ref.1, bf16[128,128]{1,0:T(8,128)(2,1)} %v_ref.1, s32[1,128]{1,0:T(1,128)} %bitcast.1), custom_call_target="tpu_custom_call" | custom-call | tf_op jit(solution)/shard_map/pack/pallas_call | solution.py:249
  2.6 1.4 %collective-permute-start.1 = (bf16[1296,128]{1,0:T(8,128)(2,1)}, bf16[1296,128]{1,0:T(8,128)(2,1)S(1)}, u32[]{:S(2)}, u32[]{:S(2)}) collective-permute-start(bf16[1296,128]{1,0:T(8,128)(2,1)} %get-tuple-element.37.refs_0_), channel_id=1, source_target_pairs={{0,8},{4,12},{8,0},{12,4},{16,24},{20,28},{24,16},{28,20},{1,9},{5... | collective-permute-start | bytes 995336 | tf_op jit(solution)/shard_map/ppermute | solution.py:206
  4.0 1.2 %collective-permute-start = (bf16[1296,128]{1,0:T(8,128)(2,1)}, bf16[1296,128]{1,0:T(8,128)(2,1)S(1)}, u32[]{:S(2)}, u32[]{:S(2)}) collective-permute-start(bf16[1296,128]{1,0:T(8,128)(2,1)} %get-tuple-element.37.refs_0_), channel_id=1, source_target_pairs={{0,4},{4,0},{8,12},{12,8},{16,20},{20,16},{24,28},{28,24},{1,5},{5... | collective-permute-start | bytes 995336 | tf_op jit(solution)/shard_map/ppermute | solution.py:206
  5.2 0.0 collective-permute-start.3
  5.2 2.3 %collective-permute-start.2 = (bf16[272,128]{1,0:T(8,128)(2,1)}, bf16[272,128]{1,0:T(8,128)(2,1)S(1)}, u32[]{:S(2)}, u32[]{:S(2)}) collective-permute-start(bf16[272,128]{1,0:T(8,128)(2,1)} %get-tuple-element.36), channel_id=1, source_target_pairs={{0,16},{4,20},{8,24},{12,28},{16,0},{20,4},{24,8},{28,12},{1,17},{... | collective-permute-start | bytes 208904 | tf_op jit(solution)/shard_map/ppermute | solution.py:206
  7.5 7.1 %collective-permute-done.3.refs_5_ = bf16[272,128]{1,0:T(8,128)(2,1)S(1)} collective-permute-done((bf16[272,128]{1,0:T(8,128)(2,1)}, bf16[272,128]{1,0:T(8,128)(2,1)S(1)}, u32[]{:S(2)}, u32[]{:S(2)}) %collective-permute-start.3) | collective-permute-done | bytes 69664 | tf_op jit(solution)/shard_map/ppermute | solution.py:206
  14.7 0.5 collective-permute-done.2.refs_4_
  15.2 0.0 collective-permute-done.1.refs_2_
  15.2 0.0 collective-permute-done.refs_1_
  15.2 1.2 %collective-permute-start.4 = (bf16[1296,128]{1,0:T(8,128)(2,1)S(1)}, bf16[1296,128]{1,0:T(8,128)(2,1)S(1)}, u32[]{:S(2)}, u32[]{:S(2)}) collective-permute-start(bf16[1296,128]{1,0:T(8,128)(2,1)S(1)} %collective-permute-done.1.refs_2_), channel_id=1, source_target_pairs={{0,4},{4,0},{8,12},{12,8},{16,20},{20,16},{24,28},{28,24},{1,5},{5... | collective-permute-start | bytes 995336 | tf_op jit(solution)/shard_map/ppermute | solution.py:206
  16.4 0.2 collective-permute-start.7
  16.6 2.3 %collective-permute-start.5 = (bf16[272,128]{1,0:T(8,128)(2,1)S(1)}, bf16[272,128]{1,0:T(8,128)(2,1)S(1)}, u32[]{:S(2)}, u32[]{:S(2)}) collective-permute-start(bf16[272,128]{1,0:T(8,128)(2,1)S(1)} %collective-permute-done.2.refs_4_), channel_id=1, source_target_pairs={{0,8},{4,12},{8,0},{12,4},{16,24},{20,28},{24,16},{28,20},{1,9},{5... | collective-permute-start | bytes 208904 | tf_op jit(solution)/shard_map/ppermute | solution.py:206
  18.9 0.0 collective-permute-start.6
  19.0 7.0 %collective-permute-done.5.refs_6_ = bf16[272,128]{1,0:T(8,128)(2,1)S(1)} collective-permute-done((bf16[272,128]{1,0:T(8,128)(2,1)S(1)}, bf16[272,128]{1,0:T(8,128)(2,1)S(1)}, u32[]{:S(2)}, u32[]{:S(2)}) %collective-permute-start.5) | collective-permute-done | bytes 69664 | tf_op jit(solution)/shard_map/ppermute | solution.py:206
  26.0 1.4 %collective-permute-done.6.refs_7_ = bf16[272,128]{1,0:T(8,128)(2,1)S(1)} collective-permute-done((bf16[272,128]{1,0:T(8,128)(2,1)S(1)}, bf16[272,128]{1,0:T(8,128)(2,1)S(1)}, u32[]{:S(2)}, u32[]{:S(2)}) %collective-permute-start.6) | collective-permute-done | bytes 69664 | tf_op jit(solution)/shard_map/ppermute | solution.py:206
  27.4 0.0 collective-permute-done.4.refs_3_
  27.4 1.0 %copy-done.1 = bf16[1296,128]{1,0:T(8,128)(2,1)S(1)} copy-done((bf16[1296,128]{1,0:T(8,128)(2,1)S(1)}, bf16[1296,128]{1,0:T(8,128)(2,1)}, u32[]{:S(2)}) %copy-start.1) | copy-done | bytes 331800
  28.4 3.2 %attend.5 = (bf16[128,1024]{1,0:T(8,128)(2,1)S(1)}, bf16[128,1024]{1,0:T(8,128)(2,1)S(1)}) custom-call(bf16[1296,128]{1,0:T(8,128)(2,1)S(1)} %copy-done.1, bf16[1296,128]{1,0:T(8,128)(2,1)S(1)} %collective-permute-done.refs_1_, bf16[1296,128]{1,0:T(8,128)(2,1)S(1)} %collective-permute-done.1.refs_2_, bf16[1296,128]{1,0:T(8,128)(2,1)S(1)} %collective-permute-done.4.refs_3_, ...), custom_call_target="tpu_custom_call" | custom-call | tf_op jit(solution)/shard_map/attend/pallas_call | solution.py:279
  31.6 0.9 %collective-permute-start.9 = (bf16[1024,128]{1,0:T(8,128)(2,1)S(1)}, bf16[1024,128]{1,0:T(8,128)(2,1)S(1)}, u32[]{:S(2)}, u32[]{:S(2)}) collective-permute-start(bf16[1024,128]{1,0:T(8,128)(2,1)S(1)} %collective-permute-done.7.refs_8_), channel_id=1, source_target_pairs={{0,8},{4,12},{8,0},{12,4},{16,24},{20,28},{24,16},{28,20},{1,9},{5... | collective-permute-start | bytes 786440 | tf_op jit(solution)/shard_map/ppermute | solution.py:206
  32.6 0.2 collective-permute-start.8
  32.8 2.8 %attend.7 = (bf16[128,1024]{1,0:T(8,128)(2,1)S(1)}, bf16[128,1024]{1,0:T(8,128)(2,1)S(1)}) custom-call(bf16[1296,128]{1,0:T(8,128)(2,1)S(1)} %copy-done.1, bf16[1296,128]{1,0:T(8,128)(2,1)S(1)} %collective-permute-done.refs_1_, bf16[1296,128]{1,0:T(8,128)(2,1)S(1)} %collective-permute-done.1.refs_2_, bf16[1296,128]{1,0:T(8,128)(2,1)S(1)} %collective-permute-done.4.refs_3_, ...), custom_call_target="tpu_custom_call" | custom-call | tf_op jit(solution)/shard_map/attend/pallas_call | solution.py:279
  35.6 1.0 %attend.6 = (bf16[64,1024]{1,0:T(8,128)(2,1)S(1)}, bf16[64,1024]{1,0:T(8,128)(2,1)S(1)}) custom-call(bf16[1296,128]{1,0:T(8,128)(2,1)S(1)} %copy-done.1, bf16[1296,128]{1,0:T(8,128)(2,1)S(1)} %collective-permute-done.refs_1_, bf16[1296,128]{1,0:T(8,128)(2,1)S(1)} %collective-permute-done.1.refs_2_, bf16[1296,128]{1,0:T(8,128)(2,1)S(1)} %collective-permute-done.4.refs_3_, ...), custom_call_target="tpu_custom_call" | custom-call | tf_op jit(solution)/shard_map/attend/pallas_call | solution.py:279
  36.6 0.0 copy-start
  36.7 0.9 %collective-permute-done.9.refs_9_ = bf16[1024,128]{1,0:T(8,128)(2,1)S(1)} collective-permute-done((bf16[1024,128]{1,0:T(8,128)(2,1)S(1)}, bf16[1024,128]{1,0:T(8,128)(2,1)S(1)}, u32[]{:S(2)}, u32[]{:S(2)}) %collective-permute-start.9) | collective-permute-done | bytes 262176 | tf_op jit(solution)/shard_map/ppermute | solution.py:206
  37.5 1.6 %collective-permute-done.8.refs_8_ = bf16[1024,128]{1,0:T(8,128)(2,1)S(1)} collective-permute-done((bf16[1024,128]{1,0:T(8,128)(2,1)S(1)}, bf16[1024,128]{1,0:T(8,128)(2,1)S(1)}, u32[]{:S(2)}, u32[]{:S(2)}) %collective-permute-start.8) | collective-permute-done | bytes 262176 | tf_op jit(solution)/shard_map/ppermute | solution.py:206
  39.2 0.2 collective-permute-start.11
  39.4 2.4 %collective-permute-start.14 = (bf16[128,1024]{1,0:T(8,128)(2,1)S(1)}, bf16[128,1024]{1,0:T(8,128)(2,1)S(1)}, u32[]{:S(2)}, u32[]{:S(2)}) collective-permute-start(bf16[128,1024]{1,0:T(8,128)(2,1)S(1)} %get-tuple-element.58), channel_id=1, source_target_pairs={{0,1},{1,0},{2,3},{3,2},{4,5},{5,4},{6,7},{7,6},{8,9},{9,8},{10,11... | collective-permute-start | bytes 786440 | tf_op jit(solution)/shard_map/ppermute | solution.py:300
  41.8 2.0 %attend.8 = (bf16[128,1024]{1,0:T(8,128)(2,1)S(1)}, bf16[128,1024]{1,0:T(8,128)(2,1)S(1)}) custom-call(bf16[1296,128]{1,0:T(8,128)(2,1)S(1)} %copy-done.1, bf16[1296,128]{1,0:T(8,128)(2,1)S(1)} %collective-permute-done.refs_1_, bf16[1296,128]{1,0:T(8,128)(2,1)S(1)} %collective-permute-done.1.refs_2_, bf16[1296,128]{1,0:T(8,128)(2,1)S(1)} %collective-permute-done.4.refs_3_, ...), custom_call_target="tpu_custom_call" | custom-call | tf_op jit(solution)/shard_map/attend/pallas_call | solution.py:279
  43.9 0.6 collective-permute-start.10
  44.4 0.4 collective-permute-done.11.refs_8_
  44.8 3.1 %collective-permute-start.15 = (bf16[64,1024]{1,0:T(8,128)(2,1)S(1)}, bf16[64,1024]{1,0:T(8,128)(2,1)S(1)}, u32[]{:S(2)}, u32[]{:S(2)}) collective-permute-start(bf16[64,1024]{1,0:T(8,128)(2,1)S(1)} %get-tuple-element.60), channel_id=1, source_target_pairs={{0,1},{1,0},{2,3},{3,2},{4,5},{5,4},{6,7},{7,6},{8,9},{9,8},{10,11... | collective-permute-start | bytes 393224 | tf_op jit(solution)/shard_map/ppermute | solution.py:300
  47.9 1.4 %attend.9 = (bf16[64,1024]{1,0:T(8,128)(2,1)S(1)}, bf16[64,1024]{1,0:T(8,128)(2,1)S(1)}) custom-call(bf16[1296,128]{1,0:T(8,128)(2,1)S(1)} %copy-done.1, bf16[1296,128]{1,0:T(8,128)(2,1)S(1)} %collective-permute-done.refs_1_, bf16[1296,128]{1,0:T(8,128)(2,1)S(1)} %collective-permute-done.1.refs_2_, bf16[1296,128]{1,0:T(8,128)(2,1)S(1)} %collective-permute-done.4.refs_3_, ...), custom_call_target="tpu_custom_call" | custom-call | tf_op jit(solution)/shard_map/attend/pallas_call | solution.py:279
  49.3 0.0 collective-permute-done.14.refs_3_
  49.3 0.1 collective-permute-start.12
  49.4 0.0 collective-permute-done.15.refs_5_
  49.4 0.0 collective-permute-done.16.refs_7_.refs_6_
  49.4 1.5 %project_early.1.refs_4_ = bf16[320,1024]{1,0:T(8,128)(2,1)S(1)} custom-call(bf16[128,1024]{1,0:T(8,128)(2,1)S(1)} %get-tuple-element.55.refs_0_, bf16[128,1024]{1,0:T(8,128)(2,1)S(1)} %collective-permute-done.13.refs_1_, bf16[128,1024]{1,0:T(8,128)(2,1)S(1)} %get-tuple-element.57.refs_2_, bf16[128,1024]{1,0:T(8,128)(2,1)S(1)} %collective-permute-done.14.refs_3_, ...), custom_call_target="tpu_custom_call" | custom-call | tf_op jit(solution)/shard_map/project_early/pallas_call | solution.py:306
  51.0 0.0 collective-permute-done.10.refs_1_
  51.0 1.0 %project.1 = (bf16[128,1024]{1,0:T(8,128)(2,1)S(1)}, bf16[128,1024]{1,0:T(8,128)(2,1)S(1)}, bf16[128,1024]{1,0:T(8,128)(2,1)S(1)}, bf16[128,1024]{1,0:T(8,128)(2,1)S(1)}) custom-call(bf16[128,1024]{1,0:T(8,128)(2,1)S(1)} %get-tuple-element.51.refs_0_, bf16[128,1024]{1,0:T(8,128)(2,1)S(1)} %collective-permute-done.10.refs_1_, ...), custom_call_target="tpu_custom_call" | custom-call | tf_op jit(solution)/shard_map/project/pallas_call | solution.py:315
  52.0 1.4 %collective-permute-start.17 = (bf16[128,1024]{1,0:T(8,128)(2,1)S(1)}, bf16[128,1024]{1,0:T(8,128)(2,1)S(1)}, u32[]{:S(2)}, u32[]{:S(2)}) collective-permute-start(bf16[128,1024]{1,0:T(8,128)(2,1)S(1)} %get-tuple-element.61), channel_id=1, source_target_pairs={{0,24},{1,28},{2,16},{3,20},{4,8},{5,12},{6,0},{7,4},{8,1},{9,5},{... | collective-permute-start | bytes 786440 | tf_op jit(solution)/shard_map/ppermute | solution.py:334
  53.5 1.9 %collective-permute-start.18 = (bf16[128,1024]{1,0:T(8,128)(2,1)S(1)}, bf16[128,1024]{1,0:T(8,128)(2,1)S(1)}, u32[]{:S(2)}, u32[]{:S(2)}) collective-permute-start(bf16[128,1024]{1,0:T(8,128)(2,1)S(1)} %get-tuple-element.62), channel_id=1, source_target_pairs={{0,16},{1,20},{2,24},{3,28},{4,0},{5,4},{6,8},{7,12},{8,9},{9,13},... | collective-permute-start | bytes 786440 | tf_op jit(solution)/shard_map/ppermute | solution.py:334
  55.4 3.0 %collective-permute-start.20 = (bf16[128,1024]{1,0:T(8,128)(2,1)S(1)}, bf16[128,1024]{1,0:T(8,128)(2,1)S(1)}, u32[]{:S(2)}, u32[]{:S(2)}) collective-permute-start(bf16[128,1024]{1,0:T(8,128)(2,1)S(1)} %get-tuple-element.64), channel_id=1, source_target_pairs={{0,0},{1,4},{2,8},{3,12},{4,16},{5,20},{6,24},{7,28},{8,25},{9,29}... | collective-permute-start | bytes 786440 | tf_op jit(solution)/shard_map/ppermute | solution.py:334
  58.5 14.4 %collective-permute-done.17.refs_0_ = bf16[128,1024]{1,0:T(8,128)(2,1)S(1)} collective-permute-done((bf16[128,1024]{1,0:T(8,128)(2,1)S(1)}, bf16[128,1024]{1,0:T(8,128)(2,1)S(1)}, u32[]{:S(2)}, u32[]{:S(2)}) %collective-permute-start.17) | collective-permute-done | bytes 262176 | tf_op jit(solution)/shard_map/ppermute | solution.py:334
  72.9 4.7 %collective-permute-done.18.refs_1_ = bf16[128,1024]{1,0:T(8,128)(2,1)S(1)} collective-permute-done((bf16[128,1024]{1,0:T(8,128)(2,1)S(1)}, bf16[128,1024]{1,0:T(8,128)(2,1)S(1)}, u32[]{:S(2)}, u32[]{:S(2)}) %collective-permute-start.18) | collective-permute-done | bytes 262176 | tf_op jit(solution)/shard_map/ppermute | solution.py:334
  77.6 0.0 collective-permute-done.19.refs_2_
  77.6 1.4 %collective-permute-done.20.refs_3_ = bf16[128,1024]{1,0:T(8,128)(2,1)S(1)} collective-permute-done((bf16[128,1024]{1,0:T(8,128)(2,1)S(1)}, bf16[128,1024]{1,0:T(8,128)(2,1)S(1)}, u32[]{:S(2)}, u32[]{:S(2)}) %collective-permute-start.20) | collective-permute-done | bytes 262176 | tf_op jit(solution)/shard_map/ppermute | solution.py:334
  79.1 0.9 %final_sum.1 = bf16[128,2048]{1,0:T(8,128)(2,1)} custom-call(bf16[128,1024]{1,0:T(8,128)(2,1)S(1)} %collective-permute-done.17.refs_0_, bf16[128,1024]{1,0:T(8,128)(2,1)S(1)} %collective-permute-done.18.refs_1_, bf16[128,1024]{1,0:T(8,128)(2,1)S(1)} %collective-permute-done.19.refs_2_, bf16[128,1024]{1,0:T(8,128)(2,1)S(1)} %collective-permute-done.20.refs_3_), custom_call_target="tpu_custom_call" | custom-call | tf_op jit(solution)/shard_map/final_sum/pallas_call | solution.py:335
  (7 shorter events, 0.0 us)
Async XLA Ops:
  0.0 49.4 %collective-permute-start.16 = (bf16[1024,1024]{1,0:T(8,128)(2,1)}, bf16[1024,1024]{1,0:T(8,128)(2,1)S(1)}, u32[]{:S(2)}, u32[]{:S(2)}) collective-permute-start(bf16[1024,1024]{1,0:T(8,128)(2,1)} %refs_5_.1), channel_id=1, source_target_pairs={{0,1},{1,0},{2,3},{3,2},{4,5},{5,4},{6,7},{7,6},{8,9},{9,8},{10,11... | collective-permute-start | bytes 6291464 | tf_op jit(solution)/shard_map/ppermute | solution.py:248
  2.6 12.6 %collective-permute-start.1 = (bf16[1296,128]{1,0:T(8,128)(2,1)}, bf16[1296,128]{1,0:T(8,128)(2,1)S(1)}, u32[]{:S(2)}, u32[]{:S(2)}) collective-permute-start(bf16[1296,128]{1,0:T(8,128)(2,1)} %get-tuple-element.37.refs_0_), channel_id=1, source_target_pairs={{0,8},{4,12},{8,0},{12,4},{16,24},{20,28},{24,16},{28,20},{1,9},{5... | collective-permute-start | bytes 995336 | tf_op jit(solution)/shard_map/ppermute | solution.py:206
  4.0 11.2 %collective-permute-start = (bf16[1296,128]{1,0:T(8,128)(2,1)}, bf16[1296,128]{1,0:T(8,128)(2,1)S(1)}, u32[]{:S(2)}, u32[]{:S(2)}) collective-permute-start(bf16[1296,128]{1,0:T(8,128)(2,1)} %get-tuple-element.37.refs_0_), channel_id=1, source_target_pairs={{0,4},{4,0},{8,12},{12,8},{16,20},{20,16},{24,28},{28,24},{1,5},{5... | collective-permute-start | bytes 995336 | tf_op jit(solution)/shard_map/ppermute | solution.py:206
  5.2 9.4 %collective-permute-start.3 = (bf16[272,128]{1,0:T(8,128)(2,1)}, bf16[272,128]{1,0:T(8,128)(2,1)S(1)}, u32[]{:S(2)}, u32[]{:S(2)}) collective-permute-start(bf16[272,128]{1,0:T(8,128)(2,1)} %get-tuple-element.36), channel_id=1, source_target_pairs={{0,20},{4,16},{8,28},{12,24},{16,4},{20,0},{24,12},{28,8},{1,21},{... | collective-permute-start | bytes 208904 | tf_op jit(solution)/shard_map/ppermute | solution.py:206
  5.2 10.0 %collective-permute-start.2 = (bf16[272,128]{1,0:T(8,128)(2,1)}, bf16[272,128]{1,0:T(8,128)(2,1)S(1)}, u32[]{:S(2)}, u32[]{:S(2)}) collective-permute-start(bf16[272,128]{1,0:T(8,128)(2,1)} %get-tuple-element.36), channel_id=1, source_target_pairs={{0,16},{4,20},{8,24},{12,28},{16,0},{20,4},{24,8},{28,12},{1,17},{... | collective-permute-start | bytes 208904 | tf_op jit(solution)/shard_map/ppermute | solution.py:206
  15.2 12.2 %collective-permute-start.4 = (bf16[1296,128]{1,0:T(8,128)(2,1)S(1)}, bf16[1296,128]{1,0:T(8,128)(2,1)S(1)}, u32[]{:S(2)}, u32[]{:S(2)}) collective-permute-start(bf16[1296,128]{1,0:T(8,128)(2,1)S(1)} %collective-permute-done.1.refs_2_), channel_id=1, source_target_pairs={{0,4},{4,0},{8,12},{12,8},{16,20},{20,16},{24,28},{28,24},{1,5},{5... | collective-permute-start | bytes 995336 | tf_op jit(solution)/shard_map/ppermute | solution.py:206
  16.4 15.2 %collective-permute-start.7 = (bf16[1024,128]{1,0:T(8,128)(2,1)}, bf16[1024,128]{1,0:T(8,128)(2,1)S(1)}, u32[]{:S(2)}, u32[]{:S(2)}) collective-permute-start(bf16[1024,128]{1,0:T(8,128)(2,1)} %get-tuple-element.43), channel_id=1, source_target_pairs={{0,16},{4,20},{8,24},{12,28},{16,0},{20,4},{24,8},{28,12},{1,17},{... | collective-permute-start | bytes 786440 | tf_op jit(solution)/shard_map/ppermute | solution.py:206
  16.6 9.4 %collective-permute-start.5 = (bf16[272,128]{1,0:T(8,128)(2,1)S(1)}, bf16[272,128]{1,0:T(8,128)(2,1)S(1)}, u32[]{:S(2)}, u32[]{:S(2)}) collective-permute-start(bf16[272,128]{1,0:T(8,128)(2,1)S(1)} %collective-permute-done.2.refs_4_), channel_id=1, source_target_pairs={{0,8},{4,12},{8,0},{12,4},{16,24},{20,28},{24,16},{28,20},{1,9},{5... | collective-permute-start | bytes 208904 | tf_op jit(solution)/shard_map/ppermute | solution.py:206
  18.9 8.5 %collective-permute-start.6 = (bf16[272,128]{1,0:T(8,128)(2,1)S(1)}, bf16[272,128]{1,0:T(8,128)(2,1)S(1)}, u32[]{:S(2)}, u32[]{:S(2)}) collective-permute-start(bf16[272,128]{1,0:T(8,128)(2,1)S(1)} %collective-permute-done.3.refs_5_), channel_id=1, source_target_pairs={{0,8},{4,12},{8,0},{12,4},{16,24},{20,28},{24,16},{28,20},{1,9},{5... | collective-permute-start | bytes 208904 | tf_op jit(solution)/shard_map/ppermute | solution.py:206
  27.4 1.0 %copy-start.1 = (bf16[1296,128]{1,0:T(8,128)(2,1)S(1)}, bf16[1296,128]{1,0:T(8,128)(2,1)}, u32[]{:S(2)}) copy-start(bf16[1296,128]{1,0:T(8,128)(2,1)} %get-tuple-element.37.refs_0_) | copy-start | bytes 995332
  31.6 5.9 %collective-permute-start.9 = (bf16[1024,128]{1,0:T(8,128)(2,1)S(1)}, bf16[1024,128]{1,0:T(8,128)(2,1)S(1)}, u32[]{:S(2)}, u32[]{:S(2)}) collective-permute-start(bf16[1024,128]{1,0:T(8,128)(2,1)S(1)} %collective-permute-done.7.refs_8_), channel_id=1, source_target_pairs={{0,8},{4,12},{8,0},{12,4},{16,24},{20,28},{24,16},{28,20},{1,9},{5... | collective-permute-start | bytes 786440 | tf_op jit(solution)/shard_map/ppermute | solution.py:206
  32.6 6.6 %collective-permute-start.8 = (bf16[1024,128]{1,0:T(8,128)(2,1)S(1)}, bf16[1024,128]{1,0:T(8,128)(2,1)S(1)}, u32[]{:S(2)}, u32[]{:S(2)}) collective-permute-start(bf16[1024,128]{1,0:T(8,128)(2,1)S(1)} %collective-permute-done.7.refs_8_), channel_id=1, source_target_pairs={{0,4},{4,0},{8,12},{12,8},{16,20},{20,16},{24,28},{28,24},{1,5},{5... | collective-permute-start | bytes 786440 | tf_op jit(solution)/shard_map/ppermute | solution.py:206
  36.6 12.8 %copy-start = (bf16[1024,1024]{1,0:T(8,128)(2,1)S(1)}, bf16[1024,1024]{1,0:T(8,128)(2,1)}, u32[]{:S(2)}) copy-start(bf16[1024,1024]{1,0:T(8,128)(2,1)} %refs_5_.1) | copy-start | bytes 6291460
  39.2 5.7 %collective-permute-start.11 = (bf16[1024,128]{1,0:T(8,128)(2,1)S(1)}, bf16[1024,128]{1,0:T(8,128)(2,1)S(1)}, u32[]{:S(2)}, u32[]{:S(2)}) collective-permute-start(bf16[1024,128]{1,0:T(8,128)(2,1)S(1)} %collective-permute-done.9.refs_9_), channel_id=1, source_target_pairs={{0,4},{4,0},{8,12},{12,8},{16,20},{20,16},{24,28},{28,24},{1,5},{5... | collective-permute-start | bytes 786440 | tf_op jit(solution)/shard_map/ppermute | solution.py:206
  39.4 9.9 %collective-permute-start.14 = (bf16[128,1024]{1,0:T(8,128)(2,1)S(1)}, bf16[128,1024]{1,0:T(8,128)(2,1)S(1)}, u32[]{:S(2)}, u32[]{:S(2)}) collective-permute-start(bf16[128,1024]{1,0:T(8,128)(2,1)S(1)} %get-tuple-element.58), channel_id=1, source_target_pairs={{0,1},{1,0},{2,3},{3,2},{4,5},{5,4},{6,7},{7,6},{8,9},{9,8},{10,11... | collective-permute-start | bytes 786440 | tf_op jit(solution)/shard_map/ppermute | solution.py:300
  41.8 7.6 %collective-permute-start.13 = (bf16[128,1024]{1,0:T(8,128)(2,1)S(1)}, bf16[128,1024]{1,0:T(8,128)(2,1)S(1)}, u32[]{:S(2)}, u32[]{:S(2)}) collective-permute-start(bf16[128,1024]{1,0:T(8,128)(2,1)S(1)} %get-tuple-element.56), channel_id=1, source_target_pairs={{0,1},{1,0},{2,3},{3,2},{4,5},{5,4},{6,7},{7,6},{8,9},{9,8},{10,11... | collective-permute-start | bytes 786440 | tf_op jit(solution)/shard_map/ppermute | solution.py:300
  43.9 7.1 %collective-permute-start.10 = (bf16[128,1024]{1,0:T(8,128)(2,1)S(1)}, bf16[128,1024]{1,0:T(8,128)(2,1)S(1)}, u32[]{:S(2)}, u32[]{:S(2)}) collective-permute-start(bf16[128,1024]{1,0:T(8,128)(2,1)S(1)} %get-tuple-element.52), channel_id=1, source_target_pairs={{0,1},{1,0},{2,3},{3,2},{4,5},{5,4},{6,7},{7,6},{8,9},{9,8},{10,11... | collective-permute-start | bytes 786440 | tf_op jit(solution)/shard_map/ppermute | solution.py:300
  44.8 4.6 %collective-permute-start.15 = (bf16[64,1024]{1,0:T(8,128)(2,1)S(1)}, bf16[64,1024]{1,0:T(8,128)(2,1)S(1)}, u32[]{:S(2)}, u32[]{:S(2)}) collective-permute-start(bf16[64,1024]{1,0:T(8,128)(2,1)S(1)} %get-tuple-element.60), channel_id=1, source_target_pairs={{0,1},{1,0},{2,3},{3,2},{4,5},{5,4},{6,7},{7,6},{8,9},{9,8},{10,11... | collective-permute-start | bytes 393224 | tf_op jit(solution)/shard_map/ppermute | solution.py:300
  49.3 1.7 %collective-permute-start.12 = (bf16[64,1024]{1,0:T(8,128)(2,1)S(1)}, bf16[64,1024]{1,0:T(8,128)(2,1)S(1)}, u32[]{:S(2)}, u32[]{:S(2)}) collective-permute-start(bf16[64,1024]{1,0:T(8,128)(2,1)S(1)} %get-tuple-element.54), channel_id=1, source_target_pairs={{0,1},{1,0},{2,3},{3,2},{4,5},{5,4},{6,7},{7,6},{8,9},{9,8},{10,11... | collective-permute-start | bytes 393224 | tf_op jit(solution)/shard_map/ppermute | solution.py:300
  52.0 20.9 %collective-permute-start.17 = (bf16[128,1024]{1,0:T(8,128)(2,1)S(1)}, bf16[128,1024]{1,0:T(8,128)(2,1)S(1)}, u32[]{:S(2)}, u32[]{:S(2)}) collective-permute-start(bf16[128,1024]{1,0:T(8,128)(2,1)S(1)} %get-tuple-element.61), channel_id=1, source_target_pairs={{0,24},{1,28},{2,16},{3,20},{4,8},{5,12},{6,0},{7,4},{8,1},{9,5},{... | collective-permute-start | bytes 786440 | tf_op jit(solution)/shard_map/ppermute | solution.py:334
  53.5 24.2 %collective-permute-start.18 = (bf16[128,1024]{1,0:T(8,128)(2,1)S(1)}, bf16[128,1024]{1,0:T(8,128)(2,1)S(1)}, u32[]{:S(2)}, u32[]{:S(2)}) collective-permute-start(bf16[128,1024]{1,0:T(8,128)(2,1)S(1)} %get-tuple-element.62), channel_id=1, source_target_pairs={{0,16},{1,20},{2,24},{3,28},{4,0},{5,4},{6,8},{7,12},{8,9},{9,13},... | collective-permute-start | bytes 786440 | tf_op jit(solution)/shard_map/ppermute | solution.py:334
  55.4 22.2 %collective-permute-start.19 = (bf16[128,1024]{1,0:T(8,128)(2,1)S(1)}, bf16[128,1024]{1,0:T(8,128)(2,1)S(1)}, u32[]{:S(2)}, u32[]{:S(2)}) collective-permute-start(bf16[128,1024]{1,0:T(8,128)(2,1)S(1)} %get-tuple-element.63), channel_id=1, source_target_pairs={{0,8},{1,12},{2,0},{3,4},{4,24},{5,28},{6,16},{7,20},{8,17},{9,21}... | collective-permute-start | bytes 786440 | tf_op jit(solution)/shard_map/ppermute | solution.py:334
  55.4 23.7 %collective-permute-start.20 = (bf16[128,1024]{1,0:T(8,128)(2,1)S(1)}, bf16[128,1024]{1,0:T(8,128)(2,1)S(1)}, u32[]{:S(2)}, u32[]{:S(2)}) collective-permute-start(bf16[128,1024]{1,0:T(8,128)(2,1)S(1)} %get-tuple-element.64), channel_id=1, source_target_pairs={{0,0},{1,4},{2,8},{3,12},{4,16},{5,20},{6,24},{7,28},{8,25},{9,29}... | collective-permute-start | bytes 786440 | tf_op jit(solution)/shard_map/ppermute | solution.py:334
